TPU v7x, 32 devices: a whole 2x2x4 slice. The times are simulated.
32 devices in a mesh: wide: 8 (over z, y), narrow: 4 (over x, core).
Axes of the slice: x: 2, y: 2, z: 4, core: 2. Of those that a mesh axis runs over, the one named last changes fastest.
Arguments:
- inputs: bfloat16 [2, 4096, 2048], P(None, 'wide', 'narrow'), may hold values from -6 to 6
- lengths: int32 [2, 8, 4], P(None, 'wide'), may hold values from 1 to 384, 512 in all within a row
- hidden_counts: int32 [4], replicated, may hold values from 1 to 1536, 5461 in all
- w_qkv: bfloat16 [3, 2048, 2048], P(None, 'wide', 'narrow'), may hold values from -0.1875 to 0.1875
- w_out: bfloat16 [2048, 2048], P('narrow', 'wide'), may hold values from -0.75 to 0.75
- w_gate_up: bfloat16 [2, 2048, 6144], P(None, 'wide', 'narrow'), may hold values from -0.125 to 0.125
- w_down: bfloat16 [6144, 2048], P('narrow', 'wide'), may hold values from -0.078125 to 0.078125
- norm1_gain: bfloat16 [2048], P('wide'), may hold values from 0.5 to 1.5
- norm1_bias: bfloat16 [2048], P('wide'), may hold values from -3 to 3
- norm2_gain: bfloat16 [2048], P('wide'), may hold values from 0.5 to 1.5
- norm2_bias: bfloat16 [2048], P('wide'), may hold values from -3 to 3
- out_cotangent: bfloat16 [2, 4096, 2048], P(None, 'wide', 'narrow'), may hold values from -6 to 6
Outputs:
- layer_out: bfloat16 [2, 4096, 2048], P(None, 'wide', 'narrow')
- input_grad: bfloat16 [2, 4096, 2048], P(None, 'wide', 'narrow')
- qkv_grad: float32 [3, 2048, 2048], P(None, 'wide', 'narrow')
- out_proj_grad: float32 [2048, 2048], P('narrow', 'wide')
- gate_up_grad: float32 [2, 2048, 6144], P(None, 'wide', 'narrow')
- down_grad: float32 [6144, 2048], P('narrow', 'wide')
- norm1_gain_grad: float32 [2048], P('wide')
- norm1_bias_grad: float32 [2048], P('wide')
- norm2_gain_grad: float32 [2048], P('wide')
- norm2_bias_grad: float32 [2048], P('wide')
Inputs may be any that keep to these rules, and one draw needn't show every extreme that they name: Protein lengths of each block of 512 rows, in order; each block's sum to 512 and the longest of each block is exactly 384. `hidden_counts`: hidden units used in each column block of 1536 slots; they sum to 5461 and the largest is exactly 1536.
All inputs are finite; a program needn't handle non-finite values.
Results may differ from a plain program's by a relative error of at most 0.014.
The roundings to bfloat16 on the way count: a program that leaves them out, or rounds other values in their place, can miss the bound.
Values may be sent and summed in bfloat16 or wider, within the bound.
A program may use at most 320 MiB of HBM per device.

v0:
```python
import jax
import jax.numpy as jnp
from jax import lax
from jax.sharding import PartitionSpec as P

HEAD_DIM = 128


eps = 1e-05


def layer_norm(values, gain, shift):
    average = jnp.mean(values, axis=-1, keepdims=True)
    centred = values - average
    spread = jnp.mean(centred * centred, axis=-1, keepdims=True)
    return centred * lax.rsqrt(spread + eps) * gain + shift


def protein_layout(length_row, row_count):
    seq_ends = jnp.cumsum(length_row)
    seq_starts = seq_ends - length_row
    places = jnp.arange(row_count, dtype=jnp.int32)
    protein_id = jnp.sum((places[:, None] >= seq_ends[None, :]).astype(jnp.int32), axis=1)
    onehot = protein_id[:, None] == jnp.arange(length_row.shape[0], dtype=jnp.int32)[None, :]
    positions = places - jnp.sum(jnp.where(onehot, seq_starts[None, :], 0), axis=1)
    return (protein_id, positions)


def rotary_tables(positions):
    half_dim = HEAD_DIM // 2
    frequency = 10000.0 ** (-jnp.arange(half_dim, dtype=jnp.float32) / half_dim)
    angles = positions.astype(jnp.float32)[:, None] * frequency[None, :]
    return (jnp.cos(angles)[:, None, :], jnp.sin(angles)[:, None, :])


def rotate(values, cosine_table, sine_table):
    half_dim = values.shape[-1] // 2
    first_half = values[..., :half_dim]
    second_half = values[..., half_dim:]
    return jnp.concatenate(
        [
            first_half * cosine_table - second_half * sine_table,
            second_half * cosine_table + first_half * sine_table,
        ],
        axis=-1,
    )


def micro_pass(params, token_rows, cotangent, length_row, column_mask, narrow_index, narrow_count):
    w_qkv_all, w_out_all, w_gate_up_all, w_down_all = (params[0], params[1], params[2], params[3])
    gain_one = params[4].astype(jnp.float32)
    shift_one = params[5].astype(jnp.float32)
    gain_two = params[6].astype(jnp.float32)
    shift_two = params[7].astype(jnp.float32)
    inputs = token_rows.astype(jnp.float32)
    token_count = inputs.shape[0]
    model_width = inputs.shape[1]
    feature_width = model_width // narrow_count
    start = narrow_index * feature_width
    slice_width = w_out_all.shape[0]
    head_count = slice_width // HEAD_DIM
    score_scale = HEAD_DIM ** (-0.5)
    protein_id, positions = protein_layout(length_row, token_count)
    cosine_table, sine_table = rotary_tables(positions)
    same_protein = (protein_id[:, None] == protein_id[None, :])[None]

    def own_cols(values):
        return lax.dynamic_slice_in_dim(values, start, feature_width, values.ndim - 1)

    normed_one, norm_one_back = jax.vjp(layer_norm, inputs, gain_one, shift_one)
    lowered_one = normed_one.astype(jnp.bfloat16)
    projected_qkv = jnp.einsum(
        "td,cde->cte", lowered_one, w_qkv_all, preferred_element_type=jnp.float32
    )
    shaped = projected_qkv.reshape(3, token_count, head_count, HEAD_DIM)
    queries = rotate(shaped[0], cosine_table, sine_table).astype(jnp.bfloat16)
    key_rows = rotate(shaped[1], cosine_table, sine_table).astype(jnp.bfloat16)
    value_rows = shaped[2].astype(jnp.bfloat16)
    scores = (
        jnp.einsum("thd,shd->hts", queries, key_rows, preferred_element_type=jnp.float32)
        * score_scale
    )
    scores = jnp.where(same_protein, scores, -1e30)
    top_score = jnp.max(scores, axis=-1, keepdims=True)
    exp_scores = jnp.exp(scores - top_score)
    row_total = jnp.sum(exp_scores, axis=-1, keepdims=True)
    log_total = top_score + jnp.log(row_total)
    attention_probs = (exp_scores / row_total).astype(jnp.bfloat16)
    attended = jnp.einsum(
        "hts,shd->thd", attention_probs, value_rows, preferred_element_type=jnp.float32
    )
    attended = attended.reshape(token_count, slice_width).astype(jnp.bfloat16)
    heads_part = jnp.dot(attended, w_out_all, preferred_element_type=jnp.float32)
    middle = inputs + lax.psum(heads_part, "narrow")
    normed_two, norm_two_back = jax.vjp(layer_norm, middle, gain_two, shift_two)
    lowered_two = normed_two.astype(jnp.bfloat16)
    middle_mine = own_cols(middle)
    gate_up = jnp.einsum(
        "td,cdf->ctf", lowered_two, w_gate_up_all, preferred_element_type=jnp.float32
    )

    def activate(gate_part, up_part):
        return jax.nn.gelu(gate_part, approximate=False) * up_part * column_mask

    activated, activate_back = jax.vjp(activate, gate_up[0], gate_up[1])
    hidden = activated.astype(jnp.bfloat16)
    ffn_part = jnp.dot(hidden, w_down_all, preferred_element_type=jnp.float32)
    ffn_mine = lax.psum_scatter(
        ffn_part.astype(jnp.bfloat16), "narrow", scatter_dimension=1, tiled=True
    ).astype(jnp.float32)
    out_slice = (middle_mine + ffn_mine).astype(jnp.bfloat16)
    down_grad = jnp.einsum("tf,td->fd", hidden, cotangent, preferred_element_type=jnp.float32)
    hidden_grad = jnp.einsum("td,fd->tf", cotangent, w_down_all, preferred_element_type=jnp.float32)
    gate_grad, up_grad = activate_back(hidden_grad)
    gate_up_low = jnp.stack([gate_grad, up_grad]).astype(jnp.bfloat16)
    gate_up_grad = jnp.einsum(
        "td,ctf->cdf", lowered_two, gate_up_low, preferred_element_type=jnp.float32
    )
    normed_two_part = jnp.einsum(
        "ctf,cdf->td", gate_up_low, w_gate_up_all, preferred_element_type=jnp.float32
    )
    normed_two_grad = lax.psum(normed_two_part, "narrow")
    middle_norm_grad, gain_two_grad, shift_two_grad = norm_two_back(normed_two_grad)
    middle_grad = cotangent.astype(jnp.float32) + middle_norm_grad
    branch_low = middle_grad.astype(jnp.bfloat16)
    out_proj_grad = jnp.einsum(
        "te,td->ed", attended, branch_low, preferred_element_type=jnp.float32
    )
    attended_grad = jnp.einsum(
        "td,ed->te", branch_low, w_out_all, preferred_element_type=jnp.float32
    )
    attended_grad = attended_grad.astype(jnp.bfloat16).reshape(token_count, head_count, HEAD_DIM)
    scores_again = (
        jnp.einsum("thd,shd->hts", queries, key_rows, preferred_element_type=jnp.float32)
        * score_scale
    )
    scores_again = jnp.where(same_protein, scores_again, -1e30)
    probs_again = jnp.exp(scores_again - log_total)
    prob_grad = jnp.einsum(
        "thd,shd->hts", attended_grad, value_rows, preferred_element_type=jnp.float32
    )
    value_grad = jnp.einsum(
        "hts,thd->shd",
        probs_again.astype(jnp.bfloat16),
        attended_grad,
        preferred_element_type=jnp.float32,
    )
    row_dot = jnp.sum(probs_again * prob_grad, axis=-1, keepdims=True)
    score_grad = (probs_again * (prob_grad - row_dot)).astype(jnp.bfloat16)
    query_grad = (
        jnp.einsum("hts,shd->thd", score_grad, key_rows, preferred_element_type=jnp.float32)
        * score_scale
    )
    key_grad = (
        jnp.einsum("hts,thd->shd", score_grad, queries, preferred_element_type=jnp.float32)
        * score_scale
    )
    qkv_low = jnp.stack(
        [
            rotate(query_grad, cosine_table, -sine_table),
            rotate(key_grad, cosine_table, -sine_table),
            value_grad,
        ]
    )
    qkv_low = qkv_low.reshape(3, token_count, slice_width).astype(jnp.bfloat16)
    qkv_grad = jnp.einsum("td,cte->cde", lowered_one, qkv_low, preferred_element_type=jnp.float32)
    normed_one_part = jnp.einsum(
        "cte,cde->td", qkv_low, w_qkv_all, preferred_element_type=jnp.float32
    )
    normed_one_grad = lax.psum(normed_one_part, "narrow")
    input_norm_grad, gain_one_grad, shift_one_grad = norm_one_back(normed_one_grad)
    input_mine = own_cols(middle_grad + input_norm_grad).astype(jnp.bfloat16)
    grad_terms = (
        qkv_grad,
        out_proj_grad,
        gate_up_grad,
        down_grad,
        gain_one_grad,
        shift_one_grad,
        gain_two_grad,
        shift_two_grad,
    )
    return (out_slice, input_mine, grad_terms)


def on_device(
    inputs,
    lengths,
    hidden_counts,
    w_qkv,
    w_out,
    w_gate_up,
    w_down,
    norm1_gain,
    norm1_bias,
    norm2_gain,
    norm2_bias,
    out_cotangent,
):
    narrow_index = lax.axis_index("narrow")
    narrow_count = lax.axis_size("narrow")
    rows_in, rows_back = (
        lax.all_gather(inputs, "narrow", axis=2, tiled=True),
        lax.all_gather(out_cotangent, "narrow", axis=2, tiled=True),
    )
    slot_count = w_gate_up.shape[2]
    slice_width = w_out.shape[0]
    model_width = rows_in.shape[2]
    own_count = jnp.sum(
        jnp.where(
            jnp.arange(hidden_counts.shape[0], dtype=jnp.int32) == narrow_index, hidden_counts, 0
        )
    )
    column_mask = (jnp.arange(slot_count, dtype=jnp.int32) < own_count).astype(jnp.float32)
    totals = (
        jnp.zeros((3, model_width, slice_width), jnp.float32),
        jnp.zeros((slice_width, model_width), jnp.float32),
        jnp.zeros((2, model_width, slot_count), jnp.float32),
        jnp.zeros((slot_count, model_width), jnp.float32),
        jnp.zeros((model_width,), jnp.float32),
        jnp.zeros((model_width,), jnp.float32),
        jnp.zeros((model_width,), jnp.float32),
        jnp.zeros((model_width,), jnp.float32),
    )
    out_slices = []
    input_slices = []
    for micro_step in range(rows_in.shape[0]):
        params = (
            lax.all_gather(w_qkv, "wide", axis=1, tiled=True),
            lax.all_gather(w_out, "wide", axis=1, tiled=True),
            lax.all_gather(w_gate_up, "wide", axis=1, tiled=True),
            lax.all_gather(w_down, "wide", axis=1, tiled=True),
            lax.all_gather(norm1_gain, "wide", axis=0, tiled=True),
            lax.all_gather(norm1_bias, "wide", axis=0, tiled=True),
            lax.all_gather(norm2_gain, "wide", axis=0, tiled=True),
            lax.all_gather(norm2_bias, "wide", axis=0, tiled=True),
        )
        out_slice, input_mine, grad_terms = micro_pass(
            params,
            rows_in[micro_step],
            rows_back[micro_step],
            lengths[micro_step, 0],
            column_mask,
            narrow_index,
            narrow_count,
        )
        out_slices.append(out_slice)
        input_slices.append(input_mine)
        totals = jax.tree.map(jnp.add, totals, grad_terms)
    return (
        jnp.stack(out_slices),
        jnp.stack(input_slices),
        lax.psum_scatter(totals[0], "wide", scatter_dimension=1, tiled=True),
        lax.psum_scatter(totals[1], "wide", scatter_dimension=1, tiled=True),
        lax.psum_scatter(totals[2], "wide", scatter_dimension=1, tiled=True),
        lax.psum_scatter(totals[3], "wide", scatter_dimension=1, tiled=True),
        lax.psum_scatter(totals[4], "wide", scatter_dimension=0, tiled=True),
        lax.psum_scatter(totals[5], "wide", scatter_dimension=0, tiled=True),
        lax.psum_scatter(totals[6], "wide", scatter_dimension=0, tiled=True),
        lax.psum_scatter(totals[7], "wide", scatter_dimension=0, tiled=True),
    )


def solution(mesh):
    return jax.shard_map(
        on_device,
        mesh=mesh,
        in_specs=(
            P(None, "wide", "narrow"),
            P(None, "wide", None),
            P(),
            P(None, "wide", "narrow"),
            P("narrow", "wide"),
            P(None, "wide", "narrow"),
            P("narrow", "wide"),
            P("wide"),
            P("wide"),
            P("wide"),
            P("wide"),
            P(None, "wide", "narrow"),
        ),
        out_specs=(
            P(None, "wide", "narrow"),
            P(None, "wide", "narrow"),
            P(None, "wide", "narrow"),
            P("narrow", "wide"),
            P(None, "wide", "narrow"),
            P("narrow", "wide"),
            P("wide"),
            P("wide"),
            P("wide"),
            P("wide"),
        ),
        check_vma=False,
    )
```

profile of v0, /device:TPU:0, one launch (start us, length us, event | category | flops | bytes accessed | tf_op | source)
XLA Modules:
  0.0 2038.9 jit_solution(9983237638388731135)
XLA Ops:
  12.7 22.3 %all-gather.1 = bf16[8,1,256]{2,1,0:T(2,128)(2,1)S(1)} all-gather(bf16[1,1,256]{2,1,0:T(2,128)(2,1)S(1)} %reshape.523), channel_id=1, replica_groups=mesh['wide'=8,'narrow'=4] {'wide'}, dimensions={0}, use_global_device_ids=true | all-gather | bytes 4608 | tf_op jit(solution)/shard_map/all_gather | solution.py:234
  34.9 16.3 all-gather
  56.4 3.3 convert_reduce_fusion.1
  62.6 86.8 %all-gather.13.cloned.1.call-done = bf16[3,2048,512]{1,2,0:T(8,128)(2,1)} async-done(((bf16[3,256,512]{1,2,0:T(8,128)(2,1)}), bf16[3,2048,512]{1,2,0:T(8,128)(2,1)}) %all-gather.13.cloned.1.call-update) | async-done | bytes 6291472 | tf_op jit(solution)/shard_map/all_gather | solution.py:229
  149.4 6.5 convolution_bitcast_fusion.6
  163.2 6.9 convolution_bitcast_fusion.7
  197.3 3.5 all-gather.15.cloned.1.call-done
  200.8 5.1 fusion.317
  207.6 3.2 fusion.316
  211.7 17.8 all-gather.3
  229.5 16.8 all-gather.2
  247.6 89.1 %all-gather.19.cloned.1.call-done = bf16[1536,2048]{1,0:T(8,128)(2,1)} async-done(((bf16[1536,256]{1,0:T(8,128)(2,1)}), bf16[1536,2048]{1,0:T(8,128)(2,1)}) %all-gather.19.cloned.1.call-update) | async-done | bytes 6291472 | tf_op jit(solution)/shard_map/all_gather | solution.py:232
  336.7 7.7 convolution_multiply_fusion.1
  344.5 5.1 convolution_multiply_fusion
  349.6 141.0 %all-reduce.16.cloned.1.call-done = (f32[512,2048]{1,0:T(8,128)}, f32[512,2048]{1,0:T(8,128)}) async-done(((f32[512,2048]{1,0:T(8,128)}, f32[512,2048]{1,0:T(8,128)}), (f32[512,2048]{1,0:T(8,128)}, f32[512,2048]{1,0:T(8,128)})) %all-reduce.16.cloned.1.call-update) | async-done | bytes 8388624 | tf_op jit(solution)/shard_map/psum | solution.py:94
  490.6 5.5 fusion.304
  499.4 170.0 %all-gather.17.cloned.1.call-done = bf16[2,2048,1536]{2,1,0:T(8,128)(2,1)} async-done(((bf16[2,256,1536]{2,1,0:T(8,128)(2,1)}), bf16[2,2048,1536]{2,1,0:T(8,128)(2,1)}) %all-gather.17.cloned.1.call-update) | async-done | bytes 12582928 | tf_op jit(solution)/shard_map/all_gather | solution.py:231
  669.4 10.7 convolution_bitcast_fusion.1
  680.1 7.5 fusion.180
  691.5 10.5 convolution_bitcast_fusion
  702.0 7.5 fusion.181
  710.8 11.7 convolution_bitcast_fusion.5
  722.5 11.1 convolution_bitcast_fusion.3
  733.7 11.1 convolution_convert_fusion.1
  744.8 9.5 convolution_convert_fusion
  754.4 130.8 %all-reduce.14.cloned.1.call-done = (f32[512,2048]{1,0:T(8,128)}, f32[512,2048]{1,0:T(8,128)}) async-done(((f32[512,2048]{1,0:T(8,128)}, f32[512,2048]{1,0:T(8,128)}), (f32[512,2048]{1,0:T(8,128)}, f32[512,2048]{1,0:T(8,128)})) %all-reduce.14.cloned.1.call-update) | async-done | bytes 8388624 | tf_op jit(solution)/shard_map/psum | solution.py:122
  885.2 8.9 multiply_reduce_fusion.1
  899.3 3.3 add_add_fusion.5
  921.6 3.3 multiply_reduce_fusion.4
  933.6 8.7 convolution_bitcast_fusion.4
  942.3 7.7 convolution_bitcast_fusion.2
  951.2 5.6 fusion.201
  956.8 9.1 add_bitcast_fusion.1
  966.2 15.0 fusion.108
  981.3 18.6 add_bitcast_fusion
  1000.9 3.7 fusion.198
  1004.6 3.3 convolution_add_fusion.1
  1008.5 12.9 fusion.109
  1021.5 15.0 convolution_add_fusion
  1043.0 66.8 %all-reduce.12.cloned.1.call-done = (f32[512,2048]{1,0:T(8,128)}, f32[512,2048]{1,0:T(8,128)}) async-done(((f32[512,2048]{1,0:T(8,128)}, f32[512,2048]{1,0:T(8,128)}), (f32[512,2048]{1,0:T(8,128)}, f32[512,2048]{1,0:T(8,128)})) %all-reduce.12.cloned.1.call-update) | async-done | bytes 8388624 | tf_op jit(solution)/shard_map/psum | solution.py:170
  1109.8 6.4 fusion.21
  1116.2 39.0 %all-reduce.4 = (f32[2048]{0:T(1024)S(1)}, f32[2048]{0:T(1024)S(1)}, f32[2048]{0:T(1024)S(1)}, f32[2048]{0:T(1024)S(1)}) all-reduce(f32[2048]{0:T(1024)S(1)} %add.235, f32[2048]{0:T(1024)S(1)} %add.236, f32[2048]{0:T(1024)S(1)} %add.237, f32[2048]{0:T(1024)S(1)} %add.238), channel_id=8, replica_groups=mesh['wide'=8,'narrow'=4] {'wide'}, use_global_device_ids=true, to_apply=%region_43.44.clone | all-reduce | flops 8192 | bytes 65536
  1157.7 6.1 fusion.298
  1167.9 153.4 %reduce-scatter.11.cloned.1.call-done = f32[3,256,512]{1,2,0:T(8,128)} async-done(((f32[3,2048,512]{1,2,0:T(8,128)}), f32[3,256,512]{1,2,0:T(8,128)}) %reduce-scatter.11.cloned.1.call-update) | async-done | bytes 1572880 | tf_op jit(solution)/shard_map/reduce_scatter | solution.py:253
  1324.3 404.3 %reduce-scatter.15.cloned.1.call-done = f32[2,256,1536]{1,2,0:T(8,128)} async-done(((f32[2,2048,1536]{1,2,0:T(8,128)}), f32[2,256,1536]{1,2,0:T(8,128)}) %reduce-scatter.15.cloned.1.call-update) | async-done | bytes 3145744 | tf_op jit(solution)/shard_map/reduce_scatter | solution.py:255
  1728.6 3.5 copy.197
  1732.1 88.1 %reduce-scatter.13.cloned.1.call-done = f32[512,256]{1,0:T(8,128)} async-done(((f32[512,2048]{1,0:T(8,128)}), f32[512,256]{1,0:T(8,128)}) %reduce-scatter.13.cloned.1.call-update) | async-done | bytes 524304 | tf_op jit(solution)/shard_map/reduce_scatter | solution.py:254
  1820.2 212.0 %reduce-scatter.17.cloned.1.call-done = f32[1536,256]{1,0:T(8,128)} async-done(((f32[1536,2048]{1,0:T(8,128)}), f32[1536,256]{1,0:T(8,128)}) %reduce-scatter.17.cloned.1.call-update) | async-done | bytes 1572880 | tf_op jit(solution)/shard_map/reduce_scatter | solution.py:256
  (340 shorter events, 110.6 us)
Async XLA Ops:
  7.2 49.2 %all-gather.11.cloned.1.call-start = ((), (), s32[]{:S(2)}) async-start(), calls=%async_computation.6 | async-start | bytes 5242880 | tf_op jit(solution)/shard_map/all_gather | solution.py:203
  7.9 141.5 %all-gather.13.cloned.1.call-start = ((), (), s32[]{:S(2)}) async-start(), calls=%async_computation.7 | async-start | bytes 7077888 | tf_op jit(solution)/shard_map/all_gather | solution.py:229
  10.3 190.5 %all-gather.15.cloned.1.call-start = ((), (), s32[]{:S(2)}) async-start(), calls=%async_computation.8 | async-start | bytes 2359296 | tf_op jit(solution)/shard_map/all_gather | solution.py:230
  11.0 236.6 %all-gather.21.cloned.1.call-start = ((), (), s32[]{:S(2)}) async-start(), calls=%async_computation.13 | async-start | bytes 5242880 | tf_op jit(solution)/shard_map/all_gather | solution.py:204
  11.6 325.1 %all-gather.19.cloned.1.call-start = ((), (), s32[]{:S(2)}) async-start(), calls=%async_computation.10 | async-start | bytes 7077888 | tf_op jit(solution)/shard_map/all_gather | solution.py:232
  12.2 478.4 %all-reduce.16.cloned.1.call-start = ((), (), s32[]{:S(2)}) async-start(), calls=%async_computation.20 | async-start | bytes 16777216 | tf_op jit(solution)/shard_map/psum | solution.py:94
  34.9 128.3 %copy-start.80 = (f32[8,1,256]{2,1,0:T(1,128)}, f32[8,1,256]{2,1,0:T(1,128)S(1)}, u32[]{:S(2)}) copy-start(f32[8,1,256]{2,1,0:T(1,128)S(1)} %convert_element_type.229) | copy-start | bytes 24580
  51.2 112.0 %copy-start.68 = (f32[8,1,256]{2,1,0:T(1,128)}, f32[8,1,256]{2,1,0:T(1,128)S(1)}, u32[]{:S(2)}) copy-start(f32[8,1,256]{2,1,0:T(1,128)S(1)} %convert_element_type.228) | copy-start | bytes 24580
  56.4 128.5 %copy-start.49 = (f32[512,64]{1,0:T(8,128)}, f32[512,64]{1,0:T(8,128)S(1)}, u32[]{:S(2)}) copy-start(f32[512,64]{1,0:T(8,128)S(1)} %get-tuple-element.143) | copy-start | bytes 393220
  59.8 96.2 %copy-start.70 = (f32[512]{0:T(512)}, f32[512]{0:T(512)S(1)}, u32[]{:S(2)}) copy-start(f32[512]{0:T(512)S(1)} %get-tuple-element.162) | copy-start | bytes 6148
  59.8 103.5 %copy-start.72 = (f32[512]{0:T(512)}, f32[512]{0:T(512)S(1)}, u32[]{:S(2)}) copy-start(f32[512]{0:T(512)S(1)} %get-tuple-element.163) | copy-start | bytes 6148
  62.0 94.0 %copy-start.86 = (f32[512]{0:T(512)}, f32[512]{0:T(512)S(1)}, u32[]{:S(2)}) copy-start(f32[512]{0:T(512)S(1)} %get-tuple-element.65) | copy-start | bytes 6148
  62.6 100.7 %copy-start.82 = (f32[512]{0:T(512)}, f32[512]{0:T(512)S(1)}, u32[]{:S(2)}) copy-start(f32[512]{0:T(512)S(1)} %fusion.209) | copy-start | bytes 6148
  62.6 93.4 %copy-start.74 = (f32[512]{0:T(512)}, f32[512]{0:T(512)S(1)}, u32[]{:S(2)}) copy-start(f32[512]{0:T(512)S(1)} %fusion.211) | copy-start | bytes 6148
  197.3 8.6 copy-start.57
  210.9 35.5 %copy-start.94 = (s32[4]{0:T(128)S(1)}, s32[4]{0:T(128)}, u32[]{:S(2)}) copy-start(s32[4]{0:T(128)} %param.14) | copy-start | bytes 52
  210.9 458.5 %all-gather.17.cloned.1.call-start = ((), (), s32[]{:S(2)}) async-start(), calls=%async_computation.9 | async-start | bytes 14155776 | tf_op jit(solution)/shard_map/all_gather | solution.py:231
  211.6 673.6 %all-reduce.14.cloned.1.call-start = ((), (), s32[]{:S(2)}) async-start(), calls=%async_computation.19 | async-start | bytes 16777216 | tf_op jit(solution)/shard_map/psum | solution.py:122
  336.7 7.7 copy-start.45
  336.7 7.7 copy-start.89
  680.1 7.6 copy-start.18
  687.7 23.1 %copy-start.59 = (bf16[1,512,1536]{2,1,0:T(8,128)(2,1)}, bf16[1,512,1536]{2,1,0:T(8,128)(2,1)S(1)}, u32[]{:S(2)}) copy-start(bf16[1,512,1536]{2,1,0:T(8,128)(2,1)S(1)} %get-tuple-element.86) | copy-start | bytes 4718596
  691.5 19.2 copy-start.60
  691.5 10.5 copy-start.20
  702.0 7.6 copy-start.19
  709.6 12.9 copy-start.24
  710.8 11.7 copy-start.26
  733.6 304.8 %reduce-scatter.7.cloned.1.call-start = ((), (), s32[]{:S(2)}) async-start(), calls=%async_computation.11 | async-start | bytes 2621440 | tf_op jit(solution)/shard_map/reduce_scatter | solution.py:108
  744.8 295.4 %reduce-scatter.9.cloned.1.call-start = ((), (), s32[]{:S(2)}) async-start(), calls=%async_computation.12 | async-start | bytes 2621440 | tf_op jit(solution)/shard_map/reduce_scatter | solution.py:108
  754.4 355.4 %all-reduce.12.cloned.1.call-start = ((), (), s32[]{:S(2)}) async-start(), calls=%async_computation.18 | async-start | bytes 16777216 | tf_op jit(solution)/shard_map/psum | solution.py:170
  885.2 8.9 copy-start.4
  885.2 8.9 copy-start.12
  885.2 9.9 copy-start.16
  885.2 11.5 copy-start.17
  902.7 10.5 copy-start.15
  902.7 5.1 copy-start.10
  950.0 6.7 copy-start.71
  950.0 6.7 copy-start.75
  950.0 371.2 %reduce-scatter.11.cloned.1.call-start = ((), (), s32[]{:S(2)}) async-start(), calls=%async_computation.14 | async-start | bytes 14155776 | tf_op jit(solution)/shard_map/reduce_scatter | solution.py:253
  951.2 5.6 copy-start.1
  965.9 15.4 copy-start.25
  965.9 15.3 copy-start.27
  965.9 762.6 %reduce-scatter.15.cloned.1.call-start = ((), (), s32[]{:S(2)}) async-start(), calls=%async_computation.16 | async-start | bytes 28311552 | tf_op jit(solution)/shard_map/reduce_scatter | solution.py:255
  999.9 820.3 %reduce-scatter.13.cloned.1.call-start = ((), (), s32[]{:S(2)}) async-start(), calls=%async_computation.15 | async-start | bytes 4718592 | tf_op jit(solution)/shard_map/reduce_scatter | solution.py:254
  1008.0 1024.2 %reduce-scatter.17.cloned.1.call-start = ((), (), s32[]{:S(2)}) async-start(), calls=%async_computation.17 | async-start | bytes 14155776 | tf_op jit(solution)/shard_map/reduce_scatter | solution.py:256
  1008.5 13.0 copy-start.46
  1109.8 47.9 %copy-start.87 = (f32[512]{0:T(512)S(1)}, f32[512]{0:T(512)}, u32[]{:S(2)}) copy-start(f32[512]{0:T(512)} %copy-done.86) | copy-start | bytes 6148
  1109.8 47.9 %copy-start.85 = (f32[512]{0:T(512)S(1)}, f32[512]{0:T(512)}, u32[]{:S(2)}) copy-start(f32[512]{0:T(512)} %copy-done.84) | copy-start | bytes 6148
  (63 other events, 131.3 us)
Sparse Core Ops, SparseCore 0:
  9.6 37.1 all-gather.10
  49.4 99.9 all-gather.12
  151.5 49.2 all-gather.14
  202.2 32.6 all-gather.20
  236.8 99.9 all-gather.18
  339.2 151.3 all-reduce.15
  492.8 176.5 all-gather.16
  733.8 151.3 all-reduce.13
  887.7 31.5 reduce-scatter.6
  922.4 31.4 reduce-scatter.8
  956.5 153.2 all-reduce.11
  1113.2 207.9 reduce-scatter.10
  1325.1 403.3 reduce-scatter.14
  1732.6 87.5 reduce-scatter.12
  1824.6 207.4 reduce-scatter.16
where the time goes:
time: 2050 us; the launch traced here: 2040 us
  waiting for transfers between devices  1550 us (76%)
  matrix products  216 us (11%)
  blocking collectives  112 us (5%)
  other arithmetic  85 us (4%)
  local copies, waits for them, and re-layouts  59.2 us (3%)
    reduce_scatter x1, waiting for transfers between devices, on_device(): lax.psum_scatter(totals[2], 'wide', scatter_dimension=1, tiled=True)  404 us
    reduce_scatter x1, waiting for transfers between devices, on_device(): lax.psum_scatter(totals[3], 'wide', scatter_dimension=1, tiled=True)  212 us
    all_gather x1, waiting for transfers between devices, on_device(): lax.all_gather(w_gate_up, 'wide', axis=1, tiled=True)  170 us
    reduce_scatter x1, waiting for transfers between devices, on_device(): lax.psum_scatter(totals[0], 'wide', scatter_dimension=1, tiled=True)  153 us
    psum x1, waiting for transfers between devices, micro_pass(): middle = inputs + lax.psum(heads_part, 'narrow')  141 us
    psum x1, waiting for transfers between devices, micro_pass(): normed_two_grad = lax.psum(normed_two_part, 'narrow')  131 us
    all_gather x1, waiting for transfers between devices, on_device(): lax.all_gather(w_down, 'wide', axis=1, tiled=True)  89.1 us
    reduce_scatter x1, waiting for transfers between devices, on_device(): lax.psum_scatter(totals[1], 'wide', scatter_dimension=1, tiled=True)  88.1 us
  transfers between devices with their start and end apart: 15, of which 11 were waited for; matrix products, arithmetic and copies ran while one was open for 14% of the time, Pallas kernels for 0%

commit v1 on v0

v1 whole, which is shorter than its diff:
```python
import functools

import jax
import jax.numpy as jnp
from jax import lax
from jax.experimental import pallas as pl
from jax.experimental.pallas import tpu as pltpu
from jax.sharding import Mesh
from jax.sharding import PartitionSpec as P

HEAD_DIM = 128
EPS = 1e-05
BF = jnp.bfloat16
F32 = jnp.float32
MESH = pl.DeviceIdType.MESH
VMEM_BYTES = 60 * 2**20
SWAP = [(0, 1), (1, 0)]
ANY = pl.BlockSpec(memory_space=pl.ANY)
VMEM = pl.BlockSpec(memory_space=pltpu.VMEM)
SMEM = pl.BlockSpec(memory_space=pltpu.SMEM)


def dot(a, b):
    return jnp.dot(a, b, preferred_element_type=F32)


def dot_nt(a, b):
    return lax.dot_general(a, b, (((1,), (1,)), ((), ())), preferred_element_type=F32)


def dot_tn(a, b):
    return lax.dot_general(a, b, (((0,), (0,)), ((), ())), preferred_element_type=F32)


def normalise(v):
    centred = v - jnp.mean(v, axis=-1, keepdims=True)
    rstd = lax.rsqrt(jnp.mean(centred * centred, axis=-1, keepdims=True) + EPS)
    return centred * rstd, rstd


def norm_back(xhat, rstd, grad, gain):
    dx = grad * gain
    a = jnp.mean(dx, axis=-1, keepdims=True)
    b = jnp.mean(dx * xhat, axis=-1, keepdims=True)
    return rstd * (dx - a - xhat * b)


def cost(us, sent=0):
    return pl.CostEstimate(flops=int(us * 1e9), bytes_accessed=int(us * 3.2e6), transcendentals=0)


class Place:
    def __init__(self):
        self.y = lax.axis_index("y")
        self.n = lax.axis_index("n")
        self.x = self.n // 2
        self.c = self.n % 2
        self.ns = self.n + 1 - 2 * self.c
        self.nx = (self.n + 2) % 4
        self.nd = (self.ns + 2) % 4
        self.sib = {"n": self.ns}
        self.xn = {"n": self.nx}
        self.yn = {"y": 1 - self.y}
        self.xs = {"n": self.nd}


def meet(devices):
    barrier = pltpu.get_barrier_semaphore()
    for d in devices:
        pl.semaphore_signal(barrier, inc=1, device_id=d, device_id_type=MESH)
    pl.semaphore_wait(barrier, len(devices))


class Wire:
    def __init__(self, send_sems, recv_sems, first=0):
        self.ss, self.rs, self.at, self.sent = send_sems, recv_sems, first, []

    def make(self, src, dst, device):
        k = self.at
        self.at += 1
        copy = pltpu.make_async_remote_copy(
            src_ref=src, dst_ref=dst, send_sem=self.ss.at[k], recv_sem=self.rs.at[k],
            device_id=device, device_id_type=MESH,
        )
        self.sent.append(copy)
        return copy

    def finish(self):
        for copy in self.sent:
            copy.wait_send()


SPREAD = 9


class Spread:
    def __init__(self, wire, at, src, slot):
        y, n, nx = at.y, at.n, at.nx
        self.first = [
            wire.make(src, slot(y, n, None), at.xn),
            wire.make(src, slot(y, n, None), at.yn),
            wire.make(src, slot(y, n, None), at.sib),
        ]
        self.on_x = [
            wire.make(slot(y, nx, 0), slot(y, nx, 0), at.yn),
            wire.make(slot(y, nx, None), slot(y, nx, None), at.sib),
        ]
        self.on_y = [
            wire.make(slot(1 - y, n, 1), slot(1 - y, n, 1), at.xn),
            wire.make(slot(1 - y, n, None), slot(1 - y, n, None), at.sib),
        ]
        self.last = [
            wire.make(slot(1 - y, nx, 0), slot(1 - y, nx, 0), at.sib),
            wire.make(slot(1 - y, nx, 1), slot(1 - y, nx, 1), at.sib),
        ]

    def begin(self):
        for copy in self.first:
            copy.start()

    def forward(self):
        self.first[0].wait_recv()
        for copy in self.on_x:
            copy.start()
        self.first[1].wait_recv()
        for copy in self.on_y:
            copy.start()

    def forward_last(self):
        self.on_x[0].wait_recv()
        self.last[0].start()
        self.on_y[0].wait_recv()
        self.last[1].start()

    def end(self):
        self.first[2].wait_recv()
        self.on_x[1].wait_recv()
        self.on_y[1].wait_recv()
        self.last[0].wait_recv()
        self.last[1].wait_recv()


REDUCE = 10


def reduce_scratch(micro, tok, sub, width):
    half = sub // 2
    return [
        pltpu.VMEM((micro, 2, tok, width), BF),
        pltpu.VMEM((micro, 2, 2, sub, width), BF),
        pltpu.VMEM((micro, sub, width), BF),
        pltpu.VMEM((micro, sub, width), BF),
        pltpu.VMEM((micro, sub, width), BF),
        pltpu.VMEM((micro, 2, half, width), BF),
        pltpu.VMEM((micro, sub, width), BF),
        pltpu.VMEM((micro, sub, width), BF),
    ]


def reduce_rows(wire, at, scratch, compute, finish):
    part, ra, sb, sx, sy, rb, rcx, rcy = scratch
    micro, sub = sb.shape[0], sb.shape[1]
    half = sub // 2
    y, x, c, n = at.y, at.x, at.c, at.n

    def rows(core, xx, lo=0, size=sub):
        return pl.ds(pl.multiple_of((2 * xx + core) * sub, sub) + lo, size)

    a = {}
    for m in range(micro):
        for yk, yy in ((1, 1 - y), (0, y)):
            compute(m, yy)
            for xk, xx in ((1, 1 - x), (0, x)):
                copy = wire.make(part.at[m, yy, rows(1 - c, xx)], ra.at[m, yy, xx], at.sib)
                copy.start()
                a[m, yk, xk] = copy

    def summed(m, yy, xx, lo, size):
        return part[m, yy, rows(c, xx, lo, size), :].astype(F32) + ra[m, yy, xx, lo : lo + size, :].astype(F32)

    b = {}
    for m in range(micro):
        a[m, 1, 1].wait_recv()
        sb[m] = summed(m, 1 - y, 1 - x, 0, sub).astype(BF)
        b[m, 0] = wire.make(sb.at[m, 0:half], rb.at[m, 0], at.xn)
        b[m, 1] = wire.make(sb.at[m, half:sub], rb.at[m, 1], at.yn)
        b[m, 0].start()
        b[m, 1].start()
    d = {}
    for m in range(micro):
        a[m, 1, 0].wait_recv()
        sy[m, half:sub] = summed(m, 1 - y, x, half, half).astype(BF)
        d[m, 0] = wire.make(sy.at[m, half:sub], rcy.at[m, half:sub], at.yn)
        d[m, 0].start()
        a[m, 0, 1].wait_recv()
        sx[m, 0:half] = summed(m, y, 1 - x, 0, half).astype(BF)
        d[m, 1] = wire.make(sx.at[m, 0:half], rcx.at[m, 0:half], at.xn)
        d[m, 1].start()
        b[m, 0].wait_recv()
        sy[m, 0:half] = (summed(m, 1 - y, x, 0, half) + rb[m, 0].astype(F32)).astype(BF)
        d[m, 2] = wire.make(sy.at[m, 0:half], rcy.at[m, 0:half], at.yn)
        d[m, 2].start()
        b[m, 1].wait_recv()
        sx[m, half:sub] = (summed(m, y, 1 - x, half, half) + rb[m, 1].astype(F32)).astype(BF)
        d[m, 3] = wire.make(sx.at[m, half:sub], rcx.at[m, half:sub], at.xn)
        d[m, 3].start()
    for m in range(micro):
        a[m, 0, 0].wait_recv()
        for k in range(4):
            d[m, k].wait_recv()
        finish(m, lambda lo, size, m=m: summed(m, y, x, lo, size) + rcx[m, lo : lo + size, :].astype(F32) + rcy[m, lo : lo + size, :].astype(F32))


def blockwise(part, m, yy, fn, tile=256):
    tok = part.shape[2]

    def step(i, carry):
        lo = pl.multiple_of(i * tile, tile)
        fn(lo, tile)
        return carry

    lax.fori_loop(0, tok // tile, step, 0)


def gather_kernel(zn, x_in, d_in, v_in, x_out, d_out, v_out, ss, rs, ls):
    at = Place()
    z = lax.axis_index("z")
    micro, tok, feat = x_in.shape
    ring = [(dz, dy) for dz in range(zn) for dy in range(2) if dz or dy]
    others = [{"z": (z + dz) % zn, "y": (at.y + dy) % 2} for dz, dy in ring]
    meet([at.sib, at.xn] + others)
    wire = Wire(ss, rs)
    half = tok // 2
    spreads, local = [], []
    for src, out in ((x_in, x_out), (d_in, d_out)):
        for m in range(micro):

            def slot(yy, nn, part, m=m, out=out):
                lo, size = (0, tok) if part is None else (part * half, half)
                return out.at[m, yy, pl.ds(lo, size), pl.ds(pl.multiple_of(nn * feat, feat), feat)]

            spreads.append(Spread(wire, at, src.at[m], slot))
            local.append(pltpu.make_async_copy(src.at[m], slot(at.y, at.n, None), ls.at[len(local)]))
    local.append(pltpu.make_async_copy(v_in, v_out.at[z, at.y], ls.at[len(local)]))
    small = [wire.make(v_in, v_out.at[z, at.y], d) for d in others]
    for copy in small:
        copy.start()
    for s in spreads:
        s.begin()
    for copy in local:
        copy.start()
    for s in spreads:
        s.forward()
    for s in spreads:
        s.forward_last()
    for s in spreads:
        s.end()
    for copy in small:
        copy.wait_recv()
    wire.finish()
    for copy in local:
        copy.wait()


def gather_all(x, d, v, zn):
    micro, tok, feat = x.shape
    whole = jax.ShapeDtypeStruct((micro, 2, tok, 4 * feat), BF)
    count = SPREAD * 2 * micro + 2 * zn - 1
    return pl.pallas_call(
        functools.partial(gather_kernel, zn),
        out_shape=(whole, whole, jax.ShapeDtypeStruct((zn, 2) + v.shape, F32)),
        in_specs=[ANY] * 3,
        out_specs=(ANY,) * 3,
        scratch_shapes=[
            pltpu.SemaphoreType.DMA((count,)),
            pltpu.SemaphoreType.DMA((count,)),
            pltpu.SemaphoreType.DMA((2 * micro + 1,)),
        ],
        compiler_params=pltpu.CompilerParams(collective_id=0, has_side_effects=True, vmem_limit_bytes=VMEM_BYTES),
        cost_estimate=cost(45),
        name="gather_all",
    )(x, d, v)


def row_slot(out, m, sub):
    half = sub // 2

    def slot(yy, nn, part):
        ref = out.at[m, yy, nn]
        return ref if part is None else ref.at[pl.ds(part * half, half)]

    return slot


def run_spreads(spreads, local):
    for s in spreads:
        s.forward()
    for s in spreads:
        s.forward_last()
    for s in spreads:
        s.end()
    for copy in local:
        copy.wait()


def attn_out_kernel(att, wo, x_all, gain, shift, middle, n2, *scratch):
    *red, xb, nb, ss, rs, ls = scratch
    at = Place()
    micro, sub, width = middle.shape
    zn, _, dz = wo.shape
    tok = red[0].shape[2]
    meet([at.sib, at.xn, at.yn])
    wire = Wire(ss, rs)
    own = [pltpu.make_async_copy(x_all.at[m, at.y, pl.ds(at.n * sub, sub)], xb.at[m], ls.at[m]) for m in range(micro)]
    for copy in own:
        copy.start()

    def compute(m, yy):
        def tile(lo, size):
            a = att[pl.ds(pl.multiple_of((m * 2 + yy) * tok, tok) + lo, size), :]
            for k in range(zn):
                red[0][m, yy, pl.ds(lo, size), k * dz : (k + 1) * dz] = dot(a, wo[k]).astype(BF)

        blockwise(red[0], m, yy, tile)

    spreads, local = [], []

    def finish(m, total):
        own[m].wait()
        step = sub // 2
        for lo in range(0, sub, step):
            mid = xb[m, lo : lo + step, :].astype(F32) + total(lo, step)
            middle[m, lo : lo + step, :] = mid
            xhat, _ = normalise(mid)
            nb[m, lo : lo + step, :] = (xhat * gain[...] + shift[...]).astype(BF)
        slot = row_slot(n2, m, sub)
        spreads.append(Spread(wire, at, nb.at[m], slot))
        spreads[-1].begin()
        local.append(pltpu.make_async_copy(nb.at[m], slot(at.y, at.n, None), ls.at[micro + m]))
        local[-1].start()

    reduce_rows(wire, at, red, compute, finish)
    run_spreads(spreads, local)
    wire.finish()


def attn_out(att, wo, x_all, gain, shift):
    micro, _, tok, width = x_all.shape
    sub = tok // 4
    count = (REDUCE + SPREAD) * micro
    return pl.pallas_call(
        attn_out_kernel,
        out_shape=(
            jax.ShapeDtypeStruct((micro, sub, width), F32),
            jax.ShapeDtypeStruct((micro, 2, 4, sub, width), BF),
        ),
        in_specs=[VMEM, VMEM, ANY, VMEM, VMEM],
        out_specs=(VMEM, ANY),
        scratch_shapes=reduce_scratch(micro, tok, sub, width)
        + [
            pltpu.VMEM((micro, sub, width), BF),
            pltpu.VMEM((micro, sub, width), BF),
            pltpu.SemaphoreType.DMA((count,)),
            pltpu.SemaphoreType.DMA((count,)),
            pltpu.SemaphoreType.DMA((2 * micro,)),
        ],
        compiler_params=pltpu.CompilerParams(collective_id=1, has_side_effects=True, vmem_limit_bytes=VMEM_BYTES),
        cost_estimate=cost(85),
        name="attn_out",
    )(att, wo, x_all, gain, shift)


def nt_compute(part, low, w):
    zn, dz, _ = w.shape
    tok = part.shape[2]

    def compute(m, yy):
        def tile(lo, size):
            a = low[pl.ds(pl.multiple_of((m * 2 + yy) * tok, tok) + lo, size), :]
            for k in range(zn):
                part[m, yy, pl.ds(lo, size), k * dz : (k + 1) * dz] = dot_nt(a, w[k]).astype(BF)

        blockwise(part, m, yy, tile)

    return compute


def ffn_back_kernel(gul, wgu, d_all, middle, gain, mid_grad, branch, vec, *scratch):
    *red, db, nb, ss, rs, ls = scratch
    at = Place()
    micro, sub, width = middle.shape
    meet([at.sib, at.xn, at.yn])
    wire = Wire(ss, rs)
    own = [pltpu.make_async_copy(d_all.at[m, at.y, pl.ds(at.n * sub, sub)], db.at[m], ls.at[m]) for m in range(micro)]
    for copy in own:
        copy.start()
    vec[...] = jnp.zeros_like(vec)
    spreads, local = [], []

    def finish(m, total):
        own[m].wait()
        step = sub // 2
        for lo in range(0, sub, step):
            grad = total(lo, step)
            xhat, rstd = normalise(middle[m, lo : lo + step, :])
            vec[0:1, :] += jnp.sum(grad * xhat, axis=0, keepdims=True)
            vec[1:2, :] += jnp.sum(grad, axis=0, keepdims=True)
            mg = db[m, lo : lo + step, :].astype(F32) + norm_back(xhat, rstd, grad, gain[...])
            mid_grad[m, lo : lo + step, :] = mg
            nb[m, lo : lo + step, :] = mg.astype(BF)
        slot = row_slot(branch, m, sub)
        spreads.append(Spread(wire, at, nb.at[m], slot))
        spreads[-1].begin()
        local.append(pltpu.make_async_copy(nb.at[m], slot(at.y, at.n, None), ls.at[micro + m]))
        local[-1].start()

    reduce_rows(wire, at, red, nt_compute(red[0], gul, wgu), finish)
    run_spreads(spreads, local)
    wire.finish()


def ffn_back(gul, wgu, d_all, middle, gain):
    micro, _, tok, width = d_all.shape
    sub = tok // 4
    count = (REDUCE + SPREAD) * micro
    return pl.pallas_call(
        ffn_back_kernel,
        out_shape=(
            jax.ShapeDtypeStruct((micro, sub, width), F32),
            jax.ShapeDtypeStruct((micro, 2, 4, sub, width), BF),
            jax.ShapeDtypeStruct((8, width), F32),
        ),
        in_specs=[VMEM, VMEM, ANY, VMEM, VMEM],
        out_specs=(VMEM, ANY, VMEM),
        scratch_shapes=reduce_scratch(micro, tok, sub, width)
        + [
            pltpu.VMEM((micro, sub, width), BF),
            pltpu.VMEM((micro, sub, width), BF),
            pltpu.SemaphoreType.DMA((count,)),
            pltpu.SemaphoreType.DMA((count,)),
            pltpu.SemaphoreType.DMA((2 * micro,)),
        ],
        compiler_params=pltpu.CompilerParams(collective_id=2, has_side_effects=True, vmem_limit_bytes=VMEM_BYTES),
        cost_estimate=cost(95),
        name="ffn_back",
    )(gul, wgu, d_all, middle, gain)


class Deal:
    def __init__(self, wire, at, rows, out, m, sems, k):
        sub, width = rows.shape[1], rows.shape[2]
        feat = width // 4

        def cols(nn):
            return rows.at[m, :, pl.ds(pl.multiple_of(nn * feat, feat), feat)]

        place = out.at[m, pl.ds(pl.multiple_of(at.n * sub, sub), sub)]
        self.local = pltpu.make_async_copy(cols(at.n), place, sems.at[k])
        self.copies = [
            wire.make(cols(at.nx), place, at.xn),
            wire.make(cols(at.nd), place, at.xs),
            wire.make(cols(at.ns), place, at.sib),
        ]

    def begin(self):
        for copy in self.copies:
            copy.start()
        self.local.start()

    def end(self):
        for copy in self.copies:
            copy.wait_recv()
        self.local.wait()


def attn_back_kernel(low, w, x_all, mid_grad, gain, out, vec, *scratch):
    *red, xb, ob, ss, rs, ls = scratch
    at = Place()
    micro, sub, width = mid_grad.shape
    meet([at.sib, at.xn, at.yn, at.xs])
    wire = Wire(ss, rs)
    own = [pltpu.make_async_copy(x_all.at[m, at.y, pl.ds(at.n * sub, sub)], xb.at[m], ls.at[m]) for m in range(micro)]
    for copy in own:
        copy.start()
    vec[...] = jnp.zeros_like(vec)
    deals = []

    def finish(m, total):
        own[m].wait()
        step = sub // 2
        for lo in range(0, sub, step):
            grad = total(lo, step)
            xhat, rstd = normalise(xb[m, lo : lo + step, :].astype(F32))
            vec[0:1, :] += jnp.sum(grad * xhat, axis=0, keepdims=True)
            vec[1:2, :] += jnp.sum(grad, axis=0, keepdims=True)
            ob[m, lo : lo + step, :] = (
                mid_grad[m, lo : lo + step, :] + norm_back(xhat, rstd, grad, gain[...])
            ).astype(BF)
        deals.append(Deal(wire, at, ob, out, m, ls, micro + m))
        deals[-1].begin()

    reduce_rows(wire, at, red, nt_compute(red[0], low, w), finish)
    for deal in deals:
        deal.end()
    wire.finish()


def attn_back(low, w, x_all, mid_grad, gain):
    micro, _, tok, width = x_all.shape
    sub = tok // 4
    count = (REDUCE + 3) * micro
    return pl.pallas_call(
        attn_back_kernel,
        out_shape=(
            jax.ShapeDtypeStruct((micro, tok, width // 4), BF),
            jax.ShapeDtypeStruct((8, width), F32),
        ),
        in_specs=[VMEM, VMEM, ANY, VMEM, VMEM],
        out_specs=(ANY, VMEM),
        scratch_shapes=reduce_scratch(micro, tok, sub, width)
        + [
            pltpu.VMEM((micro, sub, width), BF),
            pltpu.VMEM((micro, sub, width), BF),
            pltpu.SemaphoreType.DMA((count,)),
            pltpu.SemaphoreType.DMA((count,)),
            pltpu.SemaphoreType.DMA((2 * micro,)),
        ],
        compiler_params=pltpu.CompilerParams(collective_id=3, has_side_effects=True, vmem_limit_bytes=VMEM_BYTES),
        cost_estimate=cost(55),
        name="attn_back",
    )(low, w, x_all, mid_grad, gain)


def ffn_out_kernel(hidden, wd, middle, out, *scratch):
    *red, ob, ss, rs, ls = scratch
    at = Place()
    micro, sub, width = middle.shape
    zn, _, dz = wd.shape
    tok = red[0].shape[2]
    meet([at.sib, at.xn, at.yn, at.xs])
    wire = Wire(ss, rs)

    def compute(m, yy):
        def tile(lo, size):
            a = hidden[pl.ds(pl.multiple_of((m * 2 + yy) * tok, tok) + lo, size), :]
            for k in range(zn):
                red[0][m, yy, pl.ds(lo, size), k * dz : (k + 1) * dz] = dot(a, wd[k]).astype(BF)

        blockwise(red[0], m, yy, tile)

    deals = []

    def finish(m, total):
        step = sub // 2
        for lo in range(0, sub, step):
            ob[m, lo : lo + step, :] = (middle[m, lo : lo + step, :] + total(lo, step)).astype(BF)
        deals.append(Deal(wire, at, ob, out, m, ls, m))
        deals[-1].begin()

    reduce_rows(wire, at, red, compute, finish)
    for deal in deals:
        deal.end()
    wire.finish()


def ffn_out(hidden, wd, middle, tok):
    micro, sub, width = middle.shape
    count = (REDUCE + 3) * micro
    return pl.pallas_call(
        ffn_out_kernel,
        out_shape=jax.ShapeDtypeStruct((micro, tok, width // 4), BF),
        in_specs=[VMEM, VMEM, VMEM],
        out_specs=ANY,
        scratch_shapes=reduce_scratch(micro, tok, sub, width)
        + [
            pltpu.VMEM((micro, sub, width), BF),
            pltpu.SemaphoreType.DMA((count,)),
            pltpu.SemaphoreType.DMA((count,)),
            pltpu.SemaphoreType.DMA((micro,)),
        ],
        compiler_params=pltpu.CompilerParams(collective_id=4, has_side_effects=True, vmem_limit_bytes=VMEM_BYTES),
        cost_estimate=cost(55),
        name="ffn_out",
    )(hidden, wd, middle)


def local_call(body, grid, ins, in_specs, outs, out_specs, us, name, scratch=()):
    return pl.pallas_call(
        body,
        grid=grid,
        in_specs=in_specs,
        out_specs=out_specs,
        out_shape=outs,
        scratch_shapes=list(scratch),
        compiler_params=pltpu.CompilerParams(vmem_limit_bytes=VMEM_BYTES),
        cost_estimate=cost(us),
        name=name,
    )(*ins)


def tiles(rows, cols):
    return pl.BlockSpec((rows, cols), lambda i: (i, 0))


def first_norm_body(x, gain, shift, out):
    xhat, _ = normalise(x[...].astype(F32))
    out[...] = (xhat * gain[...] + shift[...]).astype(BF)


def first_norm(x, gain, shift):
    rows, width = x.shape
    tile = 256
    return local_call(
        first_norm_body, (rows // tile,), (x, gain, shift), [tiles(tile, width), VMEM, VMEM],
        jax.ShapeDtypeStruct((rows, width), BF), tiles(tile, width), 8, "first_norm",
    )


def same_protein(ends, b, tok, count):
    col = lax.broadcasted_iota(jnp.int32, (tok, 1), 0)
    row = lax.broadcasted_iota(jnp.int32, (1, tok), 1)
    pc, pr = jnp.zeros_like(col), jnp.zeros_like(row)
    for k in range(count):
        end = ends[b, k]
        pc = pc + (col >= end).astype(jnp.int32)
        pr = pr + (row >= end).astype(jnp.int32)
    return pc == pr


def turn(v, cos, sin):
    return v * cos + pltpu.roll(v, HEAD_DIM // 2, 1) * sin


def attention_body(ends, n1, w, cos, sin, qkv, att):
    zn, dz, cols = w.shape
    tok = n1.shape[0]
    heads = cols // 3 // HEAD_DIM
    span = heads * HEAD_DIM
    acc = dot(n1[:, 0:dz], w[0])
    for k in range(1, zn):
        acc = acc + dot(n1[:, k * dz : (k + 1) * dz], w[k])
    same = same_protein(ends, pl.program_id(0), tok, ends.shape[1])
    scale = HEAD_DIM ** (-0.5)
    for h in range(heads):
        lo = h * HEAD_DIM
        q = turn(acc[:, lo : lo + HEAD_DIM], cos[...], sin[...]).astype(BF)
        k = turn(acc[:, span + lo : span + lo + HEAD_DIM], cos[...], sin[...]).astype(BF)
        v = acc[:, 2 * span + lo : 2 * span + lo + HEAD_DIM].astype(BF)
        qkv[:, lo : lo + HEAD_DIM] = q
        qkv[:, span + lo : span + lo + HEAD_DIM] = k
        qkv[:, 2 * span + lo : 2 * span + lo + HEAD_DIM] = v
        s = jnp.where(same, dot_nt(q, k) * scale, -1e30)
        e = jnp.exp(s - jnp.max(s, axis=-1, keepdims=True))
        p = (e / jnp.sum(e, axis=-1, keepdims=True)).astype(BF)
        att[:, lo : lo + HEAD_DIM] = dot(p, v).astype(BF)


def attention(ends, n1, w, cos, sin):
    rows, width = n1.shape
    zn, dz, cols = w.shape
    tok = rows // ends.shape[0]
    return local_call(
        attention_body, (rows // tok,), (ends, n1, w, cos, sin),
        [SMEM, tiles(tok, width), VMEM, tiles(tok, HEAD_DIM), tiles(tok, HEAD_DIM)],
        (jax.ShapeDtypeStruct((rows, cols), BF), jax.ShapeDtypeStruct((rows, cols // 3), BF)),
        (tiles(tok, cols), tiles(tok, cols // 3)), 20, "attention",
    )


def attention_back_body(ends, branch, wo, qkv, cos, sin, low):
    zn, span, dz = wo.shape
    tok = branch.shape[0]
    heads = span // HEAD_DIM
    acc = dot_nt(branch[:, 0:dz], wo[0])
    for k in range(1, zn):
        acc = acc + dot_nt(branch[:, k * dz : (k + 1) * dz], wo[k])
    same = same_protein(ends, pl.program_id(0), tok, ends.shape[1])
    scale = HEAD_DIM ** (-0.5)
    for h in range(heads):
        lo = h * HEAD_DIM
        ag = acc[:, lo : lo + HEAD_DIM].astype(BF)
        q = qkv[:, lo : lo + HEAD_DIM]
        k = qkv[:, span + lo : span + lo + HEAD_DIM]
        v = qkv[:, 2 * span + lo : 2 * span + lo + HEAD_DIM]
        s = jnp.where(same, dot_nt(q, k) * scale, -1e30)
        e = jnp.exp(s - jnp.max(s, axis=-1, keepdims=True))
        p = e / jnp.sum(e, axis=-1, keepdims=True)
        pg = dot_nt(ag, v)
        vg = dot_tn(p.astype(BF), ag)
        rd = jnp.sum(p * pg, axis=-1, keepdims=True)
        sg = (p * (pg - rd)).astype(BF)
        qg = dot(sg, k) * scale
        kg = dot_tn(sg, q) * scale
        low[:, lo : lo + HEAD_DIM] = turn(qg, cos[...], -sin[...]).astype(BF)
        low[:, span + lo : span + lo + HEAD_DIM] = turn(kg, cos[...], -sin[...]).astype(BF)
        low[:, 2 * span + lo : 2 * span + lo + HEAD_DIM] = vg.astype(BF)


def attention_back(ends, branch, wo, qkv, cos, sin):
    rows, width = branch.shape
    cols = qkv.shape[1]
    tok = rows // ends.shape[0]
    return local_call(
        attention_back_body, (rows // tok,), (ends, branch, wo, qkv, cos, sin),
        [SMEM, tiles(tok, width), VMEM, tiles(tok, cols), tiles(tok, HEAD_DIM), tiles(tok, HEAD_DIM)],
        jax.ShapeDtypeStruct((rows, cols), BF), tiles(tok, cols), 25, "attention_back",
    )


def gate_up_body(n2, w, mask, gu, hidden):
    zn, dz, cols = w.shape
    half = cols // 2
    acc = dot(n2[:, 0:dz], w[0])
    for k in range(1, zn):
        acc = acc + dot(n2[:, k * dz : (k + 1) * dz], w[k])
    gu[...] = acc
    g, u = acc[:, :half], acc[:, half:]
    hidden[...] = (g * (0.5 * (1.0 + lax.erf(g * (0.5**0.5)))) * u * mask[...]).astype(BF)


def gate_up(n2, w, mask):
    rows, width = n2.shape
    cols = w.shape[2]
    tile = 256
    return local_call(
        gate_up_body, (rows // tile,), (n2, w, mask), [tiles(tile, width), VMEM, VMEM],
        (jax.ShapeDtypeStruct((rows, cols), F32), jax.ShapeDtypeStruct((rows, cols // 2), BF)),
        (tiles(tile, cols), tiles(tile, cols // 2)), 20, "gate_up",
    )


def hidden_back_body(dy, w, gu, mask, low):
    zn, half, dz = w.shape
    hg = dot_nt(dy[:, 0:dz], w[0])
    for k in range(1, zn):
        hg = hg + dot_nt(dy[:, k * dz : (k + 1) * dz], w[k])
    hg = hg * mask[...]
    g, u = gu[:, :half], gu[:, half:]
    phi = 0.5 * (1.0 + lax.erf(g * (0.5**0.5)))
    slope = phi + g * jnp.exp(-0.5 * g * g) * 0.3989422804014327
    low[:, :half] = (hg * u * slope).astype(BF)
    low[:, half:] = (hg * (g * phi)).astype(BF)


def hidden_back(dy, w, gu, mask):
    rows, width = dy.shape
    cols = gu.shape[1]
    tile = 256
    return local_call(
        hidden_back_body, (rows // tile,), (dy, w, gu, mask),
        [tiles(tile, width), VMEM, tiles(tile, cols), VMEM],
        jax.ShapeDtypeStruct((rows, cols), BF), tiles(tile, cols), 15, "hidden_back",
    )


def pick(w, index, axis):
    half = w.shape[axis] // 2
    return lax.dynamic_slice_in_dim(w, index * half, half, axis)


def ordered(y, keep, got, axis):
    return jnp.concatenate([jnp.where(y == 0, keep, got), jnp.where(y == 0, got, keep)], axis=axis)


def on_device(inputs, lengths, counts, w_qkv, w_out, w_gu, w_down, g1, b1, g2, b2, dy_in):
    z = lax.axis_index("z")
    y = lax.axis_index("y")
    n = lax.axis_index("n")
    zn = lax.axis_size("z")
    micro, tok, feat = inputs.shape
    width = feat * lax.axis_size("n")
    rows = micro * 2 * tok
    blocks = micro * 2

    def columns(w):
        parts, depth, cols = w.shape
        cut = lambda i: pick(w, i, 2).transpose(1, 0, 2).reshape(depth, parts * cols // 2)
        return ordered(y, cut(y), lax.ppermute(cut(1 - y), "y", SWAP), 0)

    def lines(w):
        return ordered(y, pick(w, y, 0), lax.ppermute(pick(w, 1 - y, 0), "y", SWAP), 1)

    def gather_z(w):
        return lax.all_gather(w, "z", axis=0, tiled=False)

    wq = gather_z(columns(w_qkv))
    wo = gather_z(lines(w_out))
    wgu = gather_z(columns(w_gu))
    wd = gather_z(lines(w_down))

    vecs = jnp.stack([g1, b1, g2, b2]).astype(F32)
    vecs = jnp.pad(vecs, ((0, 4), (0, 0)))
    x_all, d_all, norms = gather_all(inputs, dy_in, vecs, zn)
    norms = norms.transpose(2, 0, 1, 3).reshape(8, width)
    gain1, shift1, gain2, shift2 = (norms[i : i + 1] for i in range(4))

    half_slots = wgu.shape[2] // 2
    own = jnp.sum(jnp.where(jnp.arange(counts.shape[0]) == n, counts, 0))
    mask = (y * half_slots + jnp.arange(half_slots) < own).astype(F32)[None]

    other = lax.ppermute(lengths, "y", SWAP)
    both = ordered(y, lengths, other, 1).reshape(blocks, -1)
    count = both.shape[1]
    upto = jnp.arange(count)[:, None] >= jnp.arange(count)[None, :]
    ends = jnp.sum(jnp.where(upto[None], both[:, None, :], 0), axis=2)
    places = jnp.arange(tok, dtype=jnp.int32)
    before = places[None, :, None] >= ends[:, None, :]
    position = places[None] - jnp.max(jnp.where(before, ends[:, None, :], 0), axis=2)
    half_dim = HEAD_DIM // 2
    frequency = 10000.0 ** (-jnp.arange(half_dim, dtype=F32) / half_dim)
    angles = position.reshape(rows, 1).astype(F32) * frequency[None]
    cos, sin = jnp.cos(angles), jnp.sin(angles)
    cos = jnp.concatenate([cos, cos], 1)
    sin = jnp.concatenate([-sin, sin], 1)

    n1 = first_norm(x_all.reshape(rows, width), gain1, shift1)
    qkv, att = attention(ends, n1, wq, cos, sin)
    middle, n2 = attn_out(att, wo, x_all, gain2, shift2)
    n2 = n2.reshape(rows, width)
    gu, hidden = gate_up(n2, wgu, mask)
    dy = d_all.reshape(rows, width)

    def weight_grad(a, b):
        return jnp.einsum("ta,tb->ab", a, b, preferred_element_type=F32).astype(BF)

    def scatter_z(g, axis):
        return lax.psum_scatter(g, "z", scatter_dimension=axis, tiled=True)

    down_s = scatter_z(weight_grad(hidden, dy), 1)
    gul = hidden_back(dy, wd, gu, mask)
    gu_s = scatter_z(weight_grad(n2, gul), 0)
    mid_grad, branch, vec2 = ffn_back(gul, wgu, d_all, middle, gain2)
    branch = branch.reshape(rows, width)
    out_s = scatter_z(weight_grad(att, branch), 1)
    low = attention_back(ends, branch, wo, qkv, cos, sin)
    qkv_s = scatter_z(weight_grad(n1, low), 0)
    in_grad, vec1 = attn_back(low, wq, x_all, mid_grad, gain1)
    layer_out = ffn_out(hidden, wd, middle, tok)

    def columns_back(r, parts):
        depth, cols = r.shape[0] // 2, r.shape[1] // parts
        cut = lambda i: pick(r, i, 0)
        full = ordered(y, cut(y).reshape(depth, parts, cols), lax.ppermute(cut(1 - y), "y", SWAP).reshape(depth, parts, cols), 2)
        return full.transpose(1, 0, 2).astype(F32)

    def lines_back(r):
        return ordered(y, pick(r, y, 1), lax.ppermute(pick(r, 1 - y, 1), "y", SWAP), 0).astype(F32)

    sums = jnp.concatenate([vec1[0:2], vec2[0:2]], axis=0)
    sums = lax.psum(sums, ("z", "y", "n"))
    mine = lax.dynamic_slice_in_dim(sums, (z * 2 + y) * g1.shape[0], g1.shape[0], 1)
    return (
        layer_out,
        in_grad,
        columns_back(qkv_s, w_qkv.shape[0]),
        lines_back(out_s),
        columns_back(gu_s, w_gu.shape[0]),
        lines_back(down_s),
        mine[0],
        mine[1],
        mine[2],
        mine[3],
    )


def solution(mesh):
    wide, narrow = mesh.shape["wide"], mesh.shape["narrow"]
    grid = Mesh(mesh.devices.reshape(wide // 2, 2, narrow), ("z", "y", "n"))
    w = ("z", "y")
    tokens, depth, lines, vector = P(None, w, "n"), P(None, w, "n"), P("n", w), P(w)
    return jax.shard_map(
        on_device,
        mesh=grid,
        in_specs=(
            tokens, P(None, w, None), P(), depth, lines, depth, lines,
            vector, vector, vector, vector, tokens,
        ),
        out_specs=(
            tokens, tokens, depth, lines, depth, lines, vector, vector, vector, vector,
        ),
        check_vma=False,
    )
```

time: 2050 us -> 721 us (0.35)
  waiting for transfers between devices: 1550 us -> 98 us
  Pallas kernels: 0 us -> 455 us
  matrix products: 216 us -> 47.8 us
  blocking collectives: 112 us -> 45.8 us
  other arithmetic: 85 us -> 21.8 us
  local copies, waits for them, and re-layouts: 59.2 us -> 17.1 us
    reduce_scatter x6 -> x4, waiting for transfers between devices: 858 us -> 26.3 us  [scatter_z(): return lax.psum_scatter(g, 'z', scatter_dimension=axis, tiled=True)]
    pallas_call x0 -> x10, Pallas kernels: none -> 455 us  [the longest x1 95.2 us: ffn_back(): pl.pallas_call(ffn_back_kernel, out_shape=(jax.ShapeDtypeStruct((micro, s...]
    psum x3 -> x0, waiting for transfers between devices: 339 us -> none  [the longest x1 141 us: micro_pass(): middle = inputs + lax.psum(heads_part, 'narrow')]
    all_gather x6 -> x4, waiting for transfers between devices: 349 us -> 32.4 us  [gather_z(): return lax.all_gather(w, 'z', axis=0, tiled=False)]
    dot_general x36 -> x4, matrix products: 216 us -> 47.8 us  [weight_grad(): return jnp.einsum('ta,tb->ab', a, b, preferred_element_type=F32).astype(BF)]
    all_gather x4 -> x0, blocking collectives: 73.1 us -> none  [the longest x1 22.3 us: on_device(): lax.all_gather(norm1_bias, 'wide', axis=0, tiled=True)]
    psum x0 -> x1, blocking collectives: none -> 45.8 us  [on_device(): sums = lax.psum(sums, ('z', 'y', 'n'))]
    unnamed x212 -> x39, local copies, waits for them, and re-layouts: 47.3 us -> 5.9 us
  transfers between devices with their start and end apart: 15 -> 17, of which waited for: 11 -> 6; matrix products, arithmetic and copies ran while one was open for 14% -> 10% of each run, Pallas kernels for 0% -> 48%
where the time goes in v1:
time: 721 us; the launch traced here: 713 us
  Pallas kernels  455 us (63%)
  waiting for transfers between devices  98 us (14%)
  matrix products  47.8 us (7%)
  blocking collectives  45.8 us (6%)
  other arithmetic  21.8 us (3%)
  local copies, waits for them, and re-layouts  17.1 us (2%)
  between operations  15.1 us (2%)
  starting transfers between devices  12.7 us (2%)
    pallas_call x1, Pallas kernels, ffn_back(): pl.pallas_call(ffn_back_kernel, out_shape=(jax.ShapeDtypeStruct((micro, s...  95.2 us
    pallas_call x5, Pallas kernels, local_call(): pl.pallas_call(body, grid=grid, in_specs=in_specs, out_specs=out_specs, o...  82.4 us
    pallas_call x1, Pallas kernels, attn_out(): pl.pallas_call(attn_out_kernel, out_shape=(jax.ShapeDtypeStruct((micro, s...  79.9 us
    pallas_call x1, Pallas kernels, gather_all(): pl.pallas_call(functools.partial(gather_kernel, zn), out_shape=(whole, wh...  76.6 us
    pallas_call x1, Pallas kernels, attn_back(): pl.pallas_call(attn_back_kernel, out_shape=(jax.ShapeDtypeStruct((micro,...  60.5 us
    pallas_call x1, Pallas kernels, ffn_out(): pl.pallas_call(ffn_out_kernel, out_shape=jax.ShapeDtypeStruct((micro, tok...  60 us
    dot_general x4, matrix products, weight_grad(): return jnp.einsum('ta,tb->ab', a, b, preferred_element_type=F32).astype(BF)  47.8 us
    psum x1, blocking collectives, on_device(): sums = lax.psum(sums, ('z', 'y', 'n'))  45.8 us
  transfers between devices with their start and end apart: 17, of which 6 were waited for; matrix products, arithmetic and copies ran while one was open for 10% of the time, Pallas kernels for 48%

profile of v1, /device:TPU:0, one launch (start us, length us, event | category | flops | bytes accessed | tf_op | source)
XLA Modules:
  0.0 712.9 jit_solution(6549027093704000507)
XLA Ops:
  7.2 1.2 constant_dynamic-slice_fusion.8
  8.8 3.0 collective-permute-start.1
  12.2 8.8 %collective-permute-done.1 = bf16[256,768]{1,0:T(8,128)(2,1)S(1)} collective-permute-done((bf16[256,768]{1,0:T(8,128)(2,1)S(1)}, bf16[256,768]{1,0:T(8,128)(2,1)S(1)}, u32[]{:S(2)}, u32[]{:S(2)}) %collective-permute-start.1) | collective-permute-done | bytes 393248 | tf_op jit(solution)/shard_map/ppermute | solution.py:778
  21.0 0.9 pad_maximum_fusion.3
  22.0 1.8 collective-permute-start.2
  24.4 4.3 collective-permute-done.2
  28.6 1.0 broadcast_select_fusion.15
  30.4 13.2 %collective-permute-done.3 = bf16[256,1536]{1,0:T(8,128)(2,1)S(1)} collective-permute-done((bf16[256,1536]{1,0:T(8,128)(2,1)S(1)}, bf16[256,1536]{1,0:T(8,128)(2,1)S(1)}, u32[]{:S(2)}, u32[]{:S(2)}) %collective-permute-start.3) | collective-permute-done | bytes 786464 | tf_op jit(solution)/shard_map/ppermute | solution.py:778
  43.8 1.2 pad_maximum_fusion
  45.2 1.5 collective-permute-start
  48.1 1.2 compare_convert_fusion.mask
  49.9 76.6 %gather_all.1 = (bf16[2,2,512,2048]{3,2,1,0:T(8,128)(2,1)}, bf16[2,2,512,2048]{3,2,1,0:T(8,128)(2,1)}, f32[4,2,8,256]{3,2,1,0:T(8,128)}) custom-call(bf16[2,512,512]{2,1,0:T(8,128)(2,1)} %x_in.1, bf16[2,512,512]{2,1,0:T(8,128)(2,1)} %d_in.1, f32[8,256]{1,0:T(8,128)} %fusion.8.v_in), custom_call_target="tpu_custom_call" | custom-call | flops 44999999488 | bytes 144000000 | tf_op jit(solution)/shard_map/gather_all/pallas_call | solution.py:269
  126.6 1.7 fusion.10
  128.3 11.2 %first_norm.1.n1 = bf16[2048,2048]{1,0:T(8,128)(2,1)} custom-call(bf16[2048,2048]{1,0:T(8,128)(2,1)} %bitcast.90, f32[1,2048]{1,0:T(1,128)} %bitcast.72, f32[1,2048]{1,0:T(1,128)} %bitcast.77), custom_call_target="tpu_custom_call" | custom-call | flops 8000000000 | bytes 25600000 | tf_op jit(solution)/shard_map/first_norm/pallas_call | solution.py:588
  139.8 3.7 fusion
  143.5 1.9 pad_maximum_fusion.1
  145.6 1.0 pad_maximum_fusion.4
  146.9 18.7 %attention.1 = (bf16[2048,768]{1,0:T(8,128)(2,1)}, bf16[2048,256]{1,0:T(8,128)(2,1)}) custom-call(s32[4,4]{1,0:T(4,128)} %copy-done.8, bf16[2048,2048]{1,0:T(8,128)(2,1)} %first_norm.1.n1, bf16[4,512,768]{2,1,0:T(8,128)(2,1)} %bitcast.84, f32[2048,128]{1,0:T(8,128)} %get-tuple-element.91.cos, f32[2048,128]{1,0:T(8,128)} %get-tuple-element.92.sin), custom_call_target="tpu_custom_call" | custom-call | flops 20000000000 | bytes 64000000 | tf_op jit(solution)/shard_map/attention/pallas_call | solution.py:588
  165.6 79.9 %attn_out.1 = (f32[2,128,2048]{2,1,0:T(8,128)}, bf16[2,2,4,128,2048]{4,3,2,1,0:T(8,128)(2,1)}) custom-call(bf16[2048,256]{1,0:T(8,128)(2,1)} %get-tuple-element.26.att, bf16[4,256,512]{2,1,0:T(8,128)(2,1)} %bitcast.88, bf16[2,2,512,2048]{3,2,1,0:T(8,128)(2,1)} %get-tuple-element.24.x_all, f32[1,2048]{1,0:T(1,128)} %bitcast.74, f32[1,2048]{1,0:T(1,128)} %bitcast.76), custom_call_target="tpu_custom_call" | custom-call | flops 85000003584 | bytes 272000000 | tf_op jit(solution)/shard_map/attn_out/pallas_call | solution.py:351
  245.5 19.4 %gate_up.1 = (f32[2048,1536]{1,0:T(8,128)}, bf16[2048,768]{1,0:T(8,128)(2,1)}) custom-call(bf16[2048,2048]{1,0:T(8,128)(2,1)} %bitcast.93, bf16[4,512,1536]{2,1,0:T(8,128)(2,1)} %bitcast.82, f32[1,768]{1,0:T(1,128)} %compare_convert_fusion.mask), custom_call_target="tpu_custom_call" | custom-call | flops 20000000000 | bytes 64000000 | tf_op jit(solution)/shard_map/gate_up/pallas_call | solution.py:588
  265.0 32.3 %all-gather.15.cloned.1.call-done = bf16[3072,512]{1,0:T(8,128)(2,1)} async-done(((bf16[768,512]{1,0:T(8,128)(2,1)}), bf16[3072,512]{1,0:T(8,128)(2,1)}) %all-gather.15.cloned.1.call-update) | async-done | bytes 3145744 | tf_op jit(solution)/shard_map/all_gather | solution.py:784
  297.3 16.1 %hidden_back.1.gul = bf16[2048,1536]{1,0:T(8,128)(2,1)} custom-call(bf16[2048,2048]{1,0:T(8,128)(2,1)} %bitcast.91, bf16[4,768,512]{2,1,0:T(8,128)(2,1)} %bitcast.86, f32[2048,1536]{1,0:T(8,128)} %get-tuple-element.31.gu, f32[1,768]{1,0:T(1,128)} %compare_convert_fusion.mask), custom_call_target="tpu_custom_call" | custom-call | flops 15000000512 | bytes 48000000 | tf_op jit(solution)/shard_map/hidden_back/pallas_call | solution.py:588
  313.4 95.2 %ffn_back.1 = (f32[2,128,2048]{2,1,0:T(8,128)}, bf16[2,2,4,128,2048]{4,3,2,1,0:T(8,128)(2,1)}, f32[8,2048]{1,0:T(8,128)}) custom-call(bf16[2048,1536]{1,0:T(8,128)(2,1)} %hidden_back.1.gul, bf16[4,512,1536]{2,1,0:T(8,128)(2,1)} %bitcast.83, bf16[2,2,512,2048]{3,2,1,0:T(8,128)(2,1)} %get-tuple-element.30.d_all, f32[2,128,2048]{2,1,0:T(8,128)} %get-tuple-element.29.middle, ...), custom_call_target="tpu_custom_call" | custom-call | flops 95000002560 | bytes 304000000 | tf_op jit(solution)/shard_map/ffn_back/pallas_call | solution.py:426
  408.7 6.7 convolution_convert_fusion.3
  415.4 17.0 %attention_back.1.low = bf16[2048,768]{1,0:T(8,128)(2,1)} custom-call(s32[4,4]{1,0:T(4,128)} %copy-done.8, bf16[2048,2048]{1,0:T(8,128)(2,1)} %bitcast.58, bf16[4,256,512]{2,1,0:T(8,128)(2,1)} %bitcast.89, bf16[2048,768]{1,0:T(8,128)(2,1)} %get-tuple-element.33.qkv, f32[2048,128]{1,0:T(8,128)} %get-tuple-element.91.cos, f32[2048,128]{1,0:T(8,128)} %get-tuple-element.92.sin), custom_call_target="tpu_custom_call" | custom-call | flops 24999999488 | bytes 80000000 | tf_op jit(solution)/shard_map/attention_back/pallas_call | solution.py:588
  432.4 11.4 %convolution_convert_fusion.2 = bf16[2048,768]{1,0:T(8,128)(2,1)} fusion(bf16[2048,2048]{1,0:T(8,128)(2,1)} %first_norm.1.n1, bf16[2048,768]{1,0:T(8,128)(2,1)} %attention_back.1.low), kind=kOutput, calls=%fused_computation.2 | convolution fusion | flops 6444023808 | bytes 14680064 | tf_op jit(solution)/shard_map/ta,tb->ab/dot_general | solution.py:824
  443.9 1.8 copy-done.15
  445.7 10.3 %convolution_convert_fusion.1 = bf16[768,2048]{1,0:T(8,128)(2,1)} fusion(bf16[2048,768]{1,0:T(8,128)(2,1)S(1)} %copy-done.15, bf16[2048,2048]{1,0:T(8,128)(2,1)} %bitcast.92), kind=kOutput, calls=%fused_computation.1 | convolution fusion | flops 6444023808 | bytes 14680064 | tf_op jit(solution)/shard_map/ta,tb->ab/dot_general | solution.py:824
  456.0 19.4 %convolution_convert_fusion = bf16[2048,1536]{1,0:T(8,128)(2,1)} fusion(bf16[2048,2048]{1,0:T(8,128)(2,1)} %bitcast.94, bf16[2048,1536]{1,0:T(8,128)(2,1)} %hidden_back.1.gul), kind=kOutput, calls=%fused_computation | convolution fusion | flops 12888047616 | bytes 20971520 | tf_op jit(solution)/shard_map/ta,tb->ab/dot_general | solution.py:824
  475.5 60.5 %attn_back.1 = (bf16[2,512,512]{2,1,0:T(8,128)(2,1)}, f32[8,2048]{1,0:T(8,128)}) custom-call(bf16[2048,768]{1,0:T(8,128)(2,1)} %attention_back.1.low, bf16[4,512,768]{2,1,0:T(8,128)(2,1)} %bitcast.85, bf16[2,2,512,2048]{3,2,1,0:T(8,128)(2,1)} %get-tuple-element.24.x_all, f32[2,128,2048]{2,1,0:T(8,128)} %get-tuple-element.34.mid_grad, f32[1,2048]{1,0:T(1,128)} %bitcast.73), custom_call_target="tpu_custom_call" | custom-call | flops 54999998464 | bytes 176000000 | tf_op jit(solution)/shard_map/attn_back/pallas_call | solution.py:512
  537.7 60.0 %ffn_out.1 = bf16[2,512,512]{2,1,0:T(8,128)(2,1)} custom-call(bf16[2048,768]{1,0:T(8,128)(2,1)} %get-tuple-element.28.hidden, bf16[4,768,512]{2,1,0:T(8,128)(2,1)} %bitcast.87, f32[2,128,2048]{2,1,0:T(8,128)} %get-tuple-element.29.middle), custom_call_target="tpu_custom_call" | custom-call | flops 54999998464 | bytes 176000000 | tf_op jit(solution)/shard_map/ffn_out/pallas_call | solution.py:569
  598.6 1.0 collective-permute-start.6
  599.6 45.8 %psum.7 = f32[4,2048]{1,0:T(4,128)S(1)} all-reduce(f32[4,2048]{1,0:T(4,128)S(1)} %pad_maximum_fusion.6), channel_id=1, replica_groups=mesh['z'=4,'y'=2,'n'=4] {'z','y','n'}, use_global_device_ids=true, to_apply=%region_7.8 | all-reduce | flops 8192 | bytes 65536 | tf_op jit(solution)/shard_map/psum | solution.py:850
  646.1 1.0 broadcast_select_fusion.13
  647.1 1.1 constant_dynamic-slice_fusion.4
  648.2 2.3 collective-permute-start.5
  651.4 1.8 constant_dynamic-slice_fusion.1
  653.2 26.2 %reduce-scatter.9.cloned.1.call-done = bf16[512,1536]{1,0:T(8,128)(2,1)} async-done(((bf16[2048,1536]{1,0:T(8,128)(2,1)}), bf16[512,1536]{1,0:T(8,128)(2,1)}) %reduce-scatter.9.cloned.1.call-update) | async-done | bytes 1572880 | tf_op jit(solution)/shard_map/reduce_scatter | solution.py:827
  679.4 1.2 constant_dynamic-slice_fusion.2
  680.6 1.5 collective-permute-start.7
  682.8 1.6 copy.53
  684.4 1.4 broadcast_select_fusion.5
  685.8 1.3 maximum_convert_fusion
  687.1 13.0 %collective-permute-done.7 = bf16[256,1536]{1,0:T(8,128)(2,1)} collective-permute-done((bf16[256,1536]{1,0:T(8,128)(2,1)S(1)}, bf16[256,1536]{1,0:T(8,128)(2,1)}, u32[]{:S(2)}, u32[]{:S(2)}) %collective-permute-start.7) | collective-permute-done | bytes 786464 | tf_op jit(solution)/shard_map/ppermute | solution.py:843
  700.1 1.4 broadcast_select_fusion.1
  701.6 2.1 convert_bitcast_fusion
  703.7 1.0 copy.67
  704.7 1.0 copy.68
  (100 shorter events, 10.3 us)
Async XLA Ops:
  7.2 139.7 %all-gather.9.cloned.1.call-start = ((), (), s32[]{:S(2)}) async-start(), calls=%async_computation.8 | async-start | bytes 3932160 | tf_op jit(solution)/shard_map/all_gather | solution.py:784
  8.6 13.4 %copy-start.7 = (bf16[512,256]{1,0:T(8,128)(2,1)S(1)}, bf16[512,256]{1,0:T(8,128)(2,1)}, u32[]{:S(2)}) copy-start(bf16[512,256]{1,0:T(8,128)(2,1)} %param.16) | copy-start | bytes 786436
  8.6 15.2 %copy-start.1 = (bf16[2,256,1536]{2,1,0:T(8,128)(2,1)S(1)}, bf16[2,256,1536]{2,1,0:T(8,128)(2,1)}, u32[]{:S(2)}) copy-start(bf16[2,256,1536]{2,1,0:T(8,128)(2,1)} %param.17) | copy-start | bytes 4718596
  8.8 12.1 %collective-permute-start.1 = (bf16[256,768]{1,0:T(8,128)(2,1)S(1)}, bf16[256,768]{1,0:T(8,128)(2,1)S(1)}, u32[]{:S(2)}, u32[]{:S(2)}) collective-permute-start(bf16[256,768]{1,0:T(8,128)(2,1)S(1)} %copy.44), channel_id=1, source_target_pairs={{0,4},{4,0},{1,5},{5,1},{2,6},{6,2},{3,7},{7,3},{8,12},{12,8},{9,1... | collective-permute-start | bytes 1179656 | tf_op jit(solution)/shard_map/ppermute | solution.py:778
  21.9 143.6 %all-gather.11.cloned.1.call-start = ((), (), s32[]{:S(2)}) async-start(), calls=%async_computation.9 | async-start | bytes 1310720 | tf_op jit(solution)/shard_map/all_gather | solution.py:784
  22.0 6.6 collective-permute-start.2
  24.0 19.6 %collective-permute-start.3 = (bf16[256,1536]{1,0:T(8,128)(2,1)S(1)}, bf16[256,1536]{1,0:T(8,128)(2,1)S(1)}, u32[]{:S(2)}, u32[]{:S(2)}) collective-permute-start(bf16[256,1536]{1,0:T(8,128)(2,1)S(1)} %bitcast.68), channel_id=1, source_target_pairs={{0,4},{4,0},{1,5},{5,1},{2,6},{6,2},{3,7},{7,3},{8,12},{12,8},{9,1... | collective-permute-start | bytes 2359304 | tf_op jit(solution)/shard_map/ppermute | solution.py:778
  30.3 215.2 %all-gather.13.cloned.1.call-start = ((), (), s32[]{:S(2)}) async-start(), calls=%async_computation.10 | async-start | bytes 7864320 | tf_op jit(solution)/shard_map/all_gather | solution.py:784
  43.7 1.4 copy-start.9
  43.8 2.9 copy-start.5
  43.8 3.6 copy-start.10
  43.8 3.6 copy-start.11
  43.8 3.6 copy-start.12
  43.8 3.6 copy-start.13
  43.8 3.6 copy-start.14
  45.1 252.2 %all-gather.15.cloned.1.call-start = ((), (), s32[]{:S(2)}) async-start(), calls=%async_computation.11 | async-start | bytes 3932160 | tf_op jit(solution)/shard_map/all_gather | solution.py:784
  45.2 94.3 %collective-permute-start = (s32[2,1,4]{2,1,0:T(1,128)S(1)}, s32[2,1,4]{2,1,0:T(1,128)S(1)}, u32[]{:S(2)}, u32[]{:S(2)}) collective-permute-start(s32[2,1,4]{2,1,0:T(1,128)S(1)} %copy-done.9), channel_id=1, source_target_pairs={{0,4},{4,0},{1,5},{5,1},{2,6},{6,2},{3,7},{7,3},{8,12},{12,8},{9,1... | collective-permute-start | bytes 104 | tf_op jit(solution)/shard_map/ppermute | solution.py:801
  46.7 98.8 %collective-permute-start.4 = (bf16[768,256]{1,0:T(8,128)(2,1)S(1)}, bf16[768,256]{1,0:T(8,128)(2,1)S(1)}, u32[]{:S(2)}, u32[]{:S(2)}) collective-permute-start(bf16[768,256]{1,0:T(8,128)(2,1)S(1)} %constant_dynamic-slice_fusion.5), channel_id=1, source_target_pairs={{0,4},{4,0},{1,5},{5,1},{2,6},{6,2},{3,7},{7,3},{8,12},{12,8},{9,1... | collective-permute-start | bytes 1179656 | tf_op jit(solution)/shard_map/ppermute | solution.py:781
  139.6 5.8 copy-start.8
  146.6 451.1 %reduce-scatter.7.cloned.1.call-start = ((), (), s32[]{:S(2)}) async-start(), calls=%async_computation.5 | async-start | bytes 1310720 | tf_op jit(solution)/shard_map/reduce_scatter | solution.py:827
  313.4 95.2 %copy-start = (bf16[2048,256]{1,0:T(8,128)(2,1)S(1)}, bf16[2048,256]{1,0:T(8,128)(2,1)}, u32[]{:S(2)}) copy-start(bf16[2048,256]{1,0:T(8,128)(2,1)} %get-tuple-element.26.att) | copy-start | bytes 3145732
  415.4 231.7 %reduce-scatter.5.cloned.1.call-start = ((), (), s32[]{:S(2)}) async-start(), calls=%async_computation.4 | async-start | bytes 3932160 | tf_op jit(solution)/shard_map/reduce_scatter | solution.py:827
  443.8 1.9 copy-start.15
  443.8 207.6 %reduce-scatter.11.cloned.1.call-start = ((), (), s32[]{:S(2)}) async-start(), calls=%async_computation.7 | async-start | bytes 3932160 | tf_op jit(solution)/shard_map/reduce_scatter | solution.py:827
  456.0 223.4 %reduce-scatter.9.cloned.1.call-start = ((), (), s32[]{:S(2)}) async-start(), calls=%async_computation.6 | async-start | bytes 7864320 | tf_op jit(solution)/shard_map/reduce_scatter | solution.py:827
  598.6 47.5 %collective-permute-start.6 = (bf16[256,256]{1,0:T(8,128)(2,1)S(1)}, bf16[256,256]{1,0:T(8,128)(2,1)S(1)}, u32[]{:S(2)}, u32[]{:S(2)}) collective-permute-start(bf16[256,256]{1,0:T(8,128)(2,1)S(1)} %constant_dynamic-slice_fusion.3), channel_id=1, source_target_pairs={{0,4},{4,0},{1,5},{5,1},{2,6},{6,2},{3,7},{7,3},{8,12},{12,8},{9,1... | collective-permute-start | bytes 393224 | tf_op jit(solution)/shard_map/ppermute | solution.py:847
  647.1 35.0 %copy-start.6 = (bf16[512,768]{1,0:T(8,128)(2,1)S(1)}, bf16[512,768]{1,0:T(8,128)(2,1)}, u32[]{:S(2)}) copy-start(bf16[512,768]{1,0:T(8,128)(2,1)} %reduce-scatter.5.cloned.1.call-done) | copy-start | bytes 2359300
  648.2 33.9 %collective-permute-start.5 = (bf16[256,768]{1,0:T(8,128)(2,1)S(1)}, bf16[256,768]{1,0:T(8,128)(2,1)S(1)}, u32[]{:S(2)}, u32[]{:S(2)}) collective-permute-start(bf16[256,768]{1,0:T(8,128)(2,1)S(1)} %constant_dynamic-slice_fusion.4), channel_id=1, source_target_pairs={{0,4},{4,0},{1,5},{5,1},{2,6},{6,2},{3,7},{7,3},{8,12},{12,8},{9,1... | collective-permute-start | bytes 1179656 | tf_op jit(solution)/shard_map/ppermute | solution.py:843
  653.2 31.2 %collective-permute-start.8 = (bf16[768,256]{1,0:T(8,128)(2,1)}, bf16[768,256]{1,0:T(8,128)(2,1)}, u32[]{:S(2)}, u32[]{:S(2)}) collective-permute-start(bf16[768,256]{1,0:T(8,128)(2,1)} %constant_dynamic-slice_fusion.1), channel_id=1, source_target_pairs={{0,4},{4,0},{1,5},{5,1},{2,6},{6,2},{3,7},{7,3},{8,12},{12,8},{9,1... | collective-permute-start | bytes 1179656 | tf_op jit(solution)/shard_map/ppermute | solution.py:847
  680.6 19.5 %collective-permute-start.7 = (bf16[256,1536]{1,0:T(8,128)(2,1)S(1)}, bf16[256,1536]{1,0:T(8,128)(2,1)}, u32[]{:S(2)}, u32[]{:S(2)}) collective-permute-start(bf16[256,1536]{1,0:T(8,128)(2,1)S(1)} %constant_dynamic-slice_fusion.2), channel_id=1, source_target_pairs={{0,4},{4,0},{1,5},{5,1},{2,6},{6,2},{3,7},{7,3},{8,12},{12,8},{9,1... | collective-permute-start | bytes 2359304 | tf_op jit(solution)/shard_map/ppermute | solution.py:843
  684.4 15.7 %copy-start.2 = (bf16[512,1536]{1,0:T(8,128)(2,1)S(1)}, bf16[512,1536]{1,0:T(8,128)(2,1)}, u32[]{:S(2)}) copy-start(bf16[512,1536]{1,0:T(8,128)(2,1)} %reduce-scatter.9.cloned.1.call-done) | copy-start | bytes 4718596
  701.6 2.1 copy-start.4
  701.6 3.1 copy-start.3
Sparse Core Ops, SparseCore 0:
  22.1 66.2 all-gather.8
  90.5 26.4 all-gather.10
  119.2 114.8 all-gather.12
  235.5 61.7 all-gather.14
  415.5 25.0 reduce-scatter.6
  443.9 58.4 reduce-scatter.4
  504.8 60.2 reduce-scatter.10
  567.5 111.8 reduce-scatter.8

commit v2 on v1

v2 whole, which is shorter than its diff:
```python
import functools

import jax
import jax.numpy as jnp
from jax import lax
from jax.experimental import pallas as pl
from jax.experimental.pallas import tpu as pltpu
from jax.sharding import Mesh
from jax.sharding import PartitionSpec as P

HEAD_DIM = 128
EPS = 1e-05
BF = jnp.bfloat16
F32 = jnp.float32
MESH = pl.DeviceIdType.MESH
VMEM_BYTES = 60 * 2**20
SWAP = [(0, 1), (1, 0)]
ANY = pl.BlockSpec(memory_space=pl.ANY)
VMEM = pl.BlockSpec(memory_space=pltpu.VMEM)
SMEM = pl.BlockSpec(memory_space=pltpu.SMEM)


def dot(a, b):
    return jnp.dot(a, b, preferred_element_type=F32)


def dot_nt(a, b):
    return lax.dot_general(a, b, (((1,), (1,)), ((), ())), preferred_element_type=F32)


def dot_tn(a, b):
    return lax.dot_general(a, b, (((0,), (0,)), ((), ())), preferred_element_type=F32)


def normalise(v):
    centred = v - jnp.mean(v, axis=-1, keepdims=True)
    rstd = lax.rsqrt(jnp.mean(centred * centred, axis=-1, keepdims=True) + EPS)
    return centred * rstd, rstd


def norm_back(xhat, rstd, grad, gain):
    dx = grad * gain
    a = jnp.mean(dx, axis=-1, keepdims=True)
    b = jnp.mean(dx * xhat, axis=-1, keepdims=True)
    return rstd * (dx - a - xhat * b)


def cost(us, sent=0):
    return pl.CostEstimate(flops=int(us * 1e9), bytes_accessed=int(us * 3.2e6), transcendentals=0)


def without(body, ins, extra):
    def run(*refs):
        return body(*refs[:ins], *refs[ins + extra :])

    return run


def kernel(body, ins, in_specs, outs, out_specs, us, name, scratch=(), first=(), grid=(), talk=None, aliases=None):
    extra = len(first)
    return pl.pallas_call(
        without(body, len(ins), extra),
        grid=grid,
        in_specs=list(in_specs) + [ANY] * extra,
        out_specs=out_specs,
        out_shape=outs,
        scratch_shapes=list(scratch),
        input_output_aliases=aliases or {},
        compiler_params=pltpu.CompilerParams(
            vmem_limit_bytes=VMEM_BYTES, collective_id=talk, has_side_effects=talk is not None
        ),
        cost_estimate=cost(us),
        name=name,
    )(*ins, *first)


def sems(*counts):
    return [pltpu.SemaphoreType.DMA((k,)) for k in counts]


def shaped(shape, dtype=BF):
    return jax.ShapeDtypeStruct(tuple(shape), dtype)


class Place:
    def __init__(self):
        self.y = lax.axis_index("y")
        self.n = lax.axis_index("n")
        self.x = self.n // 2
        self.c = self.n % 2
        self.ns = self.n + 1 - 2 * self.c
        self.nx = (self.n + 2) % 4
        self.nd = (self.ns + 2) % 4
        self.sib = {"n": self.ns}
        self.xn = {"n": self.nx}
        self.yn = {"y": 1 - self.y}
        self.xs = {"n": self.nd}


def meet(devices):
    barrier = pltpu.get_barrier_semaphore()
    for d in devices:
        pl.semaphore_signal(barrier, inc=1, device_id=d, device_id_type=MESH)
    pl.semaphore_wait(barrier, len(devices))


class Wire:
    def __init__(self, send_sems, recv_sems, first=0):
        self.ss, self.rs, self.at, self.sent = send_sems, recv_sems, first, []

    def make(self, src, dst, device, keep=True, again=False):
        self.at += not again
        k = self.at - 1
        copy = pltpu.make_async_remote_copy(
            src_ref=src, dst_ref=dst, send_sem=self.ss.at[k], recv_sem=self.rs.at[k],
            device_id=device, device_id_type=MESH,
        )
        if keep:
            self.sent.append(copy)
        return copy

    def finish(self):
        for copy in self.sent:
            copy.wait_send()


SPREAD = 9


class Spread:
    def __init__(self, wire, at, src, slot):
        y, n, nx = at.y, at.n, at.nx
        self.first = [
            wire.make(src, slot(y, n, None), at.xn),
            wire.make(src, slot(y, n, None), at.yn),
            wire.make(src, slot(y, n, None), at.sib),
        ]
        self.on_x = [
            wire.make(slot(y, nx, 0), slot(y, nx, 0), at.yn),
            wire.make(slot(y, nx, None), slot(y, nx, None), at.sib),
        ]
        self.on_y = [
            wire.make(slot(1 - y, n, 1), slot(1 - y, n, 1), at.xn),
            wire.make(slot(1 - y, n, None), slot(1 - y, n, None), at.sib),
        ]
        self.last = [
            wire.make(slot(1 - y, nx, 0), slot(1 - y, nx, 0), at.sib),
            wire.make(slot(1 - y, nx, 1), slot(1 - y, nx, 1), at.sib),
        ]

    def begin(self):
        for copy in self.first:
            copy.start()

    def forward(self):
        self.first[0].wait_recv()
        for copy in self.on_x:
            copy.start()
        self.first[1].wait_recv()
        for copy in self.on_y:
            copy.start()

    def forward_last(self):
        self.on_x[0].wait_recv()
        self.last[0].start()
        self.on_y[0].wait_recv()
        self.last[1].start()

    def end(self):
        self.first[2].wait_recv()
        self.on_x[1].wait_recv()
        self.on_y[1].wait_recv()
        self.last[0].wait_recv()
        self.last[1].wait_recv()


REDUCE = 10


def reduce_scratch(micro, tok, sub, width):
    half = sub // 2
    return [
        pltpu.VMEM((micro, 2, tok, width), BF),
        pltpu.VMEM((micro, 2, 2, sub, width), BF),
        pltpu.VMEM((micro, sub, width), BF),
        pltpu.VMEM((micro, sub, width), BF),
        pltpu.VMEM((micro, sub, width), BF),
        pltpu.VMEM((micro, 2, half, width), BF),
        pltpu.VMEM((micro, sub, width), BF),
        pltpu.VMEM((micro, sub, width), BF),
    ]


class Reduce:
    def __init__(self, wire, at, scratch, compute):
        self.part, self.ra, self.sb, self.sx, self.sy, self.rb, self.rcx, self.rcy = scratch
        self.wire, self.at, self.compute = wire, at, compute
        self.micro, self.sub = self.sb.shape[0], self.sb.shape[1]
        self.a, self.b, self.d = {}, {}, {}
        self.released = False

    def rows(self, core, xx, lo=0, size=None):
        return pl.ds(pl.multiple_of((2 * xx + core) * self.sub, self.sub) + lo, size or self.sub)

    def summed(self, m, yy, xx, lo, size):
        mine = self.part[m, yy, self.rows(self.at.c, xx, lo, size), :].astype(F32)
        return mine + self.ra[m, yy, xx, lo : lo + size, :].astype(F32)

    def cores(self, m):
        at = self.at
        for yk, yy in ((1, 1 - at.y), (0, at.y)):
            self.compute(m, yy)
            for xk, xx in ((1, 1 - at.x), (0, at.x)):
                copy = self.wire.make(self.part.at[m, yy, self.rows(1 - at.c, xx)], self.ra.at[m, yy, xx], at.sib)
                copy.start()
                self.a[m, yk, xk] = copy

    def diagonal(self, m):
        at, sub, half = self.at, self.sub, self.sub // 2
        self.a[m, 1, 1].wait_recv()
        self.sb[m] = self.summed(m, 1 - at.y, 1 - at.x, 0, sub).astype(BF)
        self.b[m, 0] = self.wire.make(self.sb.at[m, 0:half], self.rb.at[m, 0], at.xn)
        self.b[m, 1] = self.wire.make(self.sb.at[m, half:sub], self.rb.at[m, 1], at.yn)
        self.b[m, 0].start()
        self.b[m, 1].start()

    def sides(self, m):
        at, sub, half = self.at, self.sub, self.sub // 2
        sx, sy, rb, rcx, rcy = self.sx, self.sy, self.rb, self.rcx, self.rcy
        self.a[m, 1, 0].wait_recv()
        sy[m, half:sub] = self.summed(m, 1 - at.y, at.x, half, half).astype(BF)
        self.d[m, 0] = self.wire.make(sy.at[m, half:sub], rcy.at[m, half:sub], at.yn)
        self.d[m, 0].start()
        self.a[m, 0, 1].wait_recv()
        sx[m, 0:half] = self.summed(m, at.y, 1 - at.x, 0, half).astype(BF)
        self.d[m, 1] = self.wire.make(sx.at[m, 0:half], rcx.at[m, 0:half], at.xn)
        self.d[m, 1].start()
        self.b[m, 0].wait_recv()
        sy[m, 0:half] = (self.summed(m, 1 - at.y, at.x, 0, half) + rb[m, 0].astype(F32)).astype(BF)
        self.d[m, 2] = self.wire.make(sy.at[m, 0:half], rcy.at[m, 0:half], at.yn)
        self.d[m, 2].start()
        self.b[m, 1].wait_recv()
        sx[m, half:sub] = (self.summed(m, at.y, 1 - at.x, half, half) + rb[m, 1].astype(F32)).astype(BF)
        self.d[m, 3] = self.wire.make(sx.at[m, half:sub], rcx.at[m, half:sub], at.xn)
        self.d[m, 3].start()

    def release(self, m):
        at = self.at
        self.a[m, 0, 0].wait_recv()
        self.ra[m, at.y, at.x] = self.summed(m, at.y, at.x, 0, self.sub).astype(BF)
        for yk in (1, 0):
            for xk in (1, 0):
                copy = self.a[m, yk, xk]
                copy.wait_send()
                self.wire.sent = [other for other in self.wire.sent if other is not copy]
        self.released = True

    def arrived(self, m):
        if not self.released:
            self.a[m, 0, 0].wait_recv()
        for k in range(4):
            self.d[m, k].wait_recv()

    def total(self, m, lo, size):
        if self.released:
            own = self.ra[m, self.at.y, self.at.x, lo : lo + size, :].astype(F32)
        else:
            own = self.summed(m, self.at.y, self.at.x, lo, size)
        return own + self.rcx[m, lo : lo + size, :].astype(F32) + self.rcy[m, lo : lo + size, :].astype(F32)


def nothing():
    pass


def reduce_rows(wire, at, scratch, compute, finish, tick=nothing):
    red = Reduce(wire, at, scratch, compute)
    for m in range(red.micro):
        red.cores(m)
        red.diagonal(m)
    tick()
    for m in range(red.micro):
        red.sides(m)
    tick()
    for m in range(red.micro):
        red.arrived(m)
        finish(m, lambda lo, size, m=m: red.total(m, lo, size))
    tick()


class Step:
    def __init__(self, wire, z, zn, s, g, prev, got, bufs, load, k):
        rows, cols = got[0].shape
        far, cap = zn - 1 - s, min(s, zn - 2)
        self.bufs, self.cols, self.ways = bufs, cols, []
        for d, (place, sign) in enumerate(((z, 1), (zn - 1 - z, -1))):
            group = (z + sign * far + zn) % zn
            here = bufs.at[d, 0, :, pl.ds(0, cols)]
            own = pltpu.make_async_copy(
                g.at[pl.ds(pl.multiple_of(group * rows, rows), rows)], here, load.at[k + 2 * d]
            )
            came = bufs.at[d, 1, :, pl.ds(0, cols)]
            carry = pltpu.make_async_copy(prev[d], came, load.at[k + 2 * d + 1]) if s else None
            peer = {"z": (z + sign + zn) % zn}
            away = wire.make(here, got[d], peer, keep=False)
            last = d * (zn - 1 - far) + (1 - d) * far
            straight = wire.make(g.at[pl.ds(last * rows, rows)], got[d], peer, keep=False, again=True)
            gets = jnp.logical_and(place >= 1, place <= cap + 1)
            adds = jnp.logical_and(place <= cap, place >= 1)
            self.ways.append((place <= cap, adds, gets, own, carry, away, place == 0, straight))

    def begin(self):
        for *_, end, straight in self.ways:
            pl.when(end)(straight.start)

    def go(self):
        for _, adds, _, own, carry, *_ in self.ways:
            if carry is not None:
                pl.when(adds)(own.start)
                pl.when(adds)(carry.start)
        for d, (_, adds, _, own, carry, away, *_) in enumerate(self.ways):
            if carry is not None:

                def add(d=d, own=own, carry=carry, away=away):
                    own.wait()
                    carry.wait()
                    cols = pl.ds(0, self.cols)
                    both = self.bufs[d, 0, :, cols].astype(F32) + self.bufs[d, 1, :, cols].astype(F32)
                    self.bufs[d, 0, :, cols] = both.astype(BF)
                    away.start()

                pl.when(adds)(add)

    def wait(self):
        for sends, _, gets, _, _, away, *_ in self.ways:
            pl.when(gets)(away.wait_recv)
            pl.when(sends)(away.wait_send)


class Host:
    def __init__(self, wire, zn, jobs, bufs, load):
        z = lax.axis_index("z")
        self.steps, self.now, self.count, self.then, k = [], None, 0, {}, 0
        for g, prev, first, outs in jobs:
            for i in range(len(outs) // 2):
                got = outs[2 * i : 2 * i + 2]
                self.steps.append(Step(wire, z, zn, first + i, g, prev, got, bufs, load, k))
                prev = got
                k += 4

    def begin(self):
        for step in self.steps:
            step.begin()
        self.next()

    def next(self):
        if self.now is not None:
            self.now.wait()
            self.count += 1
            done, self.now = self.then.pop(self.count, None), None
            if self.steps:
                self.now = self.steps.pop(0)
                self.now.go()
            if done is not None:
                done()
        elif self.steps:
            self.now = self.steps.pop(0)
            self.now.go()

    def end(self):
        while self.steps or self.now is not None:
            self.next()


class Settle:
    def __init__(self, wire, at, zn, g, got, keep, theirs, bufs, load):
        z = lax.axis_index("z")
        _, self.rows, self.cols = bufs.shape[0], keep.shape[0] * 2, keep.shape[1]
        rows, half = self.rows, keep.shape[0]
        self.bufs, self.has = bufs, (None, z >= 1, z <= zn - 2)
        view = [bufs.at[k, :, pl.ds(0, self.cols)] for k in range(3)]
        mine = g.at[pl.ds(pl.multiple_of(z * rows, rows), rows)]
        self.loads = [pltpu.make_async_copy(src, view[k], load.at[k]) for k, src in enumerate((mine, got[0], got[1]))]

        def part(i):
            return bufs.at[0, pl.ds(pl.multiple_of(i * half, half), half), pl.ds(0, self.cols)]

        self.away = wire.make(part(1 - at.y), theirs, at.yn, keep=False)
        self.here = pltpu.make_async_copy(part(at.y), keep, load.at[3])

    def go(self):
        cols = pl.ds(0, self.cols)
        self.loads[0].start()
        for k in (1, 2):
            pl.when(self.has[k])(self.loads[k].start)
        self.loads[0].wait()
        for k in (1, 2):
            pl.when(self.has[k])(self.loads[k].wait)

            def none(k=k):
                self.bufs[k, :, cols] = jnp.zeros((self.rows, self.cols), BF)

            pl.when(jnp.logical_not(self.has[k]))(none)
        total = self.bufs[0, :, cols].astype(F32)
        for k in (1, 2):
            total = total + self.bufs[k, :, cols].astype(F32)
        self.bufs[0, :, cols] = total.astype(BF)
        self.away.start()
        self.here.start()

    def wait(self):
        self.away.wait_recv()
        self.away.wait_send()
        self.here.wait()


def z_partners(zn):
    z = lax.axis_index("z")
    return [{"z": (z + 1) % zn}, {"z": (z + zn - 1) % zn}]


class Jobs:
    def __init__(self, plan, zn):
        self.plan, self.zn = plan, zn
        self.ins, self.outs = [], []
        for g, prev, first, steps in plan:
            self.ins += [g] + (list(prev) if prev is not None else [])
            self.outs += [shaped((g.shape[0] // zn, g.shape[1]))] * (2 * steps)
        self.steps = sum(p[3] for p in plan)
        wide = max([p[0].shape[1] for p in plan], default=0)
        rows = plan[0][0].shape[0] // zn if plan else 0
        self.scratch = [pltpu.VMEM((2, 2, rows, wide), BF)] + sems(4 * self.steps) if plan else []

    def host(self, wire, ins, outs, scratch):
        jobs, i, o = [], 0, 0
        for _, prev, first, steps in self.plan:
            took = 1 if prev is None else 3
            jobs.append((ins[i], None if prev is None else ins[i + 1 : i + 3], first, outs[o : o + 2 * steps]))
            i, o = i + took, o + 2 * steps
        return Host(wire, self.zn, jobs, *scratch)


def blockwise(part, m, yy, fn, tile=256):
    tok = part.shape[2]

    def step(i, carry):
        lo = pl.multiple_of(i * tile, tile)
        fn(lo, tile)
        return carry

    lax.fori_loop(0, tok // tile, step, 0)


def token_spreads(wire, at, src, out, sem, first, cut):
    micro, tok, feat = src.shape
    spreads, local = [], []
    for m in range(micro):

        def slot(yy, nn, part, m=m):
            lo, size = {None: (0, tok), 0: (0, cut), 1: (cut, tok - cut)}[part]
            return out.at[m, yy, pl.ds(lo, size), pl.ds(pl.multiple_of(nn * feat, feat), feat)]

        spreads.append(Spread(wire, at, src.at[m], slot))
        local.append(pltpu.make_async_copy(src.at[m], slot(at.y, at.n, None), sem.at[first + m]))
    return spreads, local


def attn_cut(w_qkv, w_out, i, buf):
    parts, _, cols = w_qkv.shape
    half = cols // 2
    at = pl.ds(pl.multiple_of(i * half, half), half)
    for p in range(parts):
        buf[:, p * half : (p + 1) * half] = w_qkv[p, :, at]
    buf[:, parts * half :] = w_out[at, :].astype(F32).T.astype(BF)


def chunk_cut(w_gu, w_down, i, c, one, buf):
    half = w_gu.shape[2] // 2
    at = pl.ds(pl.multiple_of(i * half, half) + c * one, one)
    buf[:, :one] = w_gu[0, :, at]
    buf[:, one : 2 * one] = w_gu[1, :, at]
    buf[:, 2 * one :] = w_down[at, :].astype(F32).T.astype(BF)


class Swap:
    def __init__(self, wire, at, bufs, out, sem):
        depth = bufs.shape[1]
        place = out.at[pl.ds(pl.multiple_of(at.y * depth, depth), depth)]
        self.away = wire.make(bufs.at[0], place, at.yn)
        self.here = pltpu.make_async_copy(bufs.at[1], place, sem)

    def end(self):
        self.away.wait_recv()
        self.here.wait()


def swap_attn_kernel(w_qkv, w_out, out, bufs, ss, rs, ls):
    at = Place()
    meet([at.yn])
    wire = Wire(ss, rs)
    swap = Swap(wire, at, bufs, out, ls.at[0])
    attn_cut(w_qkv, w_out, 1 - at.y, bufs.at[0])
    swap.away.start()
    attn_cut(w_qkv, w_out, at.y, bufs.at[1])
    swap.here.start()
    swap.end()
    wire.finish()


def swap_attn(w_qkv, w_out):
    parts, depth, cols = w_qkv.shape
    size = (parts + 1) * cols // 2
    return kernel(
        swap_attn_kernel, (w_qkv, w_out), [VMEM, VMEM], shaped((2 * depth, size)), ANY, 14, "swap_attn",
        [pltpu.VMEM((2, depth, size), BF)] + sems(1, 1, 1), talk=6,
    )


def swap_chunks(wire, at, w_gu, w_down, which, one, bufs, outs, ls):
    swaps = []
    for k, (c, out) in enumerate(zip(which, outs)):
        swap = Swap(wire, at, bufs.at[k], out, ls.at[k])
        chunk_cut(w_gu, w_down, 1 - at.y, c, one, bufs.at[k, 0])
        swap.away.start()
        chunk_cut(w_gu, w_down, at.y, c, one, bufs.at[k, 1])
        swap.here.start()
        swaps.append(swap)
    return swaps


def gather_x_kernel(zn, which, count, x_in, v_in, lens, freq, w_gu, w_down, x_out, v_out, lens_all, cos, sin, own, *scratch):
    bufs, ss, rs, ls = scratch
    at = Place()
    z = lax.axis_index("z")
    one = own.shape[2] // 3
    ring = [(dz, dy) for dz in range(zn) for dy in range(2) if dz or dy]
    others = [{"z": (z + dz) % zn, "y": (at.y + dy) % 2} for dz, dy in ring]
    meet([at.sib, at.xn] + others)
    wire = Wire(ss, rs)
    there = wire.make(lens, lens_all.at[at.y], at.yn)
    there.start()
    spreads, local = token_spreads(wire, at, x_in, x_out, ls, len(which) + 1, x_in.shape[1] // 8)
    local.append(pltpu.make_async_copy(v_in, v_out.at[z, at.y], ls.at[len(which)]))
    small = [wire.make(v_in, v_out.at[z, at.y], d) for d in others]
    for s in spreads:
        s.begin()
    for copy in small + local:
        copy.start()
    swaps = swap_chunks(wire, at, w_gu, w_down, which, one, bufs, [own.at[k] for k in range(len(which))], ls)
    lens_all[at.y] = lens[...]
    there.wait_recv()
    tok = x_in.shape[1]
    row = lax.broadcasted_iota(jnp.int32, (tok, 1), 0)
    flip = jnp.where(lax.broadcasted_iota(jnp.int32, (1, HEAD_DIM), 1) < HEAD_DIM // 2, -1.0, 1.0)

    def table(b, carry):
        m, yy = b // 2, b % 2
        line = lens_all[yy, pl.ds(m, 1), :]
        end = jnp.zeros((1, 1), jnp.int32)
        start = jnp.zeros_like(row)
        for k in range(count):
            end = end + line[:, k : k + 1]
            start = jnp.where(row >= end, end, start)
        angle = (row - start).astype(F32) * freq[...]
        place = pl.ds(pl.multiple_of(b * tok, tok), tok)
        cos[place, :] = jnp.cos(angle)
        sin[place, :] = jnp.sin(angle) * flip
        return carry

    lax.fori_loop(0, x_in.shape[0] * 2, table, 0)
    run_spreads(spreads, local)
    for copy in small:
        copy.wait_recv()
    for swap in swaps:
        swap.end()
    wire.finish()


def gather_x(x, v, lens, freq, w_gu, w_down, zn, which, one, count, first):
    micro, tok, feat = x.shape
    depth = w_gu.shape[1]
    rows = micro * 2 * tok
    links = SPREAD * micro + 2 * zn - 1 + len(which) + 1
    return kernel(
        functools.partial(gather_x_kernel, zn, which, count), (x, v, lens, freq, w_gu, w_down),
        [ANY, ANY, VMEM, VMEM, VMEM, VMEM],
        (
            shaped((micro, 2, tok, 4 * feat)), shaped((zn, 2) + v.shape, F32), shaped((2,) + lens.shape, jnp.int32),
            shaped((rows, HEAD_DIM), F32), shaped((rows, HEAD_DIM), F32), shaped((len(which), 2 * depth, 3 * one)),
        ),
        (ANY, ANY, VMEM, VMEM, VMEM, ANY), 48, "gather_x",
        [pltpu.VMEM((len(which), 2, depth, 3 * one), BF)] + sems(links, links, micro + 1 + len(which)),
        first, talk=0,
    )


def gather_d_kernel(which, one, d_in, x_all, gain, shift, w_gu, w_down, d_out, n1, *refs):
    outs, (bufs, xin, nout, ss, rs, ls, load) = refs[: len(which)], refs[len(which) :]
    at = Place()
    micro, _, tok, _ = x_all.shape
    meet([at.sib, at.xn, at.yn])
    wire = Wire(ss, rs)
    spreads, local = token_spreads(wire, at, d_in, d_out, ls, len(which), d_in.shape[1] // 16 * 5)

    def bring(b):
        return pltpu.make_async_copy(x_all.at[b // 2, b % 2], xin.at[b % 2], load.at[b])

    def put(b):
        return pltpu.make_async_copy(nout.at[b % 2], n1.at[pl.ds(b * tok, tok)], load.at[2 * micro + b])

    bring(0).start()
    bring(1).start()
    for s in spreads:
        s.begin()
    for copy in local:
        copy.start()
    swaps = swap_chunks(wire, at, w_gu, w_down, which, one, bufs, outs, ls)
    for b in range(2 * micro):
        bring(b).wait()
        if b >= 2:
            put(b - 2).wait()

        def tile(i, carry, b=b):
            place = pl.ds(pl.multiple_of(i * 128, 128), 128)
            xhat, _ = normalise(xin[b % 2, place, :].astype(F32))
            nout[b % 2, place, :] = (xhat * gain[...] + shift[...]).astype(BF)
            return carry

        lax.fori_loop(0, tok // 128, tile, 0)
        put(b).start()
        if b + 2 < 2 * micro:
            bring(b + 2).start()
        if b % 2:
            spreads[b // 2].forward()
    put(2 * micro - 2).wait()
    put(2 * micro - 1).wait()
    for s in spreads:
        s.forward_last()
    for s in spreads:
        s.end()
    for copy in local:
        copy.wait()
    for swap in swaps:
        swap.end()
    wire.finish()


def gather_d(d, x_all, gain, shift, w_gu, w_down, which, one):
    micro, tok, feat = d.shape
    depth = w_gu.shape[1]
    count = SPREAD * micro + len(which)
    return kernel(
        functools.partial(gather_d_kernel, which, one), (d, x_all, gain, shift, w_gu, w_down),
        [ANY, ANY, VMEM, VMEM, VMEM, VMEM],
        (shaped((micro, 2, tok, 4 * feat)), shaped((micro * 2 * tok, 4 * feat))) + (shaped((2 * depth, 3 * one)),) * len(which),
        (ANY,) * (2 + len(which)), 48, "gather_d",
        [pltpu.VMEM((len(which), 2, depth, 3 * one), BF)] + [pltpu.VMEM((2, tok, 4 * feat), BF)] * 2
        + sems(count, count, micro + len(which), 4 * micro),
        talk=5,
    )


def row_slot(out, m, sub):
    half = sub // 2

    def slot(yy, nn, part):
        ref = out.at[m, yy, nn]
        return ref if part is None else ref.at[pl.ds(part * half, half)]

    return slot


def run_spreads(spreads, local):
    for s in spreads:
        s.forward()
    for s in spreads:
        s.forward_last()
    for s in spreads:
        s.end()
    for copy in local:
        copy.wait()


def attn_out_kernel(att, wo, x_all, gain, shift, middle, n2, *scratch):
    *red, xb, nb, ss, rs, ls = scratch
    at = Place()
    micro, sub, width = middle.shape
    zn, dz, cols = wo.shape
    span = att.shape[1]
    tok = red[0].shape[2]
    meet([at.sib, at.xn, at.yn])
    wire = Wire(ss, rs)
    own = [pltpu.make_async_copy(x_all.at[m, at.y, pl.ds(at.n * sub, sub)], xb.at[m], ls.at[m]) for m in range(micro)]
    for copy in own:
        copy.start()

    def compute(m, yy):
        def tile(lo, size):
            a = att[pl.ds(pl.multiple_of((m * 2 + yy) * tok, tok) + lo, size), :]
            for k in range(zn):
                red[0][m, yy, pl.ds(lo, size), k * dz : (k + 1) * dz] = dot_nt(a, wo[k, :, cols - span :]).astype(BF)

        blockwise(red[0], m, yy, tile)

    spreads, local = [], []

    def finish(m, total):
        own[m].wait()
        step = sub // 2
        for lo in range(0, sub, step):
            mid = xb[m, lo : lo + step, :].astype(F32) + total(lo, step)
            middle[m, lo : lo + step, :] = mid
            xhat, _ = normalise(mid)
            nb[m, lo : lo + step, :] = (xhat * gain[...] + shift[...]).astype(BF)
        slot = row_slot(n2, m, sub)
        spreads.append(Spread(wire, at, nb.at[m], slot))
        spreads[-1].begin()
        local.append(pltpu.make_async_copy(nb.at[m], slot(at.y, at.n, None), ls.at[micro + m]))
        local[-1].start()

    reduce_rows(wire, at, red, compute, finish)
    run_spreads(spreads, local)
    wire.finish()


def attn_out(att, wo, x_all, gain, shift):
    micro, _, tok, width = x_all.shape
    sub = tok // 4
    count = (REDUCE + SPREAD) * micro
    return kernel(
        attn_out_kernel, (att, wo, x_all, gain, shift), [VMEM, VMEM, ANY, VMEM, VMEM],
        (shaped((micro, sub, width), F32), shaped((micro, 2, 4, sub, width))), (VMEM, ANY), 85, "attn_out",
        reduce_scratch(micro, tok, sub, width) + [pltpu.VMEM((micro, sub, width), BF)] * 2 + sems(count, count, 2 * micro),
        talk=1,
    )


def nt_compute(part, lows, ws, first, each=0):
    zn, dz, _ = ws[0].shape
    tok = part.shape[2]
    span = lows[0].shape[1]

    def compute(m, yy):
        def tile(lo, size):
            at = pl.multiple_of((m * 2 + yy) * tok, tok) + lo
            for k in range(zn):
                acc = None
                for i, (low, w) in enumerate(zip(lows, ws)):
                    lo_col = first + i * each
                    term = dot_nt(low[pl.ds(at, size), :], w[k, :, lo_col : lo_col + span])
                    acc = term if acc is None else acc + term
                part[m, yy, pl.ds(lo, size), k * dz : (k + 1) * dz] = acc.astype(BF)

        blockwise(part, m, yy, tile)

    return compute


class Columns:
    def __init__(self, groups, cols, bufs, load):
        self.copies = [
            pltpu.make_async_copy(src.at[:, :, cols], bufs.at[k], load.at[k]) for k, src in enumerate(groups)
        ]
        for copy in self.copies:
            copy.start()

    def wait(self):
        for copy in self.copies:
            copy.wait()


def chunk_refs(pair, last):
    return [pair.at[:, k] for k in range(pair.shape[1])] + [last]


def ffn_back_kernel(jobs, parts, *refs):
    guls = refs[:parts]
    pair, last, d_all, middle, gain, *refs = refs[parts:]
    zin, (mid_grad, branch, vec), refs = refs[: len(jobs.ins)], refs[len(jobs.ins) :][:3], refs[len(jobs.ins) + 3 :]
    zout, refs = refs[: len(jobs.outs)], refs[len(jobs.outs) :]
    *red, db, nb, wv, ss, rs, ls, lw, zb, zl = refs
    at = Place()
    micro, sub, width = middle.shape
    span = guls[0].shape[1]
    weights = Columns(chunk_refs(pair, last), pl.ds(0, span), wv, lw)
    own = [pltpu.make_async_copy(d_all.at[m, at.y, pl.ds(at.n * sub, sub)], db.at[m], ls.at[m]) for m in range(micro)]
    for copy in own:
        copy.start()
    meet([at.sib, at.xn, at.yn] + z_partners(jobs.zn))
    wire = Wire(ss, rs)
    host = jobs.host(wire, zin, zout, (zb, zl))
    host.begin()
    vec[...] = jnp.zeros_like(vec)
    spreads, local = [], []

    def finish(m, total):
        own[m].wait()
        step = sub // 2
        for lo in range(0, sub, step):
            grad = total(lo, step)
            xhat, rstd = normalise(middle[m, lo : lo + step, :])
            vec[0:1, :] += jnp.sum(grad * xhat, axis=0, keepdims=True)
            vec[1:2, :] += jnp.sum(grad, axis=0, keepdims=True)
            mg = db[m, lo : lo + step, :].astype(F32) + norm_back(xhat, rstd, grad, gain[...])
            mid_grad[m, lo : lo + step, :] = mg
            nb[m, lo : lo + step, :] = mg.astype(BF)
        slot = row_slot(branch, m, sub)
        spreads.append(Spread(wire, at, nb.at[m], slot))
        spreads[-1].begin()
        local.append(pltpu.make_async_copy(nb.at[m], slot(at.y, at.n, None), ls.at[micro + m]))
        local[-1].start()

    weights.wait()
    reduce_rows(wire, at, red, nt_compute(red[0], guls, [wv.at[k] for k in range(parts)], 0), finish, host.next)
    run_spreads(spreads, local)
    host.end()
    wire.finish()


def ffn_back(guls, pair, last, d_all, middle, gain, plan, zn, first):
    parts = len(guls)
    micro, _, tok, width = d_all.shape
    sub = tok // 4
    jobs = Jobs(plan, zn)
    count = (REDUCE + SPREAD) * micro + 2 * jobs.steps
    span = guls[0].shape[1]
    return kernel(
        functools.partial(ffn_back_kernel, jobs, parts), (*guls, pair, last, d_all, middle, gain, *jobs.ins),
        [VMEM] * parts + [ANY, ANY, ANY, VMEM, VMEM] + [ANY] * len(jobs.ins),
        (shaped((micro, sub, width), F32), shaped((micro, 2, 4, sub, width)), shaped((8, width), F32), *jobs.outs),
        (VMEM, ANY, VMEM) + (ANY,) * len(jobs.outs), 90, "ffn_back",
        reduce_scratch(micro, tok, sub, width) + [pltpu.VMEM((micro, sub, width), BF)] * 2
        + [pltpu.VMEM((parts, zn, width // zn, span), BF)] + sems(count, count, 2 * micro, parts) + jobs.scratch,
        first, talk=2,
    )


def host_kernel(jobs, *refs):
    zin, zout, (ss, rs, zb, zl) = refs[: len(jobs.ins)], refs[len(jobs.ins) :][: len(jobs.outs)], refs[-4:]
    meet(z_partners(jobs.zn))
    host = jobs.host(Wire(ss, rs), zin, zout, (zb, zl))
    host.begin()
    host.end()


def host_only(plan, zn, first):
    jobs = Jobs(plan, zn)
    return kernel(
        functools.partial(host_kernel, jobs), jobs.ins, [ANY] * len(jobs.ins), tuple(jobs.outs), (ANY,) * len(jobs.outs),
        20 * jobs.steps, "along_z", sems(2 * jobs.steps, 2 * jobs.steps) + jobs.scratch, first, talk=8,
    )


class Deal:
    def __init__(self, wire, at, rows, out, m, sems, k):
        sub, width = rows.shape[1], rows.shape[2]
        feat = width // 4

        def cols(nn):
            return rows.at[m, :, pl.ds(pl.multiple_of(nn * feat, feat), feat)]

        place = out.at[m, pl.ds(pl.multiple_of(at.n * sub, sub), sub)]
        self.local = pltpu.make_async_copy(cols(at.n), place, sems.at[k])
        self.copies = [
            wire.make(cols(at.nx), place, at.xn),
            wire.make(cols(at.nd), place, at.xs),
            wire.make(cols(at.ns), place, at.sib),
        ]

    def begin(self):
        for copy in self.copies:
            copy.start()
        self.local.start()

    def end(self):
        for copy in self.copies:
            copy.wait_recv()
        self.local.wait()


def last_kernel(jobs, zn, *refs):
    low, wa, x_all, mid_grad, gain, vec2, g1, got1, got2, *refs = refs
    zin, refs = refs[: len(jobs.ins)], refs[len(jobs.ins) :]
    in_grad, sums, *refs = refs
    settled, zout, refs = refs[:6], refs[6:][: len(jobs.outs)], refs[6 + len(jobs.outs) :]
    red, refs = refs[:8], refs[8:]
    xb, ob, w1, mine, plane, summed, lines, yb, yl, ss, rs, ls, *talk = refs
    at = Place()
    z = lax.axis_index("z")
    micro, sub, width = mid_grad.shape
    qkv = pltpu.make_async_copy(wa.at[:, :, pl.ds(0, low.shape[1])], w1, ls.at[2 * micro])
    qkv.start()
    own = [pltpu.make_async_copy(x_all.at[m, at.y, pl.ds(at.n * sub, sub)], xb.at[m], ls.at[m]) for m in range(micro)]
    for copy in own:
        copy.start()
    flips = [(dy, dn) for dy in range(2) for dn in range(4) if dy or dn]
    peers = [{"y": (at.y + dy) % 2, "n": (at.n + dn) % 4} for dy, dn in flips]
    along = [{"z": (z + dz) % zn} for dz in range(1, zn)]
    meet(peers + along)
    wire = Wire(ss, rs)
    host = jobs.host(wire, zin, zout, talk)
    host.begin()
    g2, ga = zin[0], zin[3]
    settles = [
        Settle(wire, at, zn, g1, (got1, got2), settled[0], settled[1], yb, yl),
        Settle(wire, at, zn, g2, zout[0:2], settled[2], settled[3], yb, yl),
        Settle(wire, at, zn, ga, zout[-2:], settled[4], settled[5], yb, yl),
    ]

    def settle(k):
        def run():
            if k:
                settles[k - 1].wait()
            settles[k].go()

        return run

    host.then = {1: settle(1), zn: settle(2)}
    mine[...] = jnp.zeros_like(mine)
    mine[2:4] = vec2[0:2]
    qkv.wait()
    total = Reduce(wire, at, red, nt_compute(red[0], [low], [w1], 0))
    for m in range(micro):
        total.cores(m)
        total.diagonal(m)
    settle(0)()
    host.next()
    for m in range(micro):
        total.sides(m)
    step = sub // 2
    deals = []
    for m in range(micro):
        total.arrived(m)
        own[m].wait()
        for lo in range(0, sub, step):
            grad = total.total(m, lo, step)
            xhat, rstd = normalise(xb[m, lo : lo + step, :].astype(F32))
            mine[0:1, :] += jnp.sum(grad * xhat, axis=0, keepdims=True)
            mine[1:2, :] += jnp.sum(grad, axis=0, keepdims=True)
            back = norm_back(xhat, rstd, grad, gain[...])
            ob[m, lo : lo + step, :] = (mid_grad[m, lo : lo + step, :] + back).astype(BF)
        deals.append(Deal(wire, at, ob, in_grad, m, ls, micro + m))
        deals[-1].begin()
    near = [wire.make(mine, plane.at[k], d) for k, d in enumerate(peers)]
    for copy in near:
        copy.start()
    host.next()
    for copy in near:
        copy.wait_recv()
    both = mine[...]
    for k in range(len(peers)):
        both = both + plane[k]
    summed[...] = both
    far = [wire.make(summed, lines.at[k], d) for k, d in enumerate(along)]
    for copy in far:
        copy.start()
    host.next()
    for copy in far:
        copy.wait_recv()
    both = summed[...]
    for k in range(len(along)):
        both = both + lines[k]
    sums[...] = both
    for deal in deals:
        deal.end()
    host.end()
    settles[-1].wait()
    wire.finish()


def last_sums(low, wa, x_all, mid_grad, gain, vec2, g1, got, plan, zn):
    micro, _, tok, width = x_all.shape
    sub = tok // 4
    dz, cols = width // zn, low.shape[1]
    jobs = Jobs(plan, zn)
    count = (REDUCE + 3) * micro + 7 + zn - 1 + 2 * jobs.steps + 3
    size = vec2.shape
    rows = pltpu.VMEM((micro, sub, width), BF)
    chunk_cols, big = g1.shape[1], plan[-1][0].shape[1]
    halves = [shaped((dz // 2, k)) for k in (chunk_cols,) * 4 + (big, big)]
    return kernel(
        functools.partial(last_kernel, jobs, zn),
        (low, wa, x_all, mid_grad, gain, vec2, g1, *got, *jobs.ins),
        [VMEM, ANY, ANY, VMEM, VMEM, VMEM] + [ANY] * (3 + len(jobs.ins)),
        (shaped((micro, tok, width // 4)), shaped(size, F32), *halves, *jobs.outs),
        (ANY, VMEM) + (ANY,) * (6 + len(jobs.outs)), 100, "last_sums",
        reduce_scratch(micro, tok, sub, width) + [rows] * 2 + [pltpu.VMEM((zn, dz, cols), BF)]
        + [pltpu.VMEM(size, F32), pltpu.VMEM((7,) + size, F32), pltpu.VMEM(size, F32), pltpu.VMEM((zn - 1,) + size, F32)]
        + [pltpu.VMEM((3, dz, big), BF)] + sems(4, count, count, 2 * micro + 1) + jobs.scratch,
        talk=3,
    )


def tiles(rows, cols):
    return pl.BlockSpec((rows, cols), lambda i: (i, 0))


def same_protein(lens, b, tok, count):
    col = lax.broadcasted_iota(jnp.int32, (tok, 1), 0)
    row = lax.broadcasted_iota(jnp.int32, (1, tok), 1)
    pc, pr = jnp.zeros_like(col), jnp.zeros_like(row)
    end = jnp.int32(0)
    for k in range(count):
        end = end + lens[b % 2, b // 2, k]
        pc = pc + (col >= end).astype(jnp.int32)
        pr = pr + (row >= end).astype(jnp.int32)
    return pc == pr


def turn(v, cos, sin):
    return v * cos + pltpu.roll(v, HEAD_DIM // 2, 1) * sin


def attention_body(count, ends, n1, w, cos, sin, qkv, att):
    zn, dz, _ = w.shape
    cols = qkv.shape[1]
    tok = n1.shape[0]
    heads = cols // 3 // HEAD_DIM
    span = heads * HEAD_DIM
    acc = dot(n1[:, 0:dz], w[0, :, :cols])
    for k in range(1, zn):
        acc = acc + dot(n1[:, k * dz : (k + 1) * dz], w[k, :, :cols])
    same = same_protein(ends, pl.program_id(0), tok, count)
    scale = HEAD_DIM ** (-0.5)
    for h in range(heads):
        lo = h * HEAD_DIM
        q = turn(acc[:, lo : lo + HEAD_DIM], cos[...], sin[...]).astype(BF)
        k = turn(acc[:, span + lo : span + lo + HEAD_DIM], cos[...], sin[...]).astype(BF)
        v = acc[:, 2 * span + lo : 2 * span + lo + HEAD_DIM].astype(BF)
        qkv[:, lo : lo + HEAD_DIM] = q
        qkv[:, span + lo : span + lo + HEAD_DIM] = k
        qkv[:, 2 * span + lo : 2 * span + lo + HEAD_DIM] = v
        s = jnp.where(same, dot_nt(q, k) * scale, -1e30)
        e = jnp.exp(s - jnp.max(s, axis=-1, keepdims=True))
        p = (e / jnp.sum(e, axis=-1, keepdims=True)).astype(BF)
        att[:, lo : lo + HEAD_DIM] = dot(p, v).astype(BF)


def attention(count, ends, n1, w, cos, sin, passed, tok):
    rows, width = n1.shape
    cols = w.shape[2] // 4 * 3

    def body(e, a, b, c, d, _, qkv, att, __):
        attention_body(count, e, a, b, c, d, qkv, att)

    return kernel(
        body, (ends, n1, w, cos, sin, passed),
        [SMEM, tiles(tok, width), VMEM, tiles(tok, HEAD_DIM), tiles(tok, HEAD_DIM), ANY],
        (shaped((rows, cols)), shaped((rows, cols // 3)), shaped(passed.shape)),
        (tiles(tok, cols), tiles(tok, cols // 3), ANY), 20, "attention", grid=(rows // tok,), aliases={5: 2},
    )


def attention_back_body(count, ends, b, branch, wo, qkv, cos, sin, low):
    zn, dz, span = wo.shape
    tok = branch.shape[0]
    heads = span // HEAD_DIM
    acc = dot(branch[:, 0:dz], wo[0])
    for k in range(1, zn):
        acc = acc + dot(branch[:, k * dz : (k + 1) * dz], wo[k])
    same = same_protein(ends, b, tok, count)
    scale = HEAD_DIM ** (-0.5)
    for h in range(heads):
        lo = h * HEAD_DIM
        ag = acc[:, lo : lo + HEAD_DIM].astype(BF)
        q = qkv[:, lo : lo + HEAD_DIM]
        k = qkv[:, span + lo : span + lo + HEAD_DIM]
        v = qkv[:, 2 * span + lo : 2 * span + lo + HEAD_DIM]
        s = jnp.where(same, dot_nt(q, k) * scale, -1e30)
        e = jnp.exp(s - jnp.max(s, axis=-1, keepdims=True))
        p = e / jnp.sum(e, axis=-1, keepdims=True)
        pg = dot_nt(ag, v)
        vg = dot_tn(p.astype(BF), ag)
        rd = jnp.sum(p * pg, axis=-1, keepdims=True)
        sg = (p * (pg - rd)).astype(BF)
        qg = dot(sg, k) * scale
        kg = dot_tn(sg, q) * scale
        low[:, lo : lo + HEAD_DIM] = turn(qg, cos[...], -sin[...]).astype(BF)
        low[:, span + lo : span + lo + HEAD_DIM] = turn(kg, cos[...], -sin[...]).astype(BF)
        low[:, 2 * span + lo : 2 * span + lo + HEAD_DIM] = vg.astype(BF)


def attention_back_kernel(jobs, count, parts, *refs):
    lens, branch, att, wa, qkv, cos, sin, n1, g0, got0, got1, pair, last, middle, *refs = refs
    hids, zin, refs = refs[:parts], refs[parts:][: len(jobs.ins)], refs[parts + len(jobs.ins) :]
    low, grads, keep, theirs, layer_out, *refs = refs
    zout, refs = refs[: len(jobs.outs)], refs[len(jobs.outs) :]
    red, refs = refs[:8], refs[8:]
    bv, wo, ob, yb, load, yl, ls, ss, rs, *talk = refs
    rows, width = bv.shape
    zn, dz, span = wo.shape
    tok = rows // 4
    one = hids[0].shape[1]
    micro, sub, _ = middle.shape
    at = Place()
    cols = low.shape[1]
    downs, chunks = [], chunk_refs(pair, last)
    for k in range(parts):
        place = pl.ds(k * one, one)
        downs.append(pltpu.make_async_copy(hids[k], low.at[:, place], load.at[9 + k]))
        downs.append(
            pltpu.make_async_copy(chunks[k].at[:, :, pl.ds(2 * one, one)], grads.at[:, :, place], load.at[9 + parts + k])
        )
    for copy in downs:
        copy.start()
    weights = pltpu.make_async_copy(wa.at[:, :, pl.ds(cols, span)], wo, load.at[8])
    weights.start()

    def bring(b):
        here = pl.ds(b * tok, tok)
        return (
            pltpu.make_async_copy(branch.at[here], bv.at[here], load.at[b]),
            pltpu.make_async_copy(n1.at[here], red[0].at[b // 2, b % 2], load.at[4 + b]),
        )

    for b in range(4):
        bring(b)[0].start()
    meet(z_partners(zn) + [at.sib, at.xn, at.yn, at.xs])
    wire = Wire(ss, rs)
    host = jobs.host(wire, zin, zout, talk)
    settle = Settle(wire, at, zn, g0, (got0, got1), keep, theirs, yb, yl)
    host.begin()
    for copy in downs:
        copy.wait()
    lows = [low.at[:, pl.ds(k * one, one)] for k in range(parts)]
    total = Reduce(wire, at, red, nt_compute(red[0], lows, [grads] * parts, 0, one))
    for m in range(micro):
        total.cores(m)
        total.diagonal(m)
    settle.go()
    weights.wait()

    def block(b):
        bring(b)[0].wait()
        here = pl.ds(b * tok, tok)
        attention_back_body(
            count, lens, b, bv.at[here], wo, qkv.at[here], cos.at[here], sin.at[here], low.at[here]
        )

    block(0)
    for m in range(micro):
        total.sides(m)
        total.release(m)
    for b in range(4):
        bring(b)[1].start()
    block(1)
    host.next()
    block(2)
    block(3)
    host.next()
    for b in range(4):
        bring(b)[1].wait()

    def weights_of(k, carry):
        here = pl.ds(pl.multiple_of(k * dz, dz), dz)
        acc = 0.0
        for b in range(4):
            acc = acc + dot_tn(red[0][b // 2, b % 2, :, here], low[pl.ds(b * tok, tok), :])
        grads[k, :, :cols] = acc.astype(BF)
        grads[k, :, cols:] = dot_tn(bv[:, here], att[...]).astype(BF)
        return carry

    lax.fori_loop(0, zn, weights_of, 0)
    deals, step = [], sub // 2
    for m in range(micro):
        total.arrived(m)
        for lo in range(0, sub, step):
            ob[m, lo : lo + step, :] = (middle[m, lo : lo + step, :] + total.total(m, lo, step)).astype(BF)
        deals.append(Deal(wire, at, ob, layer_out, m, ls, m))
        deals[-1].begin()
    host.next()
    settle.wait()
    for deal in deals:
        deal.end()
    host.end()
    wire.finish()


def attention_back(count, lens, branch, att, wa, qkv, cos, sin, n1, g0, got, pair, last, middle, hids, plan, zn):
    rows, width = branch.shape
    cols, span, parts = qkv.shape[1], att.shape[1], len(hids)
    micro, sub, _ = middle.shape
    tok = rows // 4
    dz = width // zn
    jobs = Jobs(plan, zn)
    half = shaped((dz // 2, g0.shape[1]))
    links = 2 * jobs.steps + 1 + (REDUCE + 3) * micro
    return kernel(
        functools.partial(attention_back_kernel, jobs, count, parts),
        (lens, branch, att, wa, qkv, cos, sin, n1, g0, *got, pair, last, middle, *hids, *jobs.ins),
        [SMEM, ANY, VMEM, ANY, VMEM, VMEM, VMEM, ANY] + [ANY] * 5 + [VMEM] + [ANY] * (parts + len(jobs.ins)),
        (shaped((rows, cols)), shaped((zn, dz, cols + span)), half, half, shaped((micro, tok, width // 4)), *jobs.outs),
        (VMEM, VMEM) + (ANY,) * (3 + len(jobs.outs)), 70, "attention_back",
        reduce_scratch(micro, tok, sub, width)
        + [pltpu.VMEM((rows, width), BF), pltpu.VMEM((zn, dz, span), BF), pltpu.VMEM((micro, sub, width), BF)]
        + [pltpu.VMEM((3, dz, g0.shape[1]), BF)]
        + sems(9 + 2 * parts, 4, micro, links, links) + jobs.scratch,
        talk=9,
    )


def chunk_body(jobs, c, n2, dy, w, mask, *refs):
    zin, (low, hidden, grad), refs = refs[: len(jobs.ins)], refs[len(jobs.ins) :][:3], refs[len(jobs.ins) + 3 :]
    zout, (nv, dv, wv, load, *talk) = refs[: len(jobs.outs)], refs[len(jobs.outs) :]
    zn, dz, cols = wv.shape
    one = cols // 3
    steps = load.shape[1] - 1
    tile = nv.shape[0] // steps
    whole = pltpu.make_async_copy(w if c is None else w.at[:, c], wv, load.at[0, steps])
    whole.start()

    def bring(t):
        at = pl.ds(pl.multiple_of(t * tile, tile), tile)
        return (
            pltpu.make_async_copy(n2.at[at], nv.at[at], load.at[0, t]),
            pltpu.make_async_copy(dy.at[at], dv.at[at], load.at[1, t]),
        )

    for t in range(steps):
        for copy in bring(t):
            copy.start()
    if talk:
        ss, rs, *talk = talk
        meet(z_partners(jobs.zn))
        host = jobs.host(Wire(ss, rs), zin, zout, talk)
        host.begin()
    whole.wait()

    def forward(t, carry):
        for copy in bring(t):
            copy.wait()
        at = pl.ds(pl.multiple_of(t * tile, tile), tile)
        acc = hg = 0.0
        for k in range(zn):
            acc = acc + dot(nv[at, k * dz : (k + 1) * dz], wv[k, :, : 2 * one])
            hg = hg + dot(dv[at, k * dz : (k + 1) * dz], wv[k, :, 2 * one :])
        hg = hg * mask[...]
        g, u = acc[:, :one], acc[:, one:]
        phi = 0.5 * (1.0 + lax.erf(g * (0.5**0.5)))
        slope = phi + g * jnp.exp(-0.5 * g * g) * 0.3989422804014327
        act = g * phi
        hidden[at, :] = (act * u * mask[...]).astype(BF)
        low[at, :one] = (hg * u * slope).astype(BF)
        low[at, one:] = (hg * act).astype(BF)
        return carry

    lax.fori_loop(0, steps, forward, 0)

    def weights(k, carry):
        at = pl.ds(pl.multiple_of(k * dz, dz), dz)
        grad[at, : 2 * one] = dot_tn(nv[:, at], low[...]).astype(BF)
        grad[at, 2 * one :] = dot_tn(dv[:, at], hidden[...]).astype(BF)
        return carry

    lax.fori_loop(0, zn, weights, 0)
    if jobs.steps:
        host.end()


def chunk(n2, dy, w, c, mask, plan, zn, talk, first):
    rows, width = n2.shape
    cols = w.shape[-1]
    one = cols // 3
    jobs = Jobs(plan, zn)
    return kernel(
        functools.partial(chunk_body, jobs, c), (n2, dy, w, mask, *jobs.ins), [ANY, ANY, ANY, VMEM] + [ANY] * len(jobs.ins),
        (shaped((rows, 2 * one)), shaped((rows, one)), shaped((width, cols)), *jobs.outs),
        (VMEM,) * 3 + (ANY,) * len(jobs.outs), 22, "ffn_chunk",
        [pltpu.VMEM((rows, width), BF)] * 2 + [pltpu.VMEM((zn, width // zn, cols), BF), pltpu.SemaphoreType.DMA((2, 5))]
        + (sems(2 * jobs.steps, 2 * jobs.steps) + jobs.scratch if jobs.steps else []),
        first, talk=talk if jobs.steps else None,
    )


def weight_grad_body(a, b, out):
    out[...] = dot_tn(a[...], b[...]).astype(BF)


def weight_grad(a, b, first=()):
    rows, width = a.shape
    cols = b.shape[1]
    tile = 512
    return kernel(
        weight_grad_body, (a, b), [pl.BlockSpec((rows, tile), lambda i: (0, i)), VMEM],
        shaped((width, cols)), tiles(tile, cols), 10, "weight_grad", first=first, grid=(width // tile,),
    )


def ordered(y, keep, got, axis):
    return jnp.concatenate([jnp.where(y == 0, keep, got), jnp.where(y == 0, got, keep)], axis=axis)


CHUNKS = 3


def on_device(inputs, lengths, counts, w_qkv, w_out, w_gu, w_down, g1, b1, g2, b2, dy_in):
    z = lax.axis_index("z")
    y = lax.axis_index("y")
    n = lax.axis_index("n")
    zn = lax.axis_size("z")
    micro, tok, feat = inputs.shape
    width = feat * lax.axis_size("n")
    rows = micro * 2 * tok
    depth = w_qkv.shape[1]
    half_slots = w_gu.shape[2] // 2
    one = half_slots // CHUNKS

    def gather_z(w):
        return lax.all_gather(w, "z", axis=0, tiled=False)

    own_attn = swap_attn(w_qkv, w_out)
    wa = gather_z(own_attn)
    vecs = jnp.stack([g1, b1, g2, b2]).astype(F32)
    vecs = jnp.pad(vecs, ((0, 4), (0, 0)))
    count = lengths.shape[2]
    lens = jnp.pad(lengths[:, 0], ((0, 8 - micro), (0, 128 - count)))
    half_dim = HEAD_DIM // 2
    freq = 10000.0 ** (-(jnp.arange(HEAD_DIM) % half_dim).astype(F32) / half_dim)
    x_all, norms, lens, cos, sin, own_01 = gather_x(
        inputs, vecs, lens, freq[None], w_gu, w_down, zn, (0, 1), one, count, (own_attn,)
    )
    norms = norms.transpose(2, 0, 1, 3).reshape(8, width)
    gain1, shift1, gain2, shift2 = (norms[i : i + 1] for i in range(4))
    own = jnp.sum(jnp.where(jnp.arange(counts.shape[0]) == n, counts, 0))
    mask = (y * half_slots + jnp.arange(half_slots) < own).astype(F32)[None]

    d_all, n1, own_2 = gather_d(dy_in, x_all, gain1, shift1, w_gu, w_down, (2,), one)
    dy = d_all.reshape(rows, width)
    qkv, att, own_2 = attention(count, lens, n1, wa, cos, sin, own_2, tok)
    w_01, w_2 = gather_z(own_01), gather_z(own_2)
    middle, n2 = attn_out(att, wa, x_all, gain2, shift2)
    n2 = n2.reshape(rows, width)

    def own_mask(c):
        return mask[:, c * one : (c + 1) * one]

    low0, hid0, g0 = chunk(n2, dy, w_01, 0, own_mask(0), [], zn, None, ())
    low1, hid1, grad1 = chunk(n2, dy, w_01, 1, own_mask(1), [], zn, None, (g0,))
    low2, hid2, grad2, *p = chunk(n2, dy, w_2, None, own_mask(2), [(g0, None, 0, 1)], zn, 7, (grad1,))
    mid_grad, branch, vec2, *q = ffn_back(
        [low0, low1, low2], w_01, w_2, d_all, middle, gain2, [(g0, p, 1, zn - 2), (grad1, None, 0, zn - 2)], zn, ()
    )
    got0, got1 = q[2 * zn - 6 : 2 * zn - 4], q[-2:]
    branch = branch.reshape(rows, width)
    low, attn_g, keep0, theirs0, layer_out, *r = attention_back(
        count, lens, branch, att, wa, qkv, cos, sin, n1, g0, got0, w_01, w_2, middle, [hid0, hid1, hid2],
        [(grad1, got1, zn - 2, 1), (grad2, None, 0, zn - 2)], zn,
    )
    in_grad, sums, keep1, theirs1, keep2, theirs2, keep, attn_theirs, *_ = last_sums(
        low, wa, x_all, mid_grad, gain1, vec2, grad1, r[0:2],
        [(grad2, r[-2:], zn - 2, 1), (attn_g.reshape(width, -1), None, 0, zn - 1)], zn,
    )
    pairs = [(keep0, theirs0), (keep1, theirs1), (keep2, theirs2)]

    def joined(k):
        mine, theirs = (jnp.concatenate([p[i][:, k * one : (k + 1) * one] for p in pairs], axis=1) for i in (0, 1))
        return ordered(y, mine, theirs, 1)

    gu_grad = jnp.stack([joined(0), joined(1)]).astype(F32)
    down_grad = joined(2).T.astype(F32)
    cols = 3 * att.shape[1]
    mine, theirs = (v[:, :cols].reshape(depth, 3, -1) for v in (keep, attn_theirs))
    qkv_grad = ordered(y, mine, theirs, 2).transpose(1, 0, 2).astype(F32)
    out_grad = ordered(y, keep[:, cols:].T, attn_theirs[:, cols:].T, 0).astype(F32)

    mine = lax.dynamic_slice_in_dim(sums, (z * 2 + y) * g1.shape[0], g1.shape[0], 1)
    return (
        layer_out,
        in_grad,
        qkv_grad,
        out_grad,
        gu_grad,
        down_grad,
        mine[0],
        mine[1],
        mine[2],
        mine[3],
    )


def solution(mesh):
    wide, narrow = mesh.shape["wide"], mesh.shape["narrow"]
    grid = Mesh(mesh.devices.reshape(wide // 2, 2, narrow), ("z", "y", "n"))
    w = ("z", "y")
    tokens, depth, lines, vector = P(None, w, "n"), P(None, w, "n"), P("n", w), P(w)
    return jax.shard_map(
        on_device,
        mesh=grid,
        in_specs=(
            tokens, P(None, w, None), P(), depth, lines, depth, lines,
            vector, vector, vector, vector, tokens,
        ),
        out_specs=(
            tokens, tokens, depth, lines, depth, lines, vector, vector, vector, vector,
        ),
        check_vma=False,
    )
```

time: 721 us -> 632 us (0.88)
  Pallas kernels: 455 us -> 578 us
  waiting for transfers between devices: 98 us -> 15.6 us
  matrix products: 47.8 us -> 0 us
  blocking collectives: 45.8 us -> 0 us
  other arithmetic: 21.8 us -> 7.51 us
  starting transfers between devices: 12.7 us -> 0.29 us
    pallas_call x10 -> x11, Pallas kernels: 455 us -> 578 us  [kernel(): pl.pallas_call(without(body, len(ins), extra), grid=grid, in_specs=list(i...]
    dot_general x4 -> x0, matrix products: 47.8 us -> none  [weight_grad(): return jnp.einsum('ta,tb->ab', a, b, preferred_element_type=F32).astype(BF)]
    psum x1 -> x0, blocking collectives: 45.8 us -> none  [on_device(): sums = lax.psum(sums, ('z', 'y', 'n'))]
    ppermute x9 -> x0, waiting for transfers between devices: 39.3 us -> none  [the longest x2 21.9 us: columns(): return ordered(y, cut(y), lax.ppermute(cut(1 - y), 'y', SWAP), 0)]
    reduce_scatter x4 -> x0, waiting for transfers between devices: 26.3 us -> none  [scatter_z(): return lax.psum_scatter(g, 'z', scatter_dimension=axis, tiled=True)]
    all_gather x4 -> x3, waiting for transfers between devices: 32.4 us -> 15.6 us  [gather_z(): return lax.all_gather(w, 'z', axis=0, tiled=False)]
    ppermute x9 -> x0, starting transfers between devices: 12.2 us -> none  [the longest x2 3.88 us: columns_back(): lax.ppermute(cut(1 - y), 'y', SWAP).reshape(depth, parts, cols)]
  transfers between devices with their start and end apart: 17 -> 3, of which waited for: 6 -> 1; matrix products, arithmetic and copies ran while one was open for 10% -> 1% of each run, Pallas kernels for 48% -> 38%
where the time goes in v2:
time: 632 us; the launch traced here: 629 us
  Pallas kernels  578 us (91%)
  waiting for transfers between devices  15.6 us (2%)
  between operations  14.5 us (2%)
  local copies, waits for them, and re-layouts  13.2 us (2%)
  other arithmetic  7.51 us (1%)
    pallas_call x11, Pallas kernels, kernel(): pl.pallas_call(without(body, len(ins), extra), grid=grid, in_specs=list(i...  578 us
    all_gather x3, waiting for transfers between devices, gather_z(): return lax.all_gather(w, 'z', axis=0, tiled=False)  15.6 us
  transfers between devices with their start and end apart: 3, of which 1 were waited for; matrix products, arithmetic and copies ran while one was open for 1% of the time, Pallas kernels for 38%

profile of v2, /device:TPU:0, one launch (start us, length us, event | category | flops | bytes accessed | tf_op | source)
XLA Modules:
  0.0 628.7 jit_solution(15391511218145942198)
XLA Ops:
  7.2 0.0 all-gather.7.cloned.1.call-start
  7.3 16.3 %swap_attn.1.refs_6_ = bf16[512,1024]{1,0:T(8,128)(2,1)} custom-call(bf16[3,256,512]{2,1,0:T(8,128)(2,1)} %refs_0_.3, bf16[512,256]{1,0:T(8,128)(2,1)} %refs_1_.1), custom_call_target="tpu_custom_call" | custom-call | flops 14000000000 | bytes 44800000 | tf_op jit(solution)/shard_map/swap_attn/pallas_call | solution.py:61
  23.6 0.0 all-gather.7.cloned.1.call-update
  23.6 0.0 all-gather.9.cloned.1.call-start
  23.8 0.6 pad.12.refs_2_
  24.4 0.5 fusion.11.refs_3_
  24.9 0.6 fusion.7.refs_1_
  25.5 53.6 %gather_x.1 = (bf16[2,2,512,2048]{3,2,1,0:T(8,128)(2,1)}, f32[4,2,8,256]{3,2,1,0:T(8,128)}, s32[2,8,128]{2,1,0:T(8,128)}, f32[2048,128]{1,0:T(8,128)}, f32[2048,...) custom-call(bf16[2,512,512]{2,1,0:T(8,128)(2,1)} %refs_0_.4, f32[8,256]{1,0:T(8,128)} %fusion.7.refs_1_, s32[8,128]{1,0:T(8,128)} %pad.12.refs_2_, ...), custom_call_target="tpu_custom_call" | custom-call | flops 48000000000 | bytes 153600000 | tf_op jit(solution)/shard_map/gather_x/pallas_call | solution.py:61
  79.2 0.2 all-gather.11.cloned.1.call-start
  79.4 0.4 copy-done.20
  79.8 0.6 fusion.12
  80.4 0.7 compare_convert_fusion
  81.1 0.6 fusion.21
  81.6 0.6 fusion.20
  82.3 46.2 %gather_d.1 = (bf16[2,2,512,2048]{3,2,1,0:T(8,128)(2,1)}, bf16[2048,2048]{1,0:T(8,128)(2,1)}, bf16[512,768]{1,0:T(8,128)(2,1)}) custom-call(bf16[2,512,512]{2,1,0:T(8,128)(2,1)} %refs_0_.5, bf16[2,2,512,2048]{3,2,1,0:T(8,128)(2,1)} %get-tuple-element.60.refs_1_.refs_2_, f32[1,2048]{1,0:T(1,128)} %bitcast.34, f32[1,2048]{1,0:T(1,128)} %bitcast.39, ...), custom_call_target="tpu_custom_call" | custom-call | flops 48000000000 | bytes 153600000 | tf_op jit(solution)/shard_map/gather_d/pallas_call | solution.py:61
  128.5 0.0 all-gather.7.cloned.1.call-done
  128.5 19.1 %attention.1 = (bf16[2048,768]{1,0:T(8,128)(2,1)}, bf16[2048,256]{1,0:T(8,128)(2,1)}, bf16[512,768]{1,0:T(8,128)(2,1)}) custom-call(s32[2,8,128]{2,1,0:T(8,128)} %get-tuple-element.59.refs_0_, bf16[2048,2048]{1,0:T(8,128)(2,1)} %get-tuple-element.62.refs_1_.refs_7_, bf16[4,512,1024]{2,1,0:T(8,128)(2,1)} %bitcast.49, ...), custom_call_target="tpu_custom_call", output_to_operand_aliasing={{2}: (5, {})} | custom-call | flops 20000000000 | bytes 64000000 | tf_op jit(solution)/shard_map/attention/pallas_call | solution.py:61
  147.6 79.9 %attn_out.1 = (f32[2,128,2048]{2,1,0:T(8,128)}, bf16[2,2,4,128,2048]{4,3,2,1,0:T(8,128)(2,1)}) custom-call(bf16[2048,256]{1,0:T(8,128)(2,1)} %get-tuple-element.66.refs_0_.refs_2_, bf16[4,512,1024]{2,1,0:T(8,128)(2,1)} %bitcast.50, bf16[2,2,512,2048]{3,2,1,0:T(8,128)(2,1)} %get-tuple-element.60.refs_1_.refs_2_, f32[1,2048]{1,0:T(1,128)} %bitcast.36, ...), custom_call_target="tpu_custom_call" | custom-call | flops 85000003584 | bytes 272000000 | tf_op jit(solution)/shard_map/attn_out/pallas_call | solution.py:61
  227.4 0.0 all-gather.9.cloned.1.call-done
  227.5 21.2 %ffn_chunk.3 = (bf16[2048,512]{1,0:T(8,128)(2,1)}, bf16[2048,256]{1,0:T(8,128)(2,1)}, bf16[2048,768]{1,0:T(8,128)(2,1)}) custom-call(bf16[2048,2048]{1,0:T(8,128)(2,1)} %bitcast.60, bf16[2048,2048]{1,0:T(8,128)(2,1)} %bitcast.56, bf16[4,2,512,768]{3,2,1,0:T(8,128)(2,1)} %bitcast.45, f32[1,256]{1,0:T(1,128)} %get-tuple-element.176.refs_3_), custom_call_target="tpu_custom_call" | custom-call | flops 22000001024 | bytes 70400000 | tf_op jit(solution)/shard_map/ffn_chunk/pallas_call | solution.py:61
  248.7 20.6 %ffn_chunk.4 = (bf16[2048,512]{1,0:T(8,128)(2,1)}, bf16[2048,256]{1,0:T(8,128)(2,1)}, bf16[2048,768]{1,0:T(8,128)(2,1)}) custom-call(bf16[2048,2048]{1,0:T(8,128)(2,1)} %bitcast.61, bf16[2048,2048]{1,0:T(8,128)(2,1)} %bitcast.57, bf16[4,2,512,768]{3,2,1,0:T(8,128)(2,1)} %bitcast.46, f32[1,256]{1,0:T(1,128)} %get-tuple-element.175.refs_3_, ...), custom_call_target="tpu_custom_call" | custom-call | flops 22000001024 | bytes 70400000 | tf_op jit(solution)/shard_map/ffn_chunk/pallas_call | solution.py:61
  269.3 15.5 %all-gather.11.cloned.1.call-done = bf16[2048,768]{1,0:T(8,128)(2,1)} async-done(((bf16[512,768]{1,0:T(8,128)(2,1)}), bf16[2048,768]{1,0:T(8,128)(2,1)}) %all-gather.11.cloned.1.call-update) | async-done | bytes 3145744 | tf_op jit(solution)/shard_map/all_gather | solution.py:1309
  284.9 21.6 %ffn_chunk.5 = (bf16[2048,512]{1,0:T(8,128)(2,1)}, bf16[2048,256]{1,0:T(8,128)(2,1)}, bf16[2048,768]{1,0:T(8,128)(2,1)}, bf16[512,768]{1,0:T(8,128)(2,1)}, bf16[512,768]{1,0:T(8,128)(2,1)}) custom-call(bf16[2048,2048]{1,0:T(8,128)(2,1)} %bitcast.62, bf16[2048,2048]{1,0:T(8,128)(2,1)} %bitcast.58, bf16[4,512,768]{2,1,0:T(8,128)(2,1)} %bitcast.53, ...), custom_call_target="tpu_custom_call" | custom-call | flops 22000001024 | bytes 70400000 | tf_op jit(solution)/shard_map/ffn_chunk/pallas_call | solution.py:61
  306.4 90.1 %ffn_back.1 = (f32[2,128,2048]{2,1,0:T(8,128)}, bf16[2,2,4,128,2048]{4,3,2,1,0:T(8,128)(2,1)}, f32[8,2048]{1,0:T(8,128)}, bf16[512,768]{1,0:T(8,128)(2,1)}, bf16...) custom-call(bf16[2048,512]{1,0:T(8,128)(2,1)} %get-tuple-element.70., ...), custom_call_target="tpu_custom_call" | custom-call | flops 89999998976 | bytes 288000000 | tf_op jit(solution)/shard_map/ffn_back/pallas_call | solution.py:61
  396.5 67.0 %attention_back.1 = (bf16[2048,768]{1,0:T(8,128)(2,1)}, bf16[4,512,1024]{2,1,0:T(8,128)(2,1)}, bf16[256,768]{1,0:T(8,128)(2,1)}, bf16[256,768]{1,0:T(8,128)(2,1)...) custom-call(s32[2,8,128]{2,1,0:T(8,128)} %get-tuple-element.59.refs_, ...), custom_call_target="tpu_custom_call" | custom-call | flops 70000001024 | bytes 224000000 | tf_op jit(solution)/shard_map/attention_back/pallas_call | solution.py:61
  463.5 142.1 %last_sums.1 = (bf16[2,512,512]{2,1,0:T(8,128)(2,1)}, f32[8,2048]{1,0:T(8,128)}, bf16[256,768]{1,0:T(8,128)(2,1)}, bf16[256,768]{1,0:T(8,128)(2,1)}, bf16[256,76...) custom-call(bf16[2048,768]{1,0:T(8,128)(2,1)} %get-tuple-element.90., ...), custom_call_target="tpu_custom_call" | custom-call | flops 99999997952 | bytes 320000000 | tf_op jit(solution)/shard_map/last_sums/pallas_call | solution.py:61
  605.6 1.3 broadcast_select_fusion.7
  607.0 1.1 select_bitcast_fusion.1
  608.1 0.7 fusion.18
  608.8 0.8 fusion.13
  609.6 0.8 fusion.15
  610.3 0.1 broadcast_select_fusion.1
  610.4 0.2 convert_bitcast_fusion
  610.6 1.6 copy.36
  612.3 1.0 copy.35
  613.3 0.2 copy.32
  613.5 0.2 copy.33
  613.7 0.1 convert_bitcast_fusion.1
  613.8 1.6 copy.34
  615.5 0.1 broadcast_select_fusion.5
  615.6 0.1 maximum_bitcast_fusion
  615.7 0.7 copy-done.6
  616.4 0.1 broadcast_select_fusion.3
  616.5 0.1 maximum_bitcast_fusion.1
  616.6 1.9 maximum_convert_fusion
  618.5 1.5 fusion.19
  620.0 1.0 copy.40
  620.9 1.0 copy.41
  (47 shorter events, 0.2 us)
Async XLA Ops:
  7.2 16.5 %copy-start.16 = (bf16[256]{0:T(256)(128)(2,1)S(1)}, bf16[256]{0:T(256)(128)(2,1)}, u32[]{:S(2)}) copy-start(bf16[256]{0:T(256)(128)(2,1)} %param.19) | copy-start | bytes 1540
  7.2 16.5 %copy-start.17 = (bf16[256]{0:T(256)(128)(2,1)S(1)}, bf16[256]{0:T(256)(128)(2,1)}, u32[]{:S(2)}) copy-start(bf16[256]{0:T(256)(128)(2,1)} %param.20) | copy-start | bytes 1540
  7.2 16.5 %copy-start.18 = (bf16[256]{0:T(256)(128)(2,1)S(1)}, bf16[256]{0:T(256)(128)(2,1)}, u32[]{:S(2)}) copy-start(bf16[256]{0:T(256)(128)(2,1)} %param.21) | copy-start | bytes 1540
  7.2 16.5 %copy-start.19 = (bf16[256]{0:T(256)(128)(2,1)S(1)}, bf16[256]{0:T(256)(128)(2,1)}, u32[]{:S(2)}) copy-start(bf16[256]{0:T(256)(128)(2,1)} %param.22) | copy-start | bytes 1540
  7.2 16.5 %copy-start.15 = (s32[2,1,4]{2,1,0:T(1,128)S(1)}, s32[2,1,4]{2,1,0:T(1,128)}, u32[]{:S(2)}) copy-start(s32[2,1,4]{2,1,0:T(1,128)} %param.13) | copy-start | bytes 100
  7.2 121.3 %all-gather.7.cloned.1.call-start = ((), (), s32[]{:S(2)}) async-start(), calls=%async_computation | async-start | bytes 5242880 | tf_op jit(solution)/shard_map/all_gather | solution.py:1309
  23.6 203.8 %all-gather.9.cloned.1.call-start = ((), (), s32[]{:S(2)}) async-start(), calls=%async_computation.1 | async-start | bytes 7864320 | tf_op jit(solution)/shard_map/all_gather | solution.py:1309
  79.1 0.7 copy-start.20
  79.1 2.5 copy-start.14
  79.2 205.7 %all-gather.11.cloned.1.call-start = ((), (), s32[]{:S(2)}) async-start(), calls=%async_computation.2 | async-start | bytes 3932160 | tf_op jit(solution)/shard_map/all_gather | solution.py:1309
  605.6 1.3 copy-start.13
  605.6 2.4 copy-start.8
  605.6 3.2 copy-start.9
  605.6 3.2 copy-start.10
  606.9 2.6 copy-start.11
  607.0 2.6 copy-start.12
  613.8 1.7 copy-start.2
  613.8 1.7 copy-start.3
  613.8 1.7 copy-start.4
  613.8 1.6 copy-start.5
  613.8 1.6 copy-start.7
  615.5 0.9 copy-start.6
  616.6 3.4 copy-start
  618.5 2.5 copy-start.1
Sparse Core Ops, SparseCore 0:
  23.7 82.2 all-gather.6
  107.6 113.8 all-gather.8
  223.1 61.7 all-gather.10

commit v3 on v2

--- a/solution.py
+++ b/solution.py
@@ -281,11 +281,10 @@
     tick()
     for m in range(red.micro):
         red.sides(m)
-    tick()
     for m in range(red.micro):
         red.arrived(m)
         finish(m, lambda lo, size, m=m: red.total(m, lo, size))
-    tick()
+        tick()
 
 
 class Step:
@@ -341,17 +340,23 @@
     def __init__(self, wire, zn, jobs, bufs, load):
         z = lax.axis_index("z")
         self.steps, self.now, self.count, self.then, k = [], None, 0, {}, 0
+        self.chains, self.sizes = [], []
         for g, prev, first, outs in jobs:
             for i in range(len(outs) // 2):
                 got = outs[2 * i : 2 * i + 2]
                 self.steps.append(Step(wire, z, zn, first + i, g, prev, got, bufs, load, k))
+                self.chains.append(len(self.sizes))
                 prev = got
                 k += 4
-
-    def begin(self):
-        for step in self.steps:
-            step.begin()
-        self.next()
+            self.sizes.append(len(outs) // 2)
+        self.all = list(self.steps)
+
+    def begin(self, chains=None):
+        for step, chain in zip(self.all, self.chains):
+            if chains is None or chain in chains:
+                step.begin()
+        if self.now is None:
+            self.next()
 
     def next(self):
         if self.now is not None:
@@ -670,9 +675,10 @@
     return slot
 
 
-def run_spreads(spreads, local):
+def run_spreads(spreads, local, tick=nothing):
     for s in spreads:
         s.forward()
+    tick()
     for s in spreads:
         s.forward_last()
     for s in spreads:
@@ -812,7 +818,7 @@
 
     weights.wait()
     reduce_rows(wire, at, red, nt_compute(red[0], guls, [wv.at[k] for k in range(parts)], 0), finish, host.next)
-    run_spreads(spreads, local)
+    run_spreads(spreads, local, host.next)
     host.end()
     wire.finish()
 
@@ -879,12 +885,12 @@
 
 
 def last_kernel(jobs, zn, *refs):
-    low, wa, x_all, mid_grad, gain, vec2, g1, got1, got2, *refs = refs
+    low, wa, x_all, mid_grad, gain, vec2, g2, got2, got3, out_g, gout2, gout3, *refs = refs
     zin, refs = refs[: len(jobs.ins)], refs[len(jobs.ins) :]
     in_grad, sums, *refs = refs
     settled, zout, refs = refs[:6], refs[6:][: len(jobs.outs)], refs[6 + len(jobs.outs) :]
     red, refs = refs[:8], refs[8:]
-    xb, ob, w1, mine, plane, summed, lines, yb, yl, ss, rs, ls, *talk = refs
+    xb, ob, w1, mine, plane, summed, lines, yb2, ybo, ybq, yl2, ylo, ylq, ss, rs, ls, *talk = refs
     at = Place()
     z = lax.axis_index("z")
     micro, sub, width = mid_grad.shape
@@ -900,22 +906,12 @@
     wire = Wire(ss, rs)
     host = jobs.host(wire, zin, zout, talk)
     host.begin()
-    g2, ga = zin[0], zin[3]
     settles = [
-        Settle(wire, at, zn, g1, (got1, got2), settled[0], settled[1], yb, yl),
-        Settle(wire, at, zn, g2, zout[0:2], settled[2], settled[3], yb, yl),
-        Settle(wire, at, zn, ga, zout[-2:], settled[4], settled[5], yb, yl),
+        Settle(wire, at, zn, g2, (got2, got3), settled[0], settled[1], yb2, yl2),
+        Settle(wire, at, zn, out_g, (gout2, gout3), settled[2], settled[3], ybo, ylo),
+        Settle(wire, at, zn, zin[0], zout[-2:], settled[4], settled[5], ybq, ylq),
     ]
-
-    def settle(k):
-        def run():
-            if k:
-                settles[k - 1].wait()
-            settles[k].go()
-
-        return run
-
-    host.then = {1: settle(1), zn: settle(2)}
+    host.then = {zn - 1: settles[2].go}
     mine[...] = jnp.zeros_like(mine)
     mine[2:4] = vec2[0:2]
     qkv.wait()
@@ -923,10 +919,11 @@
     for m in range(micro):
         total.cores(m)
         total.diagonal(m)
-    settle(0)()
-    host.next()
     for m in range(micro):
         total.sides(m)
+    settles[0].go()
+    settles[1].go()
+    host.next()
     step = sub // 2
     deals = []
     for m in range(micro):
@@ -964,29 +961,30 @@
     for deal in deals:
         deal.end()
     host.end()
-    settles[-1].wait()
+    for settle in settles:
+        settle.wait()
     wire.finish()
 
 
-def last_sums(low, wa, x_all, mid_grad, gain, vec2, g1, got, plan, zn):
+def last_sums(low, wa, x_all, mid_grad, gain, vec2, g2, got2, out_g, gout, qkv_g, zn):
     micro, _, tok, width = x_all.shape
     sub = tok // 4
     dz, cols = width // zn, low.shape[1]
-    jobs = Jobs(plan, zn)
+    jobs = Jobs([(qkv_g, None, 0, zn - 1)], zn)
     count = (REDUCE + 3) * micro + 7 + zn - 1 + 2 * jobs.steps + 3
     size = vec2.shape
     rows = pltpu.VMEM((micro, sub, width), BF)
-    chunk_cols, big = g1.shape[1], plan[-1][0].shape[1]
-    halves = [shaped((dz // 2, k)) for k in (chunk_cols,) * 4 + (big, big)]
+    sizes = (g2.shape[1], out_g.shape[1], cols)
+    halves = [shaped((dz // 2, k)) for k in sizes for _ in range(2)]
     return kernel(
         functools.partial(last_kernel, jobs, zn),
-        (low, wa, x_all, mid_grad, gain, vec2, g1, *got, *jobs.ins),
-        [VMEM, ANY, ANY, VMEM, VMEM, VMEM] + [ANY] * (3 + len(jobs.ins)),
+        (low, wa, x_all, mid_grad, gain, vec2, g2, *got2, out_g, *gout, *jobs.ins),
+        [VMEM, ANY, ANY, VMEM, VMEM, VMEM] + [ANY] * (6 + len(jobs.ins)),
         (shaped((micro, tok, width // 4)), shaped(size, F32), *halves, *jobs.outs),
         (ANY, VMEM) + (ANY,) * (6 + len(jobs.outs)), 100, "last_sums",
         reduce_scratch(micro, tok, sub, width) + [rows] * 2 + [pltpu.VMEM((zn, dz, cols), BF)]
         + [pltpu.VMEM(size, F32), pltpu.VMEM((7,) + size, F32), pltpu.VMEM(size, F32), pltpu.VMEM((zn - 1,) + size, F32)]
-        + [pltpu.VMEM((3, dz, big), BF)] + sems(4, count, count, 2 * micro + 1) + jobs.scratch,
+        + [pltpu.VMEM((3, dz, k), BF) for k in sizes] + sems(4, 4, 4, count, count, 2 * micro + 1) + jobs.scratch,
         talk=3,
     )
 
@@ -1081,10 +1079,12 @@
 
 
 def attention_back_kernel(jobs, count, parts, *refs):
-    lens, branch, att, wa, qkv, cos, sin, n1, g0, got0, got1, pair, last, middle, *refs = refs
+    lens, branch, att, wa, qkv, cos, sin, n1, g0, got0, got1, g1, got2, got3, pair, last, middle, *refs = refs
     hids, zin, refs = refs[:parts], refs[parts:][: len(jobs.ins)], refs[parts + len(jobs.ins) :]
-    low, grads, keep, theirs, layer_out, *refs = refs
+    low, grads, out_g, *refs = refs
+    settled, layer_out, refs = refs[:4], refs[4], refs[5:]
     zout, refs = refs[: len(jobs.outs)], refs[len(jobs.outs) :]
+    zout, gout = zout[: -2 * (jobs.zn - 1)], zout[-2 * (jobs.zn - 1) :]
     red, refs = refs[:8], refs[8:]
     bv, wo, ob, yb, load, yl, ls, ss, rs, *talk = refs
     rows, width = bv.shape
@@ -1117,9 +1117,12 @@
         bring(b)[0].start()
     meet(z_partners(zn) + [at.sib, at.xn, at.yn, at.xs])
     wire = Wire(ss, rs)
-    host = jobs.host(wire, zin, zout, talk)
-    settle = Settle(wire, at, zn, g0, (got0, got1), keep, theirs, yb, yl)
-    host.begin()
+    host = Host(wire, zn, [(zin[0], None, 0, zout), (out_g, None, 0, gout)], *talk)
+    settles = [
+        Settle(wire, at, zn, g0, (got0, got1), settled[0], settled[1], yb, yl),
+        Settle(wire, at, zn, g1, (got2, got3), settled[2], settled[3], yb, yl),
+    ]
+    host.begin((0,))
     for copy in downs:
         copy.wait()
     lows = [low.at[:, pl.ds(k * one, one)] for k in range(parts)]
@@ -1127,11 +1130,21 @@
     for m in range(micro):
         total.cores(m)
         total.diagonal(m)
-    settle.go()
+    settles[0].go()
     weights.wait()
+    for b in range(4):
+        bring(b)[0].wait()
+
+    def output(k, carry):
+        here = pl.ds(pl.multiple_of(k * dz, dz), dz)
+        out_g[here, :] = dot_tn(bv[:, here], att[...]).astype(BF)
+        return carry
+
+    lax.fori_loop(0, zn, output, 0)
+    host.begin((1,))
+    host.next()
 
     def block(b):
-        bring(b)[0].wait()
         here = pl.ds(b * tok, tok)
         attention_back_body(
             count, lens, b, bv.at[here], wo, qkv.at[here], cos.at[here], sin.at[here], low.at[here]
@@ -1144,6 +1157,8 @@
     for b in range(4):
         bring(b)[1].start()
     block(1)
+    settles[0].wait()
+    settles[1].go()
     host.next()
     block(2)
     block(3)
@@ -1156,8 +1171,7 @@
         acc = 0.0
         for b in range(4):
             acc = acc + dot_tn(red[0][b // 2, b % 2, :, here], low[pl.ds(b * tok, tok), :])
-        grads[k, :, :cols] = acc.astype(BF)
-        grads[k, :, cols:] = dot_tn(bv[:, here], att[...]).astype(BF)
+        grads[k] = acc.astype(BF)
         return carry
 
     lax.fori_loop(0, zn, weights_of, 0)
@@ -1169,28 +1183,30 @@
         deals.append(Deal(wire, at, ob, layer_out, m, ls, m))
         deals[-1].begin()
     host.next()
-    settle.wait()
+    settles[1].wait()
     for deal in deals:
         deal.end()
     host.end()
     wire.finish()
 
 
-def attention_back(count, lens, branch, att, wa, qkv, cos, sin, n1, g0, got, pair, last, middle, hids, plan, zn):
+def attention_back(count, lens, branch, att, wa, qkv, cos, sin, n1, g0, got0, g1, got1, pair, last, middle, hids, g2, zn):
     rows, width = branch.shape
     cols, span, parts = qkv.shape[1], att.shape[1], len(hids)
     micro, sub, _ = middle.shape
     tok = rows // 4
     dz = width // zn
-    jobs = Jobs(plan, zn)
+    out_g = shaped((width, span))
+    jobs = Jobs([(g2, None, 0, zn - 1), (out_g, None, 0, zn - 1)], zn)
+    jobs.ins = [g2]
     half = shaped((dz // 2, g0.shape[1]))
-    links = 2 * jobs.steps + 1 + (REDUCE + 3) * micro
+    links = 2 * jobs.steps + 2 + (REDUCE + 3) * micro
     return kernel(
         functools.partial(attention_back_kernel, jobs, count, parts),
-        (lens, branch, att, wa, qkv, cos, sin, n1, g0, *got, pair, last, middle, *hids, *jobs.ins),
-        [SMEM, ANY, VMEM, ANY, VMEM, VMEM, VMEM, ANY] + [ANY] * 5 + [VMEM] + [ANY] * (parts + len(jobs.ins)),
-        (shaped((rows, cols)), shaped((zn, dz, cols + span)), half, half, shaped((micro, tok, width // 4)), *jobs.outs),
-        (VMEM, VMEM) + (ANY,) * (3 + len(jobs.outs)), 70, "attention_back",
+        (lens, branch, att, wa, qkv, cos, sin, n1, g0, *got0, g1, *got1, pair, last, middle, *hids, *jobs.ins),
+        [SMEM, ANY, VMEM, ANY, VMEM, VMEM, VMEM, ANY] + [ANY] * 8 + [VMEM] + [ANY] * (parts + len(jobs.ins)),
+        (shaped((rows, cols)), shaped((zn, dz, cols)), out_g, *(half,) * 4, shaped((micro, tok, width // 4)), *jobs.outs),
+        (VMEM, VMEM, VMEM) + (ANY,) * (5 + len(jobs.outs)), 70, "attention_back",
         reduce_scratch(micro, tok, sub, width)
         + [pltpu.VMEM((rows, width), BF), pltpu.VMEM((zn, dz, span), BF), pltpu.VMEM((micro, sub, width), BF)]
         + [pltpu.VMEM((3, dz, g0.shape[1]), BF)]
@@ -1272,22 +1288,38 @@
     )
 
 
-def weight_grad_body(a, b, out):
-    out[...] = dot_tn(a[...], b[...]).astype(BF)
-
-
-def weight_grad(a, b, first=()):
-    rows, width = a.shape
-    cols = b.shape[1]
-    tile = 512
+def form_body(parts, *refs):
+    halves, (gu, down, qkv, out) = refs[: 2 * parts + 4], refs[2 * parts + 4 :]
+    y = lax.axis_index("y")
+    one = halves[0].shape[1] // 3
+
+    def pair(k):
+        keep, theirs = halves[2 * k][...].astype(F32), halves[2 * k + 1][...].astype(F32)
+        return jnp.where(y == 0, keep, theirs), jnp.where(y == 0, theirs, keep)
+
+    half = parts * one
+    for k in range(parts):
+        for i, v in enumerate(pair(k)):
+            lo = i * half + k * one
+            gu[0, :, lo : lo + one] = v[:, :one]
+            gu[1, :, lo : lo + one] = v[:, one : 2 * one]
+            down[lo : lo + one, :] = v[:, 2 * one :].T
+    for i, v in enumerate(pair(parts)):
+        span = v.shape[1]
+        out[i * span : (i + 1) * span, :] = v.T
+    for i, v in enumerate(pair(parts + 1)):
+        span = v.shape[1] // 3
+        for p in range(3):
+            qkv[p, :, i * span : (i + 1) * span] = v[:, p * span : (p + 1) * span]
+
+
+def form(halves, w_gu, w_down, w_qkv, w_out):
+    parts = (len(halves) - 4) // 2
     return kernel(
-        weight_grad_body, (a, b), [pl.BlockSpec((rows, tile), lambda i: (0, i)), VMEM],
-        shaped((width, cols)), tiles(tile, cols), 10, "weight_grad", first=first, grid=(width // tile,),
-    )
-
-
-def ordered(y, keep, got, axis):
-    return jnp.concatenate([jnp.where(y == 0, keep, got), jnp.where(y == 0, got, keep)], axis=axis)
+        functools.partial(form_body, parts), halves, [VMEM] * len(halves),
+        tuple(shaped(w.shape, F32) for w in (w_gu, w_down, w_qkv, w_out)),
+        (VMEM,) * 4, 8, "form",
+    )
 
 
 CHUNKS = 3
@@ -1338,30 +1370,20 @@
     low1, hid1, grad1 = chunk(n2, dy, w_01, 1, own_mask(1), [], zn, None, (g0,))
     low2, hid2, grad2, *p = chunk(n2, dy, w_2, None, own_mask(2), [(g0, None, 0, 1)], zn, 7, (grad1,))
     mid_grad, branch, vec2, *q = ffn_back(
-        [low0, low1, low2], w_01, w_2, d_all, middle, gain2, [(g0, p, 1, zn - 2), (grad1, None, 0, zn - 2)], zn, ()
+        [low0, low1, low2], w_01, w_2, d_all, middle, gain2, [(g0, p, 1, zn - 2), (grad1, None, 0, zn - 1)], zn, ()
     )
     got0, got1 = q[2 * zn - 6 : 2 * zn - 4], q[-2:]
     branch = branch.reshape(rows, width)
-    low, attn_g, keep0, theirs0, layer_out, *r = attention_back(
-        count, lens, branch, att, wa, qkv, cos, sin, n1, g0, got0, w_01, w_2, middle, [hid0, hid1, hid2],
-        [(grad1, got1, zn - 2, 1), (grad2, None, 0, zn - 2)], zn,
-    )
-    in_grad, sums, keep1, theirs1, keep2, theirs2, keep, attn_theirs, *_ = last_sums(
-        low, wa, x_all, mid_grad, gain1, vec2, grad1, r[0:2],
-        [(grad2, r[-2:], zn - 2, 1), (attn_g.reshape(width, -1), None, 0, zn - 1)], zn,
-    )
-    pairs = [(keep0, theirs0), (keep1, theirs1), (keep2, theirs2)]
-
-    def joined(k):
-        mine, theirs = (jnp.concatenate([p[i][:, k * one : (k + 1) * one] for p in pairs], axis=1) for i in (0, 1))
-        return ordered(y, mine, theirs, 1)
-
-    gu_grad = jnp.stack([joined(0), joined(1)]).astype(F32)
-    down_grad = joined(2).T.astype(F32)
-    cols = 3 * att.shape[1]
-    mine, theirs = (v[:, :cols].reshape(depth, 3, -1) for v in (keep, attn_theirs))
-    qkv_grad = ordered(y, mine, theirs, 2).transpose(1, 0, 2).astype(F32)
-    out_grad = ordered(y, keep[:, cols:].T, attn_theirs[:, cols:].T, 0).astype(F32)
+    low, qkv_g, out_g, *r = attention_back(
+        count, lens, branch, att, wa, qkv, cos, sin, n1, g0, got0, grad1, got1, w_01, w_2, middle, [hid0, hid1, hid2], grad2, zn
+    )
+    first, layer_out, got2, gout = r[:4], r[4], r[2 * zn + 1 : 2 * zn + 3], r[-2:]
+    in_grad, sums, *r = last_sums(
+        low, wa, x_all, mid_grad, gain1, vec2, grad2, got2, out_g, gout, qkv_g.reshape(width, -1), zn
+    )
+    gu_grad, down_grad, qkv_grad, out_grad = form(
+        [*first, *r[:6]], w_gu, w_down, w_qkv, w_out
+    )
 
     mine = lax.dynamic_slice_in_dim(sums, (z * 2 + y) * g1.shape[0], g1.shape[0], 1)
     return (

time: 632 us -> 598 us (0.946)
  Pallas kernels: 578 us -> 554 us
  local copies, waits for them, and re-layouts: 13.2 us -> 6.33 us
    pallas_call x11 -> x12, Pallas kernels: 578 us -> 554 us  [kernel(): pl.pallas_call(without(body, len(ins), extra), grid=grid, in_specs=list(i...]
  transfers between devices with their start and end apart: 3 -> 3, of which waited for: 1 -> 1; matrix products, arithmetic and copies ran while one was open for 1% -> 1% of each run, Pallas kernels for 38% -> 41%
where the time goes in v3:
time: 598 us; the launch traced here: 593 us
  Pallas kernels  554 us (93%)
  waiting for transfers between devices  15.3 us (3%)
  between operations  14.3 us (2%)
  local copies, waits for them, and re-layouts  6.33 us (1%)
    pallas_call x12, Pallas kernels, kernel(): pl.pallas_call(without(body, len(ins), extra), grid=grid, in_specs=list(i...  554 us
    all_gather x3, waiting for transfers between devices, gather_z(): return lax.all_gather(w, 'z', axis=0, tiled=False)  15.2 us
  transfers between devices with their start and end apart: 3, of which 1 were waited for; matrix products, arithmetic and copies ran while one was open for 1% of the time, Pallas kernels for 41%

profile of v3, /device:TPU:0, one launch (start us, length us, event | category | flops | bytes accessed | tf_op | source)
XLA Modules:
  0.0 592.7 jit_solution(5361250725044662906)
XLA Ops:
  7.2 0.0 copy-start.3
  7.2 0.0 copy-start.4
  7.2 0.0 copy-start.5
  7.2 0.0 copy-start.6
  7.2 0.0 copy-start.2
  7.2 0.0 all-gather.7.cloned.1.call-start
  7.3 16.3 %swap_attn.1.refs_6_ = bf16[512,1024]{1,0:T(8,128)(2,1)} custom-call(bf16[3,256,512]{2,1,0:T(8,128)(2,1)} %refs_0_.3, bf16[512,256]{1,0:T(8,128)(2,1)} %refs_1_.1), custom_call_target="tpu_custom_call" | custom-call | flops 14000000000 | bytes 44800000 | tf_op jit(solution)/shard_map/swap_attn/pallas_call | solution.py:61
  23.6 0.0 all-gather.7.cloned.1.call-update
  23.6 0.0 all-gather.9.cloned.1.call-start
  23.7 0.0 copy-done.3
  23.7 0.0 copy-done.4
  23.7 0.0 copy-done.5
  23.7 0.0 copy-done.6
  23.8 0.0 copy-done.2
  23.8 0.6 pad.12.refs_2_
  24.4 0.5 fusion.11.refs_3_
  24.9 0.6 fusion.7.refs_1_
  25.5 0.0 copy-start.7
  25.5 53.6 %gather_x.1 = (bf16[2,2,512,2048]{3,2,1,0:T(8,128)(2,1)}, f32[4,2,8,256]{3,2,1,0:T(8,128)}, s32[2,8,128]{2,1,0:T(8,128)}, f32[2048,128]{1,0:T(8,128)}, f32[2048,...) custom-call(bf16[2,512,512]{2,1,0:T(8,128)(2,1)} %refs_0_.4, f32[8,256]{1,0:T(8,128)} %fusion.7.refs_1_, s32[8,128]{1,0:T(8,128)} %pad.12.refs_2_, ...), custom_call_target="tpu_custom_call" | custom-call | flops 48000000000 | bytes 153600000 | tf_op jit(solution)/shard_map/gather_x/pallas_call | solution.py:61
  79.1 0.0 all-gather.9.cloned.1.call-update
  79.1 0.2 all-gather.11.cloned.1.call-start
  79.4 0.0 copy-done.7
  79.4 0.6 fusion.12
  80.0 0.7 compare_convert_fusion
  80.7 0.6 fusion.15
  81.2 1.7 fusion.14
  82.9 46.2 %gather_d.1 = (bf16[2,2,512,2048]{3,2,1,0:T(8,128)(2,1)}, bf16[2048,2048]{1,0:T(8,128)(2,1)}, bf16[512,768]{1,0:T(8,128)(2,1)}) custom-call(bf16[2,512,512]{2,1,0:T(8,128)(2,1)} %refs_0_.5, bf16[2,2,512,2048]{3,2,1,0:T(8,128)(2,1)} %get-tuple-element.67.refs_1_.refs_2_, f32[1,2048]{1,0:T(1,128)} %bitcast.18, f32[1,2048]{1,0:T(1,128)} %bitcast.23, ...), custom_call_target="tpu_custom_call" | custom-call | flops 48000000000 | bytes 153600000 | tf_op jit(solution)/shard_map/gather_d/pallas_call | solution.py:61
  129.1 0.0 all-gather.7.cloned.1.call-done
  129.1 19.1 %attention.1 = (bf16[2048,768]{1,0:T(8,128)(2,1)}, bf16[2048,256]{1,0:T(8,128)(2,1)}, bf16[512,768]{1,0:T(8,128)(2,1)}) custom-call(s32[2,8,128]{2,1,0:T(8,128)} %get-tuple-element.66.refs_0_, bf16[2048,2048]{1,0:T(8,128)(2,1)} %get-tuple-element.69.refs_1_.refs_7_, bf16[4,512,1024]{2,1,0:T(8,128)(2,1)} %bitcast.33, ...), custom_call_target="tpu_custom_call", output_to_operand_aliasing={{2}: (5, {})} | custom-call | flops 20000000000 | bytes 64000000 | tf_op jit(solution)/shard_map/attention/pallas_call | solution.py:61
  148.2 0.0 all-gather.11.cloned.1.call-update
  148.2 79.9 %attn_out.1 = (f32[2,128,2048]{2,1,0:T(8,128)}, bf16[2,2,4,128,2048]{4,3,2,1,0:T(8,128)(2,1)}) custom-call(bf16[2048,256]{1,0:T(8,128)(2,1)} %get-tuple-element.73.refs_0_.refs_2_, bf16[4,512,1024]{2,1,0:T(8,128)(2,1)} %bitcast.34, bf16[2,2,512,2048]{3,2,1,0:T(8,128)(2,1)} %get-tuple-element.67.refs_1_.refs_2_, f32[1,2048]{1,0:T(1,128)} %bitcast.20, ...), custom_call_target="tpu_custom_call" | custom-call | flops 85000003584 | bytes 272000000 | tf_op jit(solution)/shard_map/attn_out/pallas_call | solution.py:61
  228.1 0.0 all-gather.9.cloned.1.call-done
  228.1 21.0 %ffn_chunk.3 = (bf16[2048,512]{1,0:T(8,128)(2,1)}, bf16[2048,256]{1,0:T(8,128)(2,1)}, bf16[2048,768]{1,0:T(8,128)(2,1)}) custom-call(bf16[2048,2048]{1,0:T(8,128)(2,1)} %bitcast.44, bf16[2048,2048]{1,0:T(8,128)(2,1)} %bitcast.40, bf16[4,2,512,768]{3,2,1,0:T(8,128)(2,1)} %bitcast.29, f32[1,256]{1,0:T(1,128)} %get-tuple-element.132.refs_3_), custom_call_target="tpu_custom_call" | custom-call | flops 22000001024 | bytes 70400000 | tf_op jit(solution)/shard_map/ffn_chunk/pallas_call | solution.py:61
  249.1 20.5 %ffn_chunk.4 = (bf16[2048,512]{1,0:T(8,128)(2,1)}, bf16[2048,256]{1,0:T(8,128)(2,1)}, bf16[2048,768]{1,0:T(8,128)(2,1)}) custom-call(bf16[2048,2048]{1,0:T(8,128)(2,1)} %bitcast.45, bf16[2048,2048]{1,0:T(8,128)(2,1)} %bitcast.41, bf16[4,2,512,768]{3,2,1,0:T(8,128)(2,1)} %bitcast.30, f32[1,256]{1,0:T(1,128)} %get-tuple-element.131.refs_3_, ...), custom_call_target="tpu_custom_call" | custom-call | flops 22000001024 | bytes 70400000 | tf_op jit(solution)/shard_map/ffn_chunk/pallas_call | solution.py:61
  269.7 15.2 %all-gather.11.cloned.1.call-done = bf16[2048,768]{1,0:T(8,128)(2,1)} async-done(((bf16[512,768]{1,0:T(8,128)(2,1)}), bf16[2048,768]{1,0:T(8,128)(2,1)}) %all-gather.11.cloned.1.call-update) | async-done | bytes 3145744 | tf_op jit(solution)/shard_map/all_gather | solution.py:1341
  284.9 21.6 %ffn_chunk.5 = (bf16[2048,512]{1,0:T(8,128)(2,1)}, bf16[2048,256]{1,0:T(8,128)(2,1)}, bf16[2048,768]{1,0:T(8,128)(2,1)}, bf16[512,768]{1,0:T(8,128)(2,1)}, bf16[512,768]{1,0:T(8,128)(2,1)}) custom-call(bf16[2048,2048]{1,0:T(8,128)(2,1)} %bitcast.46, bf16[2048,2048]{1,0:T(8,128)(2,1)} %bitcast.42, bf16[4,512,768]{2,1,0:T(8,128)(2,1)} %bitcast.37, ...), custom_call_target="tpu_custom_call" | custom-call | flops 22000001024 | bytes 70400000 | tf_op jit(solution)/shard_map/ffn_chunk/pallas_call | solution.py:61
  306.5 98.9 %ffn_back.1 = (f32[2,128,2048]{2,1,0:T(8,128)}, bf16[2,2,4,128,2048]{4,3,2,1,0:T(8,128)(2,1)}, f32[8,2048]{1,0:T(8,128)}, bf16[512,768]{1,0:T(8,128)(2,1)}, bf16...) custom-call(bf16[2048,512]{1,0:T(8,128)(2,1)} %get-tuple-element.77., ...), custom_call_target="tpu_custom_call" | custom-call | flops 89999998976 | bytes 288000000 | tf_op jit(solution)/shard_map/ffn_back/pallas_call | solution.py:61
  405.4 90.0 %attention_back.1 = (bf16[2048,768]{1,0:T(8,128)(2,1)}, bf16[4,512,768]{2,1,0:T(8,128)(2,1)}, bf16[2048,256]{1,0:T(8,128)(2,1)}, bf16[256,768]{1,0:T(8,128)(2,1)...) custom-call(s32[2,8,128]{2,1,0:T(8,128)} %get-tuple-element.66.refs_, ...), custom_call_target="tpu_custom_call" | custom-call | flops 70000001024 | bytes 224000000 | tf_op jit(solution)/shard_map/attention_back/pallas_call | solution.py:61
  495.4 81.8 %last_sums.1 = (bf16[2,512,512]{2,1,0:T(8,128)(2,1)}, f32[8,2048]{1,0:T(8,128)}, bf16[256,768]{1,0:T(8,128)(2,1)}, bf16[256,768]{1,0:T(8,128)(2,1)}, bf16[256,25...) custom-call(bf16[2048,768]{1,0:T(8,128)(2,1)} %get-tuple-element.97., ...), custom_call_target="tpu_custom_call" | custom-call | flops 99999997952 | bytes 320000000 | tf_op jit(solution)/shard_map/last_sums/pallas_call | solution.py:61
  577.2 1.5 fusion.13
  578.7 0.0 copy-start
  578.7 0.0 copy-start.1
  578.7 5.3 form.1
  583.9 0.0 copy-done
  583.9 1.0 copy.26
  584.9 0.0 copy-done.1
  584.9 1.0 copy.27
  (4 shorter events, 0.0 us)
Async XLA Ops:
  7.2 16.5 %copy-start.3 = (bf16[256]{0:T(256)(128)(2,1)S(1)}, bf16[256]{0:T(256)(128)(2,1)}, u32[]{:S(2)}) copy-start(bf16[256]{0:T(256)(128)(2,1)} %param.19) | copy-start | bytes 1540
  7.2 16.5 %copy-start.4 = (bf16[256]{0:T(256)(128)(2,1)S(1)}, bf16[256]{0:T(256)(128)(2,1)}, u32[]{:S(2)}) copy-start(bf16[256]{0:T(256)(128)(2,1)} %param.20) | copy-start | bytes 1540
  7.2 16.5 %copy-start.5 = (bf16[256]{0:T(256)(128)(2,1)S(1)}, bf16[256]{0:T(256)(128)(2,1)}, u32[]{:S(2)}) copy-start(bf16[256]{0:T(256)(128)(2,1)} %param.21) | copy-start | bytes 1540
  7.2 16.5 %copy-start.6 = (bf16[256]{0:T(256)(128)(2,1)S(1)}, bf16[256]{0:T(256)(128)(2,1)}, u32[]{:S(2)}) copy-start(bf16[256]{0:T(256)(128)(2,1)} %param.22) | copy-start | bytes 1540
  7.2 16.5 %copy-start.2 = (s32[2,1,4]{2,1,0:T(1,128)S(1)}, s32[2,1,4]{2,1,0:T(1,128)}, u32[]{:S(2)}) copy-start(s32[2,1,4]{2,1,0:T(1,128)} %param.13) | copy-start | bytes 100
  7.2 121.9 %all-gather.7.cloned.1.call-start = ((), (), s32[]{:S(2)}) async-start(), calls=%async_computation | async-start | bytes 5242880 | tf_op jit(solution)/shard_map/all_gather | solution.py:1341
  23.6 204.5 %all-gather.9.cloned.1.call-start = ((), (), s32[]{:S(2)}) async-start(), calls=%async_computation.1 | async-start | bytes 7864320 | tf_op jit(solution)/shard_map/all_gather | solution.py:1341
  25.5 53.9 %copy-start.7 = (s32[4]{0:T(128)S(1)}, s32[4]{0:T(128)}, u32[]{:S(2)}) copy-start(s32[4]{0:T(128)} %param.14) | copy-start | bytes 52
  79.1 205.7 %all-gather.11.cloned.1.call-start = ((), (), s32[]{:S(2)}) async-start(), calls=%async_computation.2 | async-start | bytes 3932160 | tf_op jit(solution)/shard_map/all_gather | solution.py:1341
  578.7 5.3 copy-start
  578.7 6.2 %copy-start.1 = (bf16[2,512,512]{2,1,0:T(8,128)(2,1)S(1)}, bf16[2,512,512]{2,1,0:T(8,128)(2,1)}, u32[]{:S(2)}) copy-start(bf16[2,512,512]{2,1,0:T(8,128)(2,1)} %get-tuple-element.144) | copy-start | bytes 3145732
Sparse Core Ops, SparseCore 0:
  23.7 82.2 all-gather.6
  107.6 113.8 all-gather.8
  223.1 61.7 all-gather.10

commit v4 on v3

--- a/solution.py
+++ b/solution.py
@@ -287,129 +287,164 @@
         tick()
 
 
-class Step:
-    def __init__(self, wire, z, zn, s, g, prev, got, bufs, load, k):
-        rows, cols = got[0].shape
-        far, cap = zn - 1 - s, min(s, zn - 2)
-        self.bufs, self.cols, self.ways = bufs, cols, []
-        for d, (place, sign) in enumerate(((z, 1), (zn - 1 - z, -1))):
-            group = (z + sign * far + zn) % zn
-            here = bufs.at[d, 0, :, pl.ds(0, cols)]
-            own = pltpu.make_async_copy(
-                g.at[pl.ds(pl.multiple_of(group * rows, rows), rows)], here, load.at[k + 2 * d]
-            )
-            came = bufs.at[d, 1, :, pl.ds(0, cols)]
-            carry = pltpu.make_async_copy(prev[d], came, load.at[k + 2 * d + 1]) if s else None
-            peer = {"z": (z + sign + zn) % zn}
-            away = wire.make(here, got[d], peer, keep=False)
-            last = d * (zn - 1 - far) + (1 - d) * far
-            straight = wire.make(g.at[pl.ds(last * rows, rows)], got[d], peer, keep=False, again=True)
-            gets = jnp.logical_and(place >= 1, place <= cap + 1)
-            adds = jnp.logical_and(place <= cap, place >= 1)
-            self.ways.append((place <= cap, adds, gets, own, carry, away, place == 0, straight))
+LINE = (
+    (0, 3, 1, -1, 0),
+    (3, 0, 2, -1, 0),
+    (1, 0, 0, 2, 0),
+    (2, 3, 3, 2, 0),
+    (1, 2, 2, 2, 0),
+    (2, 1, 1, 2, 0),
+    (0, 2, 2, 0, 1),
+    (3, 1, 1, 0, 1),
+    (0, 1, 1, 1, 1),
+    (3, 2, 2, 1, 1),
+)
+
+
+def chain_results(zn, parts, rows, cols):
+    count = 2 * len(parts) if zn == 4 else (zn - 1 if 0 in parts else 0)
+    return [shaped((rows, cols))] * count
+
+
+def chain_links(zn, parts):
+    return sum(t[4] in parts for t in LINE) + (1 in parts) if zn == 4 else (zn - 1 if 0 in parts else 0)
+
+
+class Chain:
+    def __init__(self, wire, zn, parts, g, first, second, bufs, load, k):
+        z = lax.axis_index("z")
+        rows, cols = (first or second)[0].shape
+        self.moves, self.bufs, self.cols, self.joins = [], bufs, cols, zn == 4 and 1 in parts
+        self.over = False
+
+        def group(i):
+            return g.at[pl.ds(pl.multiple_of(i * rows, rows), rows)]
+
+        if zn == 4:
+            places = {2: first[0], -1: first[1]}
+            if second:
+                places.update({0: second[0], 1: second[1]})
+            for src, i, dst, place, part in LINE:
+                if part in parts:
+                    copy = wire.make(group(i), places[place], {"z": dst}, keep=False)
+                    self.moves.append((z == src, z == dst, copy, place < 0))
+        elif 0 in parts:
+            for dz in range(1, zn):
+                to = (z + dz) % zn
+                self.moves.append((None, None, wire.make(group(to), first[dz - 1], {"z": to}, keep=False), False))
+        if self.joins:
+            far = 3 * (1 - z // 2)
+            here, there = bufs.at[0, :, pl.ds(0, cols)], bufs.at[1, :, pl.ds(0, cols)]
+            self.own = pltpu.make_async_copy(group(far), here, load.at[k])
+            self.came = pltpu.make_async_copy(first[1], there, load.at[k + 1])
+            self.on = wire.make(here, second[1], {"z": far}, keep=False)
+            self.inner = jnp.logical_and(z >= 1, z <= 2)
+            self.outer = jnp.logical_not(self.inner)
 
     def begin(self):
-        for *_, end, straight in self.ways:
-            pl.when(end)(straight.start)
+        for sends, _, copy, _ in self.moves:
+            if sends is None:
+                copy.start()
+            else:
+                pl.when(sends)(copy.start)
+
+    def join(self):
+        if not self.joins:
+            return
+
+        def run():
+            self.own.start()
+            self.came.start()
+            self.own.wait()
+            self.came.wait()
+            cols = pl.ds(0, self.cols)
+            both = self.bufs[0, :, cols].astype(F32) + self.bufs[1, :, cols].astype(F32)
+            self.bufs[0, :, cols] = both.astype(BF)
+            self.on.start()
+
+        for _, gets, copy, middle in self.moves:
+            if middle:
+                pl.when(gets)(copy.wait_recv)
+        pl.when(self.inner)(run)
+
+    def settle_sent(self):
+        if self.joins:
+            pl.when(self.inner)(self.on.wait_send)
+
+    def wait(self):
+        self.over = True
+        for sends, gets, copy, middle in self.moves:
+            if sends is None:
+                copy.wait_recv()
+                copy.wait_send()
+                continue
+            if not (middle and self.joins):
+                pl.when(gets)(copy.wait_recv)
+            pl.when(sends)(copy.wait_send)
+        if self.joins:
+            pl.when(self.outer)(self.on.wait_recv)
+
+
+class Host:
+    def __init__(self, chains):
+        self.chains, self.todo, self.last = chains, list(chains), None
+
+    def begin(self, which=None):
+        for k, chain in enumerate(self.chains):
+            if which is None or k == which:
+                chain.begin()
+
+    def next(self):
+        if self.todo:
+            if self.last is not None:
+                self.last.settle_sent()
+            self.last = self.todo.pop(0)
+            self.last.join()
+
+    def end(self):
+        while self.todo:
+            self.next()
+        self.last.settle_sent()
+        for chain in self.chains:
+            if not chain.over:
+                chain.wait()
+
+
+class Settle:
+    def __init__(self, wire, at, zn, g, first, second, keep, theirs, bufs, load):
+        z = lax.axis_index("z")
+        self.rows, self.cols = keep.shape[0] * 2, keep.shape[1]
+        rows, half = self.rows, keep.shape[0]
+        came = [first[0], second[1], second[0]] if zn == 4 else list(first)
+        self.bufs, self.partly = bufs, jnp.logical_and(z >= 1, z <= 2) if zn == 4 else None
+        mine = g.at[pl.ds(pl.multiple_of(z * rows, rows), rows)]
+        self.loads = [pltpu.make_async_copy(src, bufs.at[k], load.at[k]) for k, src in enumerate([mine] + came)]
+
+        def part(i):
+            return bufs.at[0, pl.ds(pl.multiple_of(i * half, half), half)]
+
+        self.away = wire.make(part(1 - at.y), theirs, at.yn, keep=False)
+        self.here = pltpu.make_async_copy(part(at.y), keep, load.at[len(self.loads)])
 
     def go(self):
-        for _, adds, _, own, carry, *_ in self.ways:
-            if carry is not None:
-                pl.when(adds)(own.start)
-                pl.when(adds)(carry.start)
-        for d, (_, adds, _, own, carry, away, *_) in enumerate(self.ways):
-            if carry is not None:
-
-                def add(d=d, own=own, carry=carry, away=away):
-                    own.wait()
-                    carry.wait()
-                    cols = pl.ds(0, self.cols)
-                    both = self.bufs[d, 0, :, cols].astype(F32) + self.bufs[d, 1, :, cols].astype(F32)
-                    self.bufs[d, 0, :, cols] = both.astype(BF)
-                    away.start()
-
-                pl.when(adds)(add)
-
-    def wait(self):
-        for sends, _, gets, _, _, away, *_ in self.ways:
-            pl.when(gets)(away.wait_recv)
-            pl.when(sends)(away.wait_send)
-
-
-class Host:
-    def __init__(self, wire, zn, jobs, bufs, load):
-        z = lax.axis_index("z")
-        self.steps, self.now, self.count, self.then, k = [], None, 0, {}, 0
-        self.chains, self.sizes = [], []
-        for g, prev, first, outs in jobs:
-            for i in range(len(outs) // 2):
-                got = outs[2 * i : 2 * i + 2]
-                self.steps.append(Step(wire, z, zn, first + i, g, prev, got, bufs, load, k))
-                self.chains.append(len(self.sizes))
-                prev = got
-                k += 4
-            self.sizes.append(len(outs) // 2)
-        self.all = list(self.steps)
-
-    def begin(self, chains=None):
-        for step, chain in zip(self.all, self.chains):
-            if chains is None or chain in chains:
-                step.begin()
-        if self.now is None:
-            self.next()
-
-    def next(self):
-        if self.now is not None:
-            self.now.wait()
-            self.count += 1
-            done, self.now = self.then.pop(self.count, None), None
-            if self.steps:
-                self.now = self.steps.pop(0)
-                self.now.go()
-            if done is not None:
-                done()
-        elif self.steps:
-            self.now = self.steps.pop(0)
-            self.now.go()
-
-    def end(self):
-        while self.steps or self.now is not None:
-            self.next()
-
-
-class Settle:
-    def __init__(self, wire, at, zn, g, got, keep, theirs, bufs, load):
-        z = lax.axis_index("z")
-        _, self.rows, self.cols = bufs.shape[0], keep.shape[0] * 2, keep.shape[1]
-        rows, half = self.rows, keep.shape[0]
-        self.bufs, self.has = bufs, (None, z >= 1, z <= zn - 2)
-        view = [bufs.at[k, :, pl.ds(0, self.cols)] for k in range(3)]
-        mine = g.at[pl.ds(pl.multiple_of(z * rows, rows), rows)]
-        self.loads = [pltpu.make_async_copy(src, view[k], load.at[k]) for k, src in enumerate((mine, got[0], got[1]))]
-
-        def part(i):
-            return bufs.at[0, pl.ds(pl.multiple_of(i * half, half), half), pl.ds(0, self.cols)]
-
-        self.away = wire.make(part(1 - at.y), theirs, at.yn, keep=False)
-        self.here = pltpu.make_async_copy(part(at.y), keep, load.at[3])
-
-    def go(self):
-        cols = pl.ds(0, self.cols)
-        self.loads[0].start()
-        for k in (1, 2):
-            pl.when(self.has[k])(self.loads[k].start)
-        self.loads[0].wait()
-        for k in (1, 2):
-            pl.when(self.has[k])(self.loads[k].wait)
-
-            def none(k=k):
-                self.bufs[k, :, cols] = jnp.zeros((self.rows, self.cols), BF)
-
-            pl.when(jnp.logical_not(self.has[k]))(none)
-        total = self.bufs[0, :, cols].astype(F32)
-        for k in (1, 2):
-            total = total + self.bufs[k, :, cols].astype(F32)
-        self.bufs[0, :, cols] = total.astype(BF)
+        always = self.loads if self.partly is None else self.loads[:-1]
+        for copy in always:
+            copy.start()
+        if self.partly is not None:
+            k = len(always)
+            pl.when(self.partly)(self.loads[k].start)
+            pl.when(self.partly)(self.loads[k].wait)
+
+            def none():
+                self.bufs[k] = jnp.zeros((self.rows, self.cols), BF)
+
+            pl.when(jnp.logical_not(self.partly))(none)
+        for copy in always:
+            copy.wait()
+        total = self.bufs[0].astype(F32)
+        for k in range(1, len(self.loads)):
+            total = total + self.bufs[k].astype(F32)
+        self.bufs[0] = total.astype(BF)
         self.away.start()
         self.here.start()
 
@@ -419,30 +454,37 @@
         self.here.wait()
 
 
+def settle_scratch(zn, rows, cols):
+    return [pltpu.VMEM((zn, rows, cols), BF)] + sems(zn + 1)
+
+
 def z_partners(zn):
     z = lax.axis_index("z")
-    return [{"z": (z + 1) % zn}, {"z": (z + zn - 1) % zn}]
+    return [{"z": (z + dz) % zn} for dz in range(1, zn)]
 
 
 class Jobs:
     def __init__(self, plan, zn):
         self.plan, self.zn = plan, zn
-        self.ins, self.outs = [], []
-        for g, prev, first, steps in plan:
-            self.ins += [g] + (list(prev) if prev is not None else [])
-            self.outs += [shaped((g.shape[0] // zn, g.shape[1]))] * (2 * steps)
-        self.steps = sum(p[3] for p in plan)
+        self.ins, self.outs, self.links = [], [], 0
+        for g, parts, given in plan:
+            self.ins += [g] + list(given)
+            self.outs += chain_results(zn, parts, g.shape[0] // zn, g.shape[1])
+            self.links += chain_links(zn, parts)
         wide = max([p[0].shape[1] for p in plan], default=0)
         rows = plan[0][0].shape[0] // zn if plan else 0
-        self.scratch = [pltpu.VMEM((2, 2, rows, wide), BF)] + sems(4 * self.steps) if plan else []
+        self.scratch = [pltpu.VMEM((2, rows, wide), BF)] + sems(2 * len(plan)) if plan else []
 
     def host(self, wire, ins, outs, scratch):
-        jobs, i, o = [], 0, 0
-        for _, prev, first, steps in self.plan:
-            took = 1 if prev is None else 3
-            jobs.append((ins[i], None if prev is None else ins[i + 1 : i + 3], first, outs[o : o + 2 * steps]))
-            i, o = i + took, o + 2 * steps
-        return Host(wire, self.zn, jobs, *scratch)
+        chains, i, o = [], 0, 0
+        for k, (g, parts, given) in enumerate(self.plan):
+            count = len(chain_results(self.zn, parts, 8, 128))
+            made = outs[o : o + count]
+            first = ins[i + 1 : i + 1 + len(given)] if given else (made if 1 not in parts or self.zn != 4 else made[:2])
+            second = [] if 1 not in parts or self.zn != 4 else made[-2:]
+            chains.append(Chain(wire, self.zn, parts, ins[i], first, second, *scratch, 2 * k))
+            i, o = i + 1 + len(given), o + count
+        return Host(chains)
 
 
 def blockwise(part, m, yy, fn, tile=256):
@@ -828,7 +870,7 @@
     micro, _, tok, width = d_all.shape
     sub = tok // 4
     jobs = Jobs(plan, zn)
-    count = (REDUCE + SPREAD) * micro + 2 * jobs.steps
+    count = (REDUCE + SPREAD) * micro + jobs.links
     span = guls[0].shape[1]
     return kernel(
         functools.partial(ffn_back_kernel, jobs, parts), (*guls, pair, last, d_all, middle, gain, *jobs.ins),
@@ -884,8 +926,9 @@
         self.local.wait()
 
 
-def last_kernel(jobs, zn, *refs):
-    low, wa, x_all, mid_grad, gain, vec2, g2, got2, got3, out_g, gout2, gout3, *refs = refs
+def last_kernel(jobs, zn, marks, *refs):
+    low, wa, x_all, mid_grad, gain, vec2, *refs = refs
+    g2, came2, refs = refs[0], refs[1 : 1 + marks], refs[1 + marks :]
     zin, refs = refs[: len(jobs.ins)], refs[len(jobs.ins) :]
     in_grad, sums, *refs = refs
     settled, zout, refs = refs[:6], refs[6:][: len(jobs.outs)], refs[6 + len(jobs.outs) :]
@@ -906,12 +949,12 @@
     wire = Wire(ss, rs)
     host = jobs.host(wire, zin, zout, talk)
     host.begin()
+    split = len(chain_results(zn, (0,), 8, 128))
     settles = [
-        Settle(wire, at, zn, g2, (got2, got3), settled[0], settled[1], yb2, yl2),
-        Settle(wire, at, zn, out_g, (gout2, gout3), settled[2], settled[3], ybo, ylo),
-        Settle(wire, at, zn, zin[0], zout[-2:], settled[4], settled[5], ybq, ylq),
+        Settle(wire, at, zn, g2, came2[:split], came2[split:], settled[0], settled[1], yb2, yl2),
+        Settle(wire, at, zn, zin[1], zout[marks : marks + split], zout[marks + split :], settled[2], settled[3], ybo, ylo),
+        Settle(wire, at, zn, zin[0], zout[:split], zout[split:marks], settled[4], settled[5], ybq, ylq),
     ]
-    host.then = {zn - 1: settles[2].go}
     mine[...] = jnp.zeros_like(mine)
     mine[2:4] = vec2[0:2]
     qkv.wait()
@@ -921,8 +964,6 @@
         total.diagonal(m)
     for m in range(micro):
         total.sides(m)
-    settles[0].go()
-    settles[1].go()
     host.next()
     step = sub // 2
     deals = []
@@ -938,10 +979,11 @@
             ob[m, lo : lo + step, :] = (mid_grad[m, lo : lo + step, :] + back).astype(BF)
         deals.append(Deal(wire, at, ob, in_grad, m, ls, micro + m))
         deals[-1].begin()
+        if m == 0:
+            settles[0].go()
     near = [wire.make(mine, plane.at[k], d) for k, d in enumerate(peers)]
     for copy in near:
         copy.start()
-    host.next()
     for copy in near:
         copy.wait_recv()
     both = mine[...]
@@ -952,6 +994,10 @@
     for copy in far:
         copy.start()
     host.next()
+    host.chains[0].wait()
+    settles[2].go()
+    host.end()
+    settles[1].go()
     for copy in far:
         copy.wait_recv()
     both = summed[...]
@@ -960,31 +1006,30 @@
     sums[...] = both
     for deal in deals:
         deal.end()
-    host.end()
     for settle in settles:
         settle.wait()
     wire.finish()
 
 
-def last_sums(low, wa, x_all, mid_grad, gain, vec2, g2, got2, out_g, gout, qkv_g, zn):
+def last_sums(low, wa, x_all, mid_grad, gain, vec2, g2, got2, out_g, qkv_g, zn):
     micro, _, tok, width = x_all.shape
     sub = tok // 4
     dz, cols = width // zn, low.shape[1]
-    jobs = Jobs([(qkv_g, None, 0, zn - 1)], zn)
-    count = (REDUCE + 3) * micro + 7 + zn - 1 + 2 * jobs.steps + 3
+    jobs = Jobs([(qkv_g, (0, 1), ()), (out_g, (0, 1), ())], zn)
+    count = (REDUCE + 3) * micro + 7 + zn - 1 + jobs.links + 3
     size = vec2.shape
     rows = pltpu.VMEM((micro, sub, width), BF)
     sizes = (g2.shape[1], out_g.shape[1], cols)
     halves = [shaped((dz // 2, k)) for k in sizes for _ in range(2)]
     return kernel(
-        functools.partial(last_kernel, jobs, zn),
-        (low, wa, x_all, mid_grad, gain, vec2, g2, *got2, out_g, *gout, *jobs.ins),
-        [VMEM, ANY, ANY, VMEM, VMEM, VMEM] + [ANY] * (6 + len(jobs.ins)),
+        functools.partial(last_kernel, jobs, zn, len(got2)),
+        (low, wa, x_all, mid_grad, gain, vec2, g2, *got2, *jobs.ins),
+        [VMEM, ANY, ANY, VMEM, VMEM, VMEM] + [ANY] * (1 + len(got2) + len(jobs.ins)),
         (shaped((micro, tok, width // 4)), shaped(size, F32), *halves, *jobs.outs),
         (ANY, VMEM) + (ANY,) * (6 + len(jobs.outs)), 100, "last_sums",
         reduce_scratch(micro, tok, sub, width) + [rows] * 2 + [pltpu.VMEM((zn, dz, cols), BF)]
         + [pltpu.VMEM(size, F32), pltpu.VMEM((7,) + size, F32), pltpu.VMEM(size, F32), pltpu.VMEM((zn - 1,) + size, F32)]
-        + [pltpu.VMEM((3, dz, k), BF) for k in sizes] + sems(4, 4, 4, count, count, 2 * micro + 1) + jobs.scratch,
+        + [pltpu.VMEM((zn, dz, k), BF) for k in sizes] + sems(zn + 1, zn + 1, zn + 1, count, count, 2 * micro + 1) + jobs.scratch,
         talk=3,
     )
 
@@ -1078,13 +1123,15 @@
         low[:, 2 * span + lo : 2 * span + lo + HEAD_DIM] = vg.astype(BF)
 
 
-def attention_back_kernel(jobs, count, parts, *refs):
-    lens, branch, att, wa, qkv, cos, sin, n1, g0, got0, got1, g1, got2, got3, pair, last, middle, *refs = refs
+def attention_back_kernel(jobs, count, parts, marks, *refs):
+    lens, branch, att, wa, qkv, cos, sin, n1, *refs = refs
+    n0, n1s = marks
+    g0, came0, g1, came1, refs = refs[0], refs[1 : 1 + n0], refs[1 + n0], refs[2 + n0 : 2 + n0 + n1s], refs[2 + n0 + n1s :]
+    pair, last, middle, *refs = refs
     hids, zin, refs = refs[:parts], refs[parts:][: len(jobs.ins)], refs[parts + len(jobs.ins) :]
     low, grads, out_g, *refs = refs
     settled, layer_out, refs = refs[:4], refs[4], refs[5:]
     zout, refs = refs[: len(jobs.outs)], refs[len(jobs.outs) :]
-    zout, gout = zout[: -2 * (jobs.zn - 1)], zout[-2 * (jobs.zn - 1) :]
     red, refs = refs[:8], refs[8:]
     bv, wo, ob, yb, load, yl, ls, ss, rs, *talk = refs
     rows, width = bv.shape
@@ -1117,12 +1164,13 @@
         bring(b)[0].start()
     meet(z_partners(zn) + [at.sib, at.xn, at.yn, at.xs])
     wire = Wire(ss, rs)
-    host = Host(wire, zn, [(zin[0], None, 0, zout), (out_g, None, 0, gout)], *talk)
+    host = jobs.host(wire, zin, zout, talk)
+    split = len(chain_results(zn, (0,), 8, 128))
     settles = [
-        Settle(wire, at, zn, g0, (got0, got1), settled[0], settled[1], yb, yl),
-        Settle(wire, at, zn, g1, (got2, got3), settled[2], settled[3], yb, yl),
+        Settle(wire, at, zn, g0, came0[:split], came0[split:], settled[0], settled[1], yb, yl),
+        Settle(wire, at, zn, g1, came1[:split], came1[split:], settled[2], settled[3], yb, yl),
     ]
-    host.begin((0,))
+    host.begin()
     for copy in downs:
         copy.wait()
     lows = [low.at[:, pl.ds(k * one, one)] for k in range(parts)]
@@ -1132,19 +1180,9 @@
         total.diagonal(m)
     settles[0].go()
     weights.wait()
-    for b in range(4):
+
+    def block(b):
         bring(b)[0].wait()
-
-    def output(k, carry):
-        here = pl.ds(pl.multiple_of(k * dz, dz), dz)
-        out_g[here, :] = dot_tn(bv[:, here], att[...]).astype(BF)
-        return carry
-
-    lax.fori_loop(0, zn, output, 0)
-    host.begin((1,))
-    host.next()
-
-    def block(b):
         here = pl.ds(b * tok, tok)
         attention_back_body(
             count, lens, b, bv.at[here], wo, qkv.at[here], cos.at[here], sin.at[here], low.at[here]
@@ -1154,15 +1192,14 @@
     for m in range(micro):
         total.sides(m)
         total.release(m)
+    host.next()
     for b in range(4):
         bring(b)[1].start()
     block(1)
     settles[0].wait()
     settles[1].go()
-    host.next()
     block(2)
     block(3)
-    host.next()
     for b in range(4):
         bring(b)[1].wait()
 
@@ -1172,6 +1209,7 @@
         for b in range(4):
             acc = acc + dot_tn(red[0][b // 2, b % 2, :, here], low[pl.ds(b * tok, tok), :])
         grads[k] = acc.astype(BF)
+        out_g[here, :] = dot_tn(bv[:, here], att[...]).astype(BF)
         return carry
 
     lax.fori_loop(0, zn, weights_of, 0)
@@ -1182,7 +1220,6 @@
             ob[m, lo : lo + step, :] = (middle[m, lo : lo + step, :] + total.total(m, lo, step)).astype(BF)
         deals.append(Deal(wire, at, ob, layer_out, m, ls, m))
         deals[-1].begin()
-    host.next()
     settles[1].wait()
     for deal in deals:
         deal.end()
@@ -1197,20 +1234,19 @@
     tok = rows // 4
     dz = width // zn
     out_g = shaped((width, span))
-    jobs = Jobs([(g2, None, 0, zn - 1), (out_g, None, 0, zn - 1)], zn)
-    jobs.ins = [g2]
+    jobs = Jobs([(g2, (0, 1), ())], zn)
     half = shaped((dz // 2, g0.shape[1]))
-    links = 2 * jobs.steps + 2 + (REDUCE + 3) * micro
+    links = jobs.links + 2 + (REDUCE + 3) * micro
     return kernel(
-        functools.partial(attention_back_kernel, jobs, count, parts),
+        functools.partial(attention_back_kernel, jobs, count, parts, (len(got0), len(got1))),
         (lens, branch, att, wa, qkv, cos, sin, n1, g0, *got0, g1, *got1, pair, last, middle, *hids, *jobs.ins),
-        [SMEM, ANY, VMEM, ANY, VMEM, VMEM, VMEM, ANY] + [ANY] * 8 + [VMEM] + [ANY] * (parts + len(jobs.ins)),
+        [SMEM, ANY, VMEM, ANY, VMEM, VMEM, VMEM, ANY] + [ANY] * (4 + len(got0) + len(got1)) + [VMEM] + [ANY] * (parts + len(jobs.ins)),
         (shaped((rows, cols)), shaped((zn, dz, cols)), out_g, *(half,) * 4, shaped((micro, tok, width // 4)), *jobs.outs),
         (VMEM, VMEM, VMEM) + (ANY,) * (5 + len(jobs.outs)), 70, "attention_back",
         reduce_scratch(micro, tok, sub, width)
         + [pltpu.VMEM((rows, width), BF), pltpu.VMEM((zn, dz, span), BF), pltpu.VMEM((micro, sub, width), BF)]
-        + [pltpu.VMEM((3, dz, g0.shape[1]), BF)]
-        + sems(9 + 2 * parts, 4, micro, links, links) + jobs.scratch,
+        + settle_scratch(zn, dz, g0.shape[1])[:1]
+        + sems(9 + 2 * parts, zn + 1, micro, links, links) + jobs.scratch,
         talk=9,
     )
 
@@ -1269,7 +1305,7 @@
         return carry
 
     lax.fori_loop(0, zn, weights, 0)
-    if jobs.steps:
+    if jobs.links:
         host.end()
 
 
@@ -1283,8 +1319,8 @@
         (shaped((rows, 2 * one)), shaped((rows, one)), shaped((width, cols)), *jobs.outs),
         (VMEM,) * 3 + (ANY,) * len(jobs.outs), 22, "ffn_chunk",
         [pltpu.VMEM((rows, width), BF)] * 2 + [pltpu.VMEM((zn, width // zn, cols), BF), pltpu.SemaphoreType.DMA((2, 5))]
-        + (sems(2 * jobs.steps, 2 * jobs.steps) + jobs.scratch if jobs.steps else []),
-        first, talk=talk if jobs.steps else None,
+        + (sems(jobs.links, jobs.links) + jobs.scratch if jobs.links else []),
+        first, talk=talk if jobs.links else None,
     )
 
 
@@ -1368,18 +1404,19 @@
 
     low0, hid0, g0 = chunk(n2, dy, w_01, 0, own_mask(0), [], zn, None, ())
     low1, hid1, grad1 = chunk(n2, dy, w_01, 1, own_mask(1), [], zn, None, (g0,))
-    low2, hid2, grad2, *p = chunk(n2, dy, w_2, None, own_mask(2), [(g0, None, 0, 1)], zn, 7, (grad1,))
+    low2, hid2, grad2, *p = chunk(n2, dy, w_2, None, own_mask(2), [(g0, (0,), ())], zn, 7, (grad1,))
     mid_grad, branch, vec2, *q = ffn_back(
-        [low0, low1, low2], w_01, w_2, d_all, middle, gain2, [(g0, p, 1, zn - 2), (grad1, None, 0, zn - 1)], zn, ()
-    )
-    got0, got1 = q[2 * zn - 6 : 2 * zn - 4], q[-2:]
+        [low0, low1, low2], w_01, w_2, d_all, middle, gain2, [(grad1, (0, 1), ()), (g0, (1,), p)], zn, ()
+    )
+    many = len(chain_results(zn, (0, 1), 8, 128))
+    got1, got0 = q[:many], p + q[many:]
     branch = branch.reshape(rows, width)
     low, qkv_g, out_g, *r = attention_back(
         count, lens, branch, att, wa, qkv, cos, sin, n1, g0, got0, grad1, got1, w_01, w_2, middle, [hid0, hid1, hid2], grad2, zn
     )
-    first, layer_out, got2, gout = r[:4], r[4], r[2 * zn + 1 : 2 * zn + 3], r[-2:]
+    first, layer_out, got2 = r[:4], r[4], r[5:]
     in_grad, sums, *r = last_sums(
-        low, wa, x_all, mid_grad, gain1, vec2, grad2, got2, out_g, gout, qkv_g.reshape(width, -1), zn
+        low, wa, x_all, mid_grad, gain1, vec2, grad2, got2, out_g, qkv_g.reshape(width, -1), zn
     )
     gu_grad, down_grad, qkv_grad, out_grad = form(
         [*first, *r[:6]], w_gu, w_down, w_qkv, w_out

time: 598 us -> 577 us (0.965)
  Pallas kernels: 554 us -> 536 us
    pallas_call x12, Pallas kernels: 554 us -> 536 us  [kernel(): pl.pallas_call(without(body, len(ins), extra), grid=grid, in_specs=list(i...]
  transfers between devices with their start and end apart: 3 -> 3, of which waited for: 1 -> 1; matrix products, arithmetic and copies ran while one was open for 1% -> 1% of each run, Pallas kernels for 41% -> 42%
where the time goes in v4:
time: 577 us; the launch traced here: 574 us
  Pallas kernels  536 us (93%)
  waiting for transfers between devices  15.3 us (3%)
  between operations  14.3 us (2%)
  local copies, waits for them, and re-layouts  6.33 us (1%)
    pallas_call x12, Pallas kernels, kernel(): pl.pallas_call(without(body, len(ins), extra), grid=grid, in_specs=list(i...  536 us
    all_gather x3, waiting for transfers between devices, gather_z(): return lax.all_gather(w, 'z', axis=0, tiled=False)  15.2 us
  transfers between devices with their start and end apart: 3, of which 1 were waited for; matrix products, arithmetic and copies ran while one was open for 1% of the time, Pallas kernels for 42%

profile of v4, /device:TPU:0, one launch (start us, length us, event | category | flops | bytes accessed | tf_op | source)
XLA Modules:
  0.0 574.4 jit_solution(7509301668995849307)
XLA Ops:
  7.2 0.0 copy-start.3
  7.2 0.0 copy-start.4
  7.2 0.0 copy-start.5
  7.2 0.0 copy-start.6
  7.2 0.0 copy-start.2
  7.2 0.0 all-gather.7.cloned.1.call-start
  7.3 16.3 %swap_attn.1.refs_6_ = bf16[512,1024]{1,0:T(8,128)(2,1)} custom-call(bf16[3,256,512]{2,1,0:T(8,128)(2,1)} %refs_0_.3, bf16[512,256]{1,0:T(8,128)(2,1)} %refs_1_.1), custom_call_target="tpu_custom_call" | custom-call | flops 14000000000 | bytes 44800000 | tf_op jit(solution)/shard_map/swap_attn/pallas_call | solution.py:61
  23.6 0.0 all-gather.7.cloned.1.call-update
  23.6 0.0 all-gather.9.cloned.1.call-start
  23.7 0.0 copy-done.3
  23.7 0.0 copy-done.4
  23.7 0.0 copy-done.5
  23.7 0.0 copy-done.6
  23.8 0.0 copy-done.2
  23.8 0.6 pad.12.refs_2_
  24.4 0.5 fusion.11.refs_3_
  24.9 0.6 fusion.7.refs_1_
  25.5 0.0 copy-start.7
  25.5 53.6 %gather_x.1 = (bf16[2,2,512,2048]{3,2,1,0:T(8,128)(2,1)}, f32[4,2,8,256]{3,2,1,0:T(8,128)}, s32[2,8,128]{2,1,0:T(8,128)}, f32[2048,128]{1,0:T(8,128)}, f32[2048,...) custom-call(bf16[2,512,512]{2,1,0:T(8,128)(2,1)} %refs_0_.4, f32[8,256]{1,0:T(8,128)} %fusion.7.refs_1_, s32[8,128]{1,0:T(8,128)} %pad.12.refs_2_, ...), custom_call_target="tpu_custom_call" | custom-call | flops 48000000000 | bytes 153600000 | tf_op jit(solution)/shard_map/gather_x/pallas_call | solution.py:61
  79.1 0.0 all-gather.9.cloned.1.call-update
  79.1 0.2 all-gather.11.cloned.1.call-start
  79.4 0.0 copy-done.7
  79.4 0.6 fusion.12
  80.0 0.7 compare_convert_fusion
  80.7 0.6 fusion.15
  81.2 1.7 fusion.14
  82.9 46.2 %gather_d.1 = (bf16[2,2,512,2048]{3,2,1,0:T(8,128)(2,1)}, bf16[2048,2048]{1,0:T(8,128)(2,1)}, bf16[512,768]{1,0:T(8,128)(2,1)}) custom-call(bf16[2,512,512]{2,1,0:T(8,128)(2,1)} %refs_0_.5, bf16[2,2,512,2048]{3,2,1,0:T(8,128)(2,1)} %get-tuple-element.69.refs_1_.refs_2_, f32[1,2048]{1,0:T(1,128)} %bitcast.18, f32[1,2048]{1,0:T(1,128)} %bitcast.23, ...), custom_call_target="tpu_custom_call" | custom-call | flops 48000000000 | bytes 153600000 | tf_op jit(solution)/shard_map/gather_d/pallas_call | solution.py:61
  129.1 0.0 all-gather.7.cloned.1.call-done
  129.1 19.1 %attention.1 = (bf16[2048,768]{1,0:T(8,128)(2,1)}, bf16[2048,256]{1,0:T(8,128)(2,1)}, bf16[512,768]{1,0:T(8,128)(2,1)}) custom-call(s32[2,8,128]{2,1,0:T(8,128)} %get-tuple-element.68.refs_0_, bf16[2048,2048]{1,0:T(8,128)(2,1)} %get-tuple-element.71.refs_1_.refs_7_, bf16[4,512,1024]{2,1,0:T(8,128)(2,1)} %bitcast.33, ...), custom_call_target="tpu_custom_call", output_to_operand_aliasing={{2}: (5, {})} | custom-call | flops 20000000000 | bytes 64000000 | tf_op jit(solution)/shard_map/attention/pallas_call | solution.py:61
  148.2 0.0 all-gather.11.cloned.1.call-update
  148.2 79.9 %attn_out.1 = (f32[2,128,2048]{2,1,0:T(8,128)}, bf16[2,2,4,128,2048]{4,3,2,1,0:T(8,128)(2,1)}) custom-call(bf16[2048,256]{1,0:T(8,128)(2,1)} %get-tuple-element.75.refs_0_.refs_2_, bf16[4,512,1024]{2,1,0:T(8,128)(2,1)} %bitcast.34, bf16[2,2,512,2048]{3,2,1,0:T(8,128)(2,1)} %get-tuple-element.69.refs_1_.refs_2_, f32[1,2048]{1,0:T(1,128)} %bitcast.20, ...), custom_call_target="tpu_custom_call" | custom-call | flops 85000003584 | bytes 272000000 | tf_op jit(solution)/shard_map/attn_out/pallas_call | solution.py:61
  228.1 0.0 all-gather.9.cloned.1.call-done
  228.1 21.0 %ffn_chunk.3 = (bf16[2048,512]{1,0:T(8,128)(2,1)}, bf16[2048,256]{1,0:T(8,128)(2,1)}, bf16[2048,768]{1,0:T(8,128)(2,1)}) custom-call(bf16[2048,2048]{1,0:T(8,128)(2,1)} %bitcast.44, bf16[2048,2048]{1,0:T(8,128)(2,1)} %bitcast.40, bf16[4,2,512,768]{3,2,1,0:T(8,128)(2,1)} %bitcast.29, f32[1,256]{1,0:T(1,128)} %get-tuple-element.136.refs_3_), custom_call_target="tpu_custom_call" | custom-call | flops 22000001024 | bytes 70400000 | tf_op jit(solution)/shard_map/ffn_chunk/pallas_call | solution.py:61
  249.1 20.5 %ffn_chunk.4 = (bf16[2048,512]{1,0:T(8,128)(2,1)}, bf16[2048,256]{1,0:T(8,128)(2,1)}, bf16[2048,768]{1,0:T(8,128)(2,1)}) custom-call(bf16[2048,2048]{1,0:T(8,128)(2,1)} %bitcast.45, bf16[2048,2048]{1,0:T(8,128)(2,1)} %bitcast.41, bf16[4,2,512,768]{3,2,1,0:T(8,128)(2,1)} %bitcast.30, f32[1,256]{1,0:T(1,128)} %get-tuple-element.135.refs_3_, ...), custom_call_target="tpu_custom_call" | custom-call | flops 22000001024 | bytes 70400000 | tf_op jit(solution)/shard_map/ffn_chunk/pallas_call | solution.py:61
  269.7 15.2 %all-gather.11.cloned.1.call-done = bf16[2048,768]{1,0:T(8,128)(2,1)} async-done(((bf16[512,768]{1,0:T(8,128)(2,1)}), bf16[2048,768]{1,0:T(8,128)(2,1)}) %all-gather.11.cloned.1.call-update) | async-done | bytes 3145744 | tf_op jit(solution)/shard_map/all_gather | solution.py:1377
  284.9 23.2 %ffn_chunk.5 = (bf16[2048,512]{1,0:T(8,128)(2,1)}, bf16[2048,256]{1,0:T(8,128)(2,1)}, bf16[2048,768]{1,0:T(8,128)(2,1)}, bf16[512,768]{1,0:T(8,128)(2,1)}, bf16[512,768]{1,0:T(8,128)(2,1)}) custom-call(bf16[2048,2048]{1,0:T(8,128)(2,1)} %bitcast.46, bf16[2048,2048]{1,0:T(8,128)(2,1)} %bitcast.42, bf16[4,512,768]{2,1,0:T(8,128)(2,1)} %bitcast.37, ...), custom_call_target="tpu_custom_call" | custom-call | flops 22000001024 | bytes 70400000 | tf_op jit(solution)/shard_map/ffn_chunk/pallas_call | solution.py:61
  308.0 94.4 %ffn_back.1 = (f32[2,128,2048]{2,1,0:T(8,128)}, bf16[2,2,4,128,2048]{4,3,2,1,0:T(8,128)(2,1)}, f32[8,2048]{1,0:T(8,128)}, bf16[512,768]{1,0:T(8,128)(2,1)}, bf16...) custom-call(bf16[2048,512]{1,0:T(8,128)(2,1)} %get-tuple-element.79., ...), custom_call_target="tpu_custom_call" | custom-call | flops 89999998976 | bytes 288000000 | tf_op jit(solution)/shard_map/ffn_back/pallas_call | solution.py:61
  402.4 67.5 %attention_back.1 = (bf16[2048,768]{1,0:T(8,128)(2,1)}, bf16[4,512,768]{2,1,0:T(8,128)(2,1)}, bf16[2048,256]{1,0:T(8,128)(2,1)}, bf16[256,768]{1,0:T(8,128)(2,1)...) custom-call(s32[2,8,128]{2,1,0:T(8,128)} %get-tuple-element.68.refs_, ...), custom_call_target="tpu_custom_call" | custom-call | flops 70000001024 | bytes 224000000 | tf_op jit(solution)/shard_map/attention_back/pallas_call | solution.py:61
  469.9 88.9 %last_sums.1 = (bf16[2,512,512]{2,1,0:T(8,128)(2,1)}, f32[8,2048]{1,0:T(8,128)}, bf16[256,768]{1,0:T(8,128)(2,1)}, bf16[256,768]{1,0:T(8,128)(2,1)}, bf16[256,25...) custom-call(bf16[2048,768]{1,0:T(8,128)(2,1)} %get-tuple-element.101, ...), custom_call_target="tpu_custom_call" | custom-call | flops 99999997952 | bytes 320000000 | tf_op jit(solution)/shard_map/last_sums/pallas_call | solution.py:61
  558.9 1.5 fusion.13
  560.4 0.0 copy-start
  560.4 0.0 copy-start.1
  560.4 5.3 form.1
  565.6 0.0 copy-done
  565.6 1.0 copy.26
  566.6 0.0 copy-done.1
  566.6 1.0 copy.27
  (4 shorter events, 0.0 us)
Async XLA Ops:
  7.2 16.5 %copy-start.3 = (bf16[256]{0:T(256)(128)(2,1)S(1)}, bf16[256]{0:T(256)(128)(2,1)}, u32[]{:S(2)}) copy-start(bf16[256]{0:T(256)(128)(2,1)} %param.19) | copy-start | bytes 1540
  7.2 16.5 %copy-start.4 = (bf16[256]{0:T(256)(128)(2,1)S(1)}, bf16[256]{0:T(256)(128)(2,1)}, u32[]{:S(2)}) copy-start(bf16[256]{0:T(256)(128)(2,1)} %param.20) | copy-start | bytes 1540
  7.2 16.5 %copy-start.5 = (bf16[256]{0:T(256)(128)(2,1)S(1)}, bf16[256]{0:T(256)(128)(2,1)}, u32[]{:S(2)}) copy-start(bf16[256]{0:T(256)(128)(2,1)} %param.21) | copy-start | bytes 1540
  7.2 16.5 %copy-start.6 = (bf16[256]{0:T(256)(128)(2,1)S(1)}, bf16[256]{0:T(256)(128)(2,1)}, u32[]{:S(2)}) copy-start(bf16[256]{0:T(256)(128)(2,1)} %param.22) | copy-start | bytes 1540
  7.2 16.5 %copy-start.2 = (s32[2,1,4]{2,1,0:T(1,128)S(1)}, s32[2,1,4]{2,1,0:T(1,128)}, u32[]{:S(2)}) copy-start(s32[2,1,4]{2,1,0:T(1,128)} %param.13) | copy-start | bytes 100
  7.2 121.9 %all-gather.7.cloned.1.call-start = ((), (), s32[]{:S(2)}) async-start(), calls=%async_computation | async-start | bytes 5242880 | tf_op jit(solution)/shard_map/all_gather | solution.py:1377
  23.6 204.5 %all-gather.9.cloned.1.call-start = ((), (), s32[]{:S(2)}) async-start(), calls=%async_computation.1 | async-start | bytes 7864320 | tf_op jit(solution)/shard_map/all_gather | solution.py:1377
  25.5 53.9 %copy-start.7 = (s32[4]{0:T(128)S(1)}, s32[4]{0:T(128)}, u32[]{:S(2)}) copy-start(s32[4]{0:T(128)} %param.14) | copy-start | bytes 52
  79.1 205.7 %all-gather.11.cloned.1.call-start = ((), (), s32[]{:S(2)}) async-start(), calls=%async_computation.2 | async-start | bytes 3932160 | tf_op jit(solution)/shard_map/all_gather | solution.py:1377
  560.4 5.3 copy-start
  560.4 6.2 %copy-start.1 = (bf16[2,512,512]{2,1,0:T(8,128)(2,1)S(1)}, bf16[2,512,512]{2,1,0:T(8,128)(2,1)}, u32[]{:S(2)}) copy-start(bf16[2,512,512]{2,1,0:T(8,128)(2,1)} %get-tuple-element.148) | copy-start | bytes 3145732
Sparse Core Ops, SparseCore 0:
  23.7 82.2 all-gather.6
  107.6 113.8 all-gather.8
  223.1 61.7 all-gather.10

commit v5 on v4

--- a/solution.py
+++ b/solution.py
@@ -56,15 +56,41 @@
     return run
 
 
-def kernel(body, ins, in_specs, outs, out_specs, us, name, scratch=(), first=(), grid=(), talk=None, aliases=None):
+def staged_body(body, ins, staged):
+    def run(*refs):
+        bufs, sem = refs[-len(staged) - 1 : -1], refs[-1]
+        refs = list(refs[: -len(staged) - 1])
+        copies = []
+        for k, i in enumerate(staged):
+            copies.append(pltpu.make_async_copy(refs[i], bufs[k], sem.at[k]))
+            copies[-1].start()
+            refs[i] = bufs[k]
+
+        def ready():
+            for copy in copies:
+                copy.wait()
+
+        return body(ready, *refs)
+
+    return run
+
+
+def kernel(body, ins, in_specs, outs, out_specs, us, name, scratch=(), first=(), grid=(), talk=None, aliases=None, staged=()):
     extra = len(first)
+    in_specs, scratch = list(in_specs), list(scratch)
+    if staged:
+        body = staged_body(body, len(ins), staged)
+        for i in staged:
+            in_specs[i] = ANY
+            scratch.append(pltpu.VMEM(ins[i].shape, ins[i].dtype))
+        scratch += sems(len(staged))
     return pl.pallas_call(
         without(body, len(ins), extra),
         grid=grid,
-        in_specs=list(in_specs) + [ANY] * extra,
+        in_specs=in_specs + [ANY] * extra,
         out_specs=out_specs,
         out_shape=outs,
-        scratch_shapes=list(scratch),
+        scratch_shapes=scratch,
         input_output_aliases=aliases or {},
         compiler_params=pltpu.CompilerParams(
             vmem_limit_bytes=VMEM_BYTES, collective_id=talk, has_side_effects=talk is not None
@@ -821,7 +847,7 @@
     return [pair.at[:, k] for k in range(pair.shape[1])] + [last]
 
 
-def ffn_back_kernel(jobs, parts, *refs):
+def ffn_back_kernel(jobs, parts, ready, *refs):
     guls = refs[:parts]
     pair, last, d_all, middle, gain, *refs = refs[parts:]
     zin, (mid_grad, branch, vec), refs = refs[: len(jobs.ins)], refs[len(jobs.ins) :][:3], refs[len(jobs.ins) + 3 :]
@@ -859,6 +885,7 @@
         local[-1].start()
 
     weights.wait()
+    ready()
     reduce_rows(wire, at, red, nt_compute(red[0], guls, [wv.at[k] for k in range(parts)], 0), finish, host.next)
     run_spreads(spreads, local, host.next)
     host.end()
@@ -879,7 +906,7 @@
         (VMEM, ANY, VMEM) + (ANY,) * len(jobs.outs), 90, "ffn_back",
         reduce_scratch(micro, tok, sub, width) + [pltpu.VMEM((micro, sub, width), BF)] * 2
         + [pltpu.VMEM((parts, zn, width // zn, span), BF)] + sems(count, count, 2 * micro, parts) + jobs.scratch,
-        first, talk=2,
+        first, talk=2, staged=(*range(parts), parts + 3),
     )
 
 
@@ -926,7 +953,7 @@
         self.local.wait()
 
 
-def last_kernel(jobs, zn, marks, *refs):
+def last_kernel(jobs, zn, marks, ready, *refs):
     low, wa, x_all, mid_grad, gain, vec2, *refs = refs
     g2, came2, refs = refs[0], refs[1 : 1 + marks], refs[1 + marks :]
     zin, refs = refs[: len(jobs.ins)], refs[len(jobs.ins) :]
@@ -952,12 +979,13 @@
     split = len(chain_results(zn, (0,), 8, 128))
     settles = [
         Settle(wire, at, zn, g2, came2[:split], came2[split:], settled[0], settled[1], yb2, yl2),
-        Settle(wire, at, zn, zin[1], zout[marks : marks + split], zout[marks + split :], settled[2], settled[3], ybo, ylo),
+        Settle(wire, at, zn, zin[1], zin[2:], zout[marks:], settled[2], settled[3], ybo, ylo),
         Settle(wire, at, zn, zin[0], zout[:split], zout[split:marks], settled[4], settled[5], ybq, ylq),
     ]
     mine[...] = jnp.zeros_like(mine)
     mine[2:4] = vec2[0:2]
     qkv.wait()
+    ready()
     total = Reduce(wire, at, red, nt_compute(red[0], [low], [w1], 0))
     for m in range(micro):
         total.cores(m)
@@ -1011,11 +1039,11 @@
     wire.finish()
 
 
-def last_sums(low, wa, x_all, mid_grad, gain, vec2, g2, got2, out_g, qkv_g, zn):
+def last_sums(low, wa, x_all, mid_grad, gain, vec2, g2, got2, out_g, gout, qkv_g, zn):
     micro, _, tok, width = x_all.shape
     sub = tok // 4
     dz, cols = width // zn, low.shape[1]
-    jobs = Jobs([(qkv_g, (0, 1), ()), (out_g, (0, 1), ())], zn)
+    jobs = Jobs([(qkv_g, (0, 1), ()), (out_g, (1,), gout)], zn)
     count = (REDUCE + 3) * micro + 7 + zn - 1 + jobs.links + 3
     size = vec2.shape
     rows = pltpu.VMEM((micro, sub, width), BF)
@@ -1030,7 +1058,7 @@
         reduce_scratch(micro, tok, sub, width) + [rows] * 2 + [pltpu.VMEM((zn, dz, cols), BF)]
         + [pltpu.VMEM(size, F32), pltpu.VMEM((7,) + size, F32), pltpu.VMEM(size, F32), pltpu.VMEM((zn - 1,) + size, F32)]
         + [pltpu.VMEM((zn, dz, k), BF) for k in sizes] + sems(zn + 1, zn + 1, zn + 1, count, count, 2 * micro + 1) + jobs.scratch,
-        talk=3,
+        talk=3, staged=(0, 3),
     )
 
 
@@ -1123,7 +1151,7 @@
         low[:, 2 * span + lo : 2 * span + lo + HEAD_DIM] = vg.astype(BF)
 
 
-def attention_back_kernel(jobs, count, parts, marks, *refs):
+def attention_back_kernel(jobs, count, parts, marks, ready, *refs):
     lens, branch, att, wa, qkv, cos, sin, n1, *refs = refs
     n0, n1s = marks
     g0, came0, g1, came1, refs = refs[0], refs[1 : 1 + n0], refs[1 + n0], refs[2 + n0 : 2 + n0 + n1s], refs[2 + n0 + n1s :]
@@ -1164,13 +1192,13 @@
         bring(b)[0].start()
     meet(z_partners(zn) + [at.sib, at.xn, at.yn, at.xs])
     wire = Wire(ss, rs)
-    host = jobs.host(wire, zin, zout, talk)
+    host = jobs.host(wire, [zin[0], out_g], zout, talk)
     split = len(chain_results(zn, (0,), 8, 128))
     settles = [
         Settle(wire, at, zn, g0, came0[:split], came0[split:], settled[0], settled[1], yb, yl),
         Settle(wire, at, zn, g1, came1[:split], came1[split:], settled[2], settled[3], yb, yl),
     ]
-    host.begin()
+    host.begin(0)
     for copy in downs:
         copy.wait()
     lows = [low.at[:, pl.ds(k * one, one)] for k in range(parts)]
@@ -1180,9 +1208,11 @@
         total.diagonal(m)
     settles[0].go()
     weights.wait()
+    ready()
 
     def block(b):
-        bring(b)[0].wait()
+        if b < 2:
+            bring(b)[0].wait()
         here = pl.ds(b * tok, tok)
         attention_back_body(
             count, lens, b, bv.at[here], wo, qkv.at[here], cos.at[here], sin.at[here], low.at[here]
@@ -1198,6 +1228,16 @@
     block(1)
     settles[0].wait()
     settles[1].go()
+    for b in (2, 3):
+        bring(b)[0].wait()
+
+    def output(k, carry):
+        here = pl.ds(pl.multiple_of(k * dz, dz), dz)
+        out_g[here, :] = dot_tn(bv[:, here], att[...]).astype(BF)
+        return carry
+
+    lax.fori_loop(0, zn, output, 0)
+    host.begin(1)
     block(2)
     block(3)
     for b in range(4):
@@ -1209,7 +1249,6 @@
         for b in range(4):
             acc = acc + dot_tn(red[0][b // 2, b % 2, :, here], low[pl.ds(b * tok, tok), :])
         grads[k] = acc.astype(BF)
-        out_g[here, :] = dot_tn(bv[:, here], att[...]).astype(BF)
         return carry
 
     lax.fori_loop(0, zn, weights_of, 0)
@@ -1234,7 +1273,8 @@
     tok = rows // 4
     dz = width // zn
     out_g = shaped((width, span))
-    jobs = Jobs([(g2, (0, 1), ())], zn)
+    jobs = Jobs([(g2, (0, 1), ()), (out_g, (0,), ())], zn)
+    jobs.ins = [g2]
     half = shaped((dz // 2, g0.shape[1]))
     links = jobs.links + 2 + (REDUCE + 3) * micro
     return kernel(
@@ -1247,7 +1287,7 @@
         + [pltpu.VMEM((rows, width), BF), pltpu.VMEM((zn, dz, span), BF), pltpu.VMEM((micro, sub, width), BF)]
         + settle_scratch(zn, dz, g0.shape[1])[:1]
         + sems(9 + 2 * parts, zn + 1, micro, links, links) + jobs.scratch,
-        talk=9,
+        talk=9, staged=(2, 4, 5, 6, 12 + len(got0) + len(got1)),
     )
 
 
@@ -1414,9 +1454,9 @@
     low, qkv_g, out_g, *r = attention_back(
         count, lens, branch, att, wa, qkv, cos, sin, n1, g0, got0, grad1, got1, w_01, w_2, middle, [hid0, hid1, hid2], grad2, zn
     )
-    first, layer_out, got2 = r[:4], r[4], r[5:]
+    first, layer_out, got2, gout = r[:4], r[4], r[5 : 5 + many], r[5 + many :]
     in_grad, sums, *r = last_sums(
-        low, wa, x_all, mid_grad, gain1, vec2, grad2, got2, out_g, qkv_g.reshape(width, -1), zn
+        low, wa, x_all, mid_grad, gain1, vec2, grad2, got2, out_g, gout, qkv_g.reshape(width, -1), zn
     )
     gu_grad, down_grad, qkv_grad, out_grad = form(
         [*first, *r[:6]], w_gu, w_down, w_qkv, w_out

time: 577 us -> 568 us (0.984)
  Pallas kernels: 536 us -> 527 us
    pallas_call x12, Pallas kernels: 536 us -> 527 us  [kernel(): pl.pallas_call(without(body, len(ins), extra), grid=grid, in_specs=in_spe...]
  transfers between devices with their start and end apart: 3 -> 3, of which waited for: 1 -> 1; matrix products, arithmetic and copies ran while one was open for 1% -> 1% of each run, Pallas kernels for 42% -> 43%
where the time goes in v5:
time: 568 us; the launch traced here: 565 us
  Pallas kernels  527 us (93%)
  waiting for transfers between devices  15.3 us (3%)
  between operations  14.3 us (3%)
  local copies, waits for them, and re-layouts  6.33 us (1%)
    pallas_call x12, Pallas kernels, kernel(): pl.pallas_call(without(body, len(ins), extra), grid=grid, in_specs=in_spe...  527 us
    all_gather x3, waiting for transfers between devices, gather_z(): return lax.all_gather(w, 'z', axis=0, tiled=False)  15.2 us
  transfers between devices with their start and end apart: 3, of which 1 were waited for; matrix products, arithmetic and copies ran while one was open for 1% of the time, Pallas kernels for 43%

profile of v5, /device:TPU:0, one launch (start us, length us, event | category | flops | bytes accessed | tf_op | source)
XLA Modules:
  0.0 565.1 jit_solution(6066366105576322876)
XLA Ops:
  7.2 0.0 copy-start.3
  7.2 0.0 copy-start.4
  7.2 0.0 copy-start.5
  7.2 0.0 copy-start.6
  7.2 0.0 copy-start.2
  7.2 0.0 all-gather.7.cloned.1.call-start
  7.3 16.3 %swap_attn.1.refs_6_ = bf16[512,1024]{1,0:T(8,128)(2,1)} custom-call(bf16[3,256,512]{2,1,0:T(8,128)(2,1)} %refs_0_.3, bf16[512,256]{1,0:T(8,128)(2,1)} %refs_1_.1), custom_call_target="tpu_custom_call" | custom-call | flops 14000000000 | bytes 44800000 | tf_op jit(solution)/shard_map/swap_attn/pallas_call | solution.py:87
  23.6 0.0 all-gather.7.cloned.1.call-update
  23.6 0.0 all-gather.9.cloned.1.call-start
  23.7 0.0 copy-done.3
  23.7 0.0 copy-done.4
  23.7 0.0 copy-done.5
  23.7 0.0 copy-done.6
  23.8 0.0 copy-done.2
  23.8 0.6 pad.12.refs_2_
  24.4 0.5 fusion.11.refs_3_
  24.9 0.6 fusion.7.refs_1_
  25.5 0.0 copy-start.7
  25.5 53.6 %gather_x.1 = (bf16[2,2,512,2048]{3,2,1,0:T(8,128)(2,1)}, f32[4,2,8,256]{3,2,1,0:T(8,128)}, s32[2,8,128]{2,1,0:T(8,128)}, f32[2048,128]{1,0:T(8,128)}, f32[2048,...) custom-call(bf16[2,512,512]{2,1,0:T(8,128)(2,1)} %refs_0_.4, f32[8,256]{1,0:T(8,128)} %fusion.7.refs_1_, s32[8,128]{1,0:T(8,128)} %pad.12.refs_2_, ...), custom_call_target="tpu_custom_call" | custom-call | flops 48000000000 | bytes 153600000 | tf_op jit(solution)/shard_map/gather_x/pallas_call | solution.py:87
  79.1 0.0 all-gather.9.cloned.1.call-update
  79.1 0.2 all-gather.11.cloned.1.call-start
  79.4 0.0 copy-done.7
  79.4 0.6 fusion.12
  80.0 0.7 compare_convert_fusion
  80.7 0.6 fusion.15
  81.2 1.7 fusion.14
  82.9 46.2 %gather_d.1 = (bf16[2,2,512,2048]{3,2,1,0:T(8,128)(2,1)}, bf16[2048,2048]{1,0:T(8,128)(2,1)}, bf16[512,768]{1,0:T(8,128)(2,1)}) custom-call(bf16[2,512,512]{2,1,0:T(8,128)(2,1)} %refs_0_.5, bf16[2,2,512,2048]{3,2,1,0:T(8,128)(2,1)} %get-tuple-element.71.refs_1_.refs_2_, f32[1,2048]{1,0:T(1,128)} %bitcast.18, f32[1,2048]{1,0:T(1,128)} %bitcast.23, ...), custom_call_target="tpu_custom_call" | custom-call | flops 48000000000 | bytes 153600000 | tf_op jit(solution)/shard_map/gather_d/pallas_call | solution.py:87
  129.1 0.0 all-gather.7.cloned.1.call-done
  129.1 19.1 %attention.1 = (bf16[2048,768]{1,0:T(8,128)(2,1)}, bf16[2048,256]{1,0:T(8,128)(2,1)}, bf16[512,768]{1,0:T(8,128)(2,1)}) custom-call(s32[2,8,128]{2,1,0:T(8,128)} %get-tuple-element.70.refs_0_, bf16[2048,2048]{1,0:T(8,128)(2,1)} %get-tuple-element.73.refs_1_.refs_7_, bf16[4,512,1024]{2,1,0:T(8,128)(2,1)} %bitcast.33, ...), custom_call_target="tpu_custom_call", output_to_operand_aliasing={{2}: (5, {})} | custom-call | flops 20000000000 | bytes 64000000 | tf_op jit(solution)/shard_map/attention/pallas_call | solution.py:87
  148.2 0.0 all-gather.11.cloned.1.call-update
  148.2 79.9 %attn_out.1 = (f32[2,128,2048]{2,1,0:T(8,128)}, bf16[2,2,4,128,2048]{4,3,2,1,0:T(8,128)(2,1)}) custom-call(bf16[2048,256]{1,0:T(8,128)(2,1)} %get-tuple-element.77.refs_0_.refs_2_, bf16[4,512,1024]{2,1,0:T(8,128)(2,1)} %bitcast.34, bf16[2,2,512,2048]{3,2,1,0:T(8,128)(2,1)} %get-tuple-element.71.refs_1_.refs_2_, f32[1,2048]{1,0:T(1,128)} %bitcast.20, ...), custom_call_target="tpu_custom_call" | custom-call | flops 85000003584 | bytes 272000000 | tf_op jit(solution)/shard_map/attn_out/pallas_call | solution.py:87
  228.1 0.0 all-gather.9.cloned.1.call-done
  228.1 21.0 %ffn_chunk.3 = (bf16[2048,512]{1,0:T(8,128)(2,1)}, bf16[2048,256]{1,0:T(8,128)(2,1)}, bf16[2048,768]{1,0:T(8,128)(2,1)}) custom-call(bf16[2048,2048]{1,0:T(8,128)(2,1)} %bitcast.44, bf16[2048,2048]{1,0:T(8,128)(2,1)} %bitcast.40, bf16[4,2,512,768]{3,2,1,0:T(8,128)(2,1)} %bitcast.29, f32[1,256]{1,0:T(1,128)} %get-tuple-element.140.refs_3_), custom_call_target="tpu_custom_call" | custom-call | flops 22000001024 | bytes 70400000 | tf_op jit(solution)/shard_map/ffn_chunk/pallas_call | solution.py:87
  249.1 20.5 %ffn_chunk.4 = (bf16[2048,512]{1,0:T(8,128)(2,1)}, bf16[2048,256]{1,0:T(8,128)(2,1)}, bf16[2048,768]{1,0:T(8,128)(2,1)}) custom-call(bf16[2048,2048]{1,0:T(8,128)(2,1)} %bitcast.45, bf16[2048,2048]{1,0:T(8,128)(2,1)} %bitcast.41, bf16[4,2,512,768]{3,2,1,0:T(8,128)(2,1)} %bitcast.30, f32[1,256]{1,0:T(1,128)} %get-tuple-element.139.refs_3_, ...), custom_call_target="tpu_custom_call" | custom-call | flops 22000001024 | bytes 70400000 | tf_op jit(solution)/shard_map/ffn_chunk/pallas_call | solution.py:87
  269.7 15.2 %all-gather.11.cloned.1.call-done = bf16[2048,768]{1,0:T(8,128)(2,1)} async-done(((bf16[512,768]{1,0:T(8,128)(2,1)}), bf16[2048,768]{1,0:T(8,128)(2,1)}) %all-gather.11.cloned.1.call-update) | async-done | bytes 3145744 | tf_op jit(solution)/shard_map/all_gather | solution.py:1417
  284.9 23.2 %ffn_chunk.5 = (bf16[2048,512]{1,0:T(8,128)(2,1)}, bf16[2048,256]{1,0:T(8,128)(2,1)}, bf16[2048,768]{1,0:T(8,128)(2,1)}, bf16[512,768]{1,0:T(8,128)(2,1)}, bf16[512,768]{1,0:T(8,128)(2,1)}) custom-call(bf16[2048,2048]{1,0:T(8,128)(2,1)} %bitcast.46, bf16[2048,2048]{1,0:T(8,128)(2,1)} %bitcast.42, bf16[4,512,768]{2,1,0:T(8,128)(2,1)} %bitcast.37, ...), custom_call_target="tpu_custom_call" | custom-call | flops 22000001024 | bytes 70400000 | tf_op jit(solution)/shard_map/ffn_chunk/pallas_call | solution.py:87
  308.0 91.6 %ffn_back.1 = (f32[2,128,2048]{2,1,0:T(8,128)}, bf16[2,2,4,128,2048]{4,3,2,1,0:T(8,128)(2,1)}, f32[8,2048]{1,0:T(8,128)}, bf16[512,768]{1,0:T(8,128)(2,1)}, bf16...) custom-call(bf16[2048,512]{1,0:T(8,128)(2,1)} %get-tuple-element.81., ...), custom_call_target="tpu_custom_call" | custom-call | flops 89999998976 | bytes 288000000 | tf_op jit(solution)/shard_map/ffn_back/pallas_call | solution.py:87
  399.7 67.8 %attention_back.1 = (bf16[2048,768]{1,0:T(8,128)(2,1)}, bf16[4,512,768]{2,1,0:T(8,128)(2,1)}, bf16[2048,256]{1,0:T(8,128)(2,1)}, bf16[256,768]{1,0:T(8,128)(2,1)...) custom-call(s32[2,8,128]{2,1,0:T(8,128)} %get-tuple-element.70.refs_, ...), custom_call_target="tpu_custom_call" | custom-call | flops 70000001024 | bytes 224000000 | tf_op jit(solution)/shard_map/attention_back/pallas_call | solution.py:87
  467.5 82.1 %last_sums.1 = (bf16[2,512,512]{2,1,0:T(8,128)(2,1)}, f32[8,2048]{1,0:T(8,128)}, bf16[256,768]{1,0:T(8,128)(2,1)}, bf16[256,768]{1,0:T(8,128)(2,1)}, bf16[256,25...) custom-call(bf16[2048,768]{1,0:T(8,128)(2,1)} %get-tuple-element.103, ...), custom_call_target="tpu_custom_call" | custom-call | flops 99999997952 | bytes 320000000 | tf_op jit(solution)/shard_map/last_sums/pallas_call | solution.py:87
  549.6 1.5 fusion.13
  551.1 0.0 copy-start
  551.1 0.0 copy-start.1
  551.1 5.3 form.1
  556.4 0.0 copy-done
  556.4 1.0 copy.26
  557.4 0.0 copy-done.1
  557.4 1.0 copy.27
  (4 shorter events, 0.0 us)
Async XLA Ops:
  7.2 16.5 %copy-start.3 = (bf16[256]{0:T(256)(128)(2,1)S(1)}, bf16[256]{0:T(256)(128)(2,1)}, u32[]{:S(2)}) copy-start(bf16[256]{0:T(256)(128)(2,1)} %param.19) | copy-start | bytes 1540
  7.2 16.5 %copy-start.4 = (bf16[256]{0:T(256)(128)(2,1)S(1)}, bf16[256]{0:T(256)(128)(2,1)}, u32[]{:S(2)}) copy-start(bf16[256]{0:T(256)(128)(2,1)} %param.20) | copy-start | bytes 1540
  7.2 16.5 %copy-start.5 = (bf16[256]{0:T(256)(128)(2,1)S(1)}, bf16[256]{0:T(256)(128)(2,1)}, u32[]{:S(2)}) copy-start(bf16[256]{0:T(256)(128)(2,1)} %param.21) | copy-start | bytes 1540
  7.2 16.5 %copy-start.6 = (bf16[256]{0:T(256)(128)(2,1)S(1)}, bf16[256]{0:T(256)(128)(2,1)}, u32[]{:S(2)}) copy-start(bf16[256]{0:T(256)(128)(2,1)} %param.22) | copy-start | bytes 1540
  7.2 16.5 %copy-start.2 = (s32[2,1,4]{2,1,0:T(1,128)S(1)}, s32[2,1,4]{2,1,0:T(1,128)}, u32[]{:S(2)}) copy-start(s32[2,1,4]{2,1,0:T(1,128)} %param.13) | copy-start | bytes 100
  7.2 121.9 %all-gather.7.cloned.1.call-start = ((), (), s32[]{:S(2)}) async-start(), calls=%async_computation | async-start | bytes 5242880 | tf_op jit(solution)/shard_map/all_gather | solution.py:1417
  23.6 204.5 %all-gather.9.cloned.1.call-start = ((), (), s32[]{:S(2)}) async-start(), calls=%async_computation.1 | async-start | bytes 7864320 | tf_op jit(solution)/shard_map/all_gather | solution.py:1417
  25.5 53.9 %copy-start.7 = (s32[4]{0:T(128)S(1)}, s32[4]{0:T(128)}, u32[]{:S(2)}) copy-start(s32[4]{0:T(128)} %param.14) | copy-start | bytes 52
  79.1 205.7 %all-gather.11.cloned.1.call-start = ((), (), s32[]{:S(2)}) async-start(), calls=%async_computation.2 | async-start | bytes 3932160 | tf_op jit(solution)/shard_map/all_gather | solution.py:1417
  551.1 5.3 copy-start
  551.1 6.2 %copy-start.1 = (bf16[2,512,512]{2,1,0:T(8,128)(2,1)S(1)}, bf16[2,512,512]{2,1,0:T(8,128)(2,1)}, u32[]{:S(2)}) copy-start(bf16[2,512,512]{2,1,0:T(8,128)(2,1)} %get-tuple-element.152) | copy-start | bytes 3145732
Sparse Core Ops, SparseCore 0:
  23.7 82.2 all-gather.6
  107.6 113.8 all-gather.8
  223.1 61.7 all-gather.10

commit v6 on v5

--- a/solution.py
+++ b/solution.py
@@ -1009,9 +1009,12 @@
         deals[-1].begin()
         if m == 0:
             settles[0].go()
+    host.next()
     near = [wire.make(mine, plane.at[k], d) for k, d in enumerate(peers)]
     for copy in near:
         copy.start()
+    host.chains[0].wait()
+    settles[2].go()
     for copy in near:
         copy.wait_recv()
     both = mine[...]
@@ -1021,9 +1024,6 @@
     far = [wire.make(summed, lines.at[k], d) for k, d in enumerate(along)]
     for copy in far:
         copy.start()
-    host.next()
-    host.chains[0].wait()
-    settles[2].go()
     host.end()
     settles[1].go()
     for copy in far:

time: 568 us -> 562 us (0.989)
  Pallas kernels: 527 us -> 521 us
    pallas_call x12, Pallas kernels: 527 us -> 521 us  [kernel(): pl.pallas_call(without(body, len(ins), extra), grid=grid, in_specs=in_spe...]
where the time goes in v6:
time: 562 us; the launch traced here: 559 us
  Pallas kernels  521 us (93%)
  waiting for transfers between devices  15.3 us (3%)
  between operations  14.3 us (3%)
  local copies, waits for them, and re-layouts  6.33 us (1%)
    pallas_call x12, Pallas kernels, kernel(): pl.pallas_call(without(body, len(ins), extra), grid=grid, in_specs=in_spe...  521 us
    all_gather x3, waiting for transfers between devices, gather_z(): return lax.all_gather(w, 'z', axis=0, tiled=False)  15.2 us
  transfers between devices with their start and end apart: 3, of which 1 were waited for; matrix products, arithmetic and copies ran while one was open for 1% of the time, Pallas kernels for 43%

profile of v6, /device:TPU:0, one launch (start us, length us, event | category | flops | bytes accessed | tf_op | source)
XLA Modules:
  0.0 559.3 jit_solution(16392432518268220182)
XLA Ops:
  7.2 0.0 copy-start.3
  7.2 0.0 copy-start.4
  7.2 0.0 copy-start.5
  7.2 0.0 copy-start.6
  7.2 0.0 copy-start.2
  7.2 0.0 all-gather.7.cloned.1.call-start
  7.3 16.3 %swap_attn.1.refs_6_ = bf16[512,1024]{1,0:T(8,128)(2,1)} custom-call(bf16[3,256,512]{2,1,0:T(8,128)(2,1)} %refs_0_.3, bf16[512,256]{1,0:T(8,128)(2,1)} %refs_1_.1), custom_call_target="tpu_custom_call" | custom-call | flops 14000000000 | bytes 44800000 | tf_op jit(solution)/shard_map/swap_attn/pallas_call | solution.py:87
  23.6 0.0 all-gather.7.cloned.1.call-update
  23.6 0.0 all-gather.9.cloned.1.call-start
  23.7 0.0 copy-done.3
  23.7 0.0 copy-done.4
  23.7 0.0 copy-done.5
  23.7 0.0 copy-done.6
  23.8 0.0 copy-done.2
  23.8 0.6 pad.12.refs_2_
  24.4 0.5 fusion.11.refs_3_
  24.9 0.6 fusion.7.refs_1_
  25.5 0.0 copy-start.7
  25.5 53.6 %gather_x.1 = (bf16[2,2,512,2048]{3,2,1,0:T(8,128)(2,1)}, f32[4,2,8,256]{3,2,1,0:T(8,128)}, s32[2,8,128]{2,1,0:T(8,128)}, f32[2048,128]{1,0:T(8,128)}, f32[2048,...) custom-call(bf16[2,512,512]{2,1,0:T(8,128)(2,1)} %refs_0_.4, f32[8,256]{1,0:T(8,128)} %fusion.7.refs_1_, s32[8,128]{1,0:T(8,128)} %pad.12.refs_2_, ...), custom_call_target="tpu_custom_call" | custom-call | flops 48000000000 | bytes 153600000 | tf_op jit(solution)/shard_map/gather_x/pallas_call | solution.py:87
  79.1 0.0 all-gather.9.cloned.1.call-update
  79.1 0.2 all-gather.11.cloned.1.call-start
  79.4 0.0 copy-done.7
  79.4 0.6 fusion.12
  80.0 0.7 compare_convert_fusion
  80.7 0.6 fusion.15
  81.2 1.7 fusion.14
  82.9 46.2 %gather_d.1 = (bf16[2,2,512,2048]{3,2,1,0:T(8,128)(2,1)}, bf16[2048,2048]{1,0:T(8,128)(2,1)}, bf16[512,768]{1,0:T(8,128)(2,1)}) custom-call(bf16[2,512,512]{2,1,0:T(8,128)(2,1)} %refs_0_.5, bf16[2,2,512,2048]{3,2,1,0:T(8,128)(2,1)} %get-tuple-element.71.refs_1_.refs_2_, f32[1,2048]{1,0:T(1,128)} %bitcast.18, f32[1,2048]{1,0:T(1,128)} %bitcast.23, ...), custom_call_target="tpu_custom_call" | custom-call | flops 48000000000 | bytes 153600000 | tf_op jit(solution)/shard_map/gather_d/pallas_call | solution.py:87
  129.1 0.0 all-gather.7.cloned.1.call-done
  129.1 19.1 %attention.1 = (bf16[2048,768]{1,0:T(8,128)(2,1)}, bf16[2048,256]{1,0:T(8,128)(2,1)}, bf16[512,768]{1,0:T(8,128)(2,1)}) custom-call(s32[2,8,128]{2,1,0:T(8,128)} %get-tuple-element.70.refs_0_, bf16[2048,2048]{1,0:T(8,128)(2,1)} %get-tuple-element.73.refs_1_.refs_7_, bf16[4,512,1024]{2,1,0:T(8,128)(2,1)} %bitcast.33, ...), custom_call_target="tpu_custom_call", output_to_operand_aliasing={{2}: (5, {})} | custom-call | flops 20000000000 | bytes 64000000 | tf_op jit(solution)/shard_map/attention/pallas_call | solution.py:87
  148.2 0.0 all-gather.11.cloned.1.call-update
  148.2 79.9 %attn_out.1 = (f32[2,128,2048]{2,1,0:T(8,128)}, bf16[2,2,4,128,2048]{4,3,2,1,0:T(8,128)(2,1)}) custom-call(bf16[2048,256]{1,0:T(8,128)(2,1)} %get-tuple-element.77.refs_0_.refs_2_, bf16[4,512,1024]{2,1,0:T(8,128)(2,1)} %bitcast.34, bf16[2,2,512,2048]{3,2,1,0:T(8,128)(2,1)} %get-tuple-element.71.refs_1_.refs_2_, f32[1,2048]{1,0:T(1,128)} %bitcast.20, ...), custom_call_target="tpu_custom_call" | custom-call | flops 85000003584 | bytes 272000000 | tf_op jit(solution)/shard_map/attn_out/pallas_call | solution.py:87
  228.1 0.0 all-gather.9.cloned.1.call-done
  228.1 21.0 %ffn_chunk.3 = (bf16[2048,512]{1,0:T(8,128)(2,1)}, bf16[2048,256]{1,0:T(8,128)(2,1)}, bf16[2048,768]{1,0:T(8,128)(2,1)}) custom-call(bf16[2048,2048]{1,0:T(8,128)(2,1)} %bitcast.44, bf16[2048,2048]{1,0:T(8,128)(2,1)} %bitcast.40, bf16[4,2,512,768]{3,2,1,0:T(8,128)(2,1)} %bitcast.29, f32[1,256]{1,0:T(1,128)} %get-tuple-element.140.refs_3_), custom_call_target="tpu_custom_call" | custom-call | flops 22000001024 | bytes 70400000 | tf_op jit(solution)/shard_map/ffn_chunk/pallas_call | solution.py:87
  249.1 20.5 %ffn_chunk.4 = (bf16[2048,512]{1,0:T(8,128)(2,1)}, bf16[2048,256]{1,0:T(8,128)(2,1)}, bf16[2048,768]{1,0:T(8,128)(2,1)}) custom-call(bf16[2048,2048]{1,0:T(8,128)(2,1)} %bitcast.45, bf16[2048,2048]{1,0:T(8,128)(2,1)} %bitcast.41, bf16[4,2,512,768]{3,2,1,0:T(8,128)(2,1)} %bitcast.30, f32[1,256]{1,0:T(1,128)} %get-tuple-element.139.refs_3_, ...), custom_call_target="tpu_custom_call" | custom-call | flops 22000001024 | bytes 70400000 | tf_op jit(solution)/shard_map/ffn_chunk/pallas_call | solution.py:87
  269.7 15.2 %all-gather.11.cloned.1.call-done = bf16[2048,768]{1,0:T(8,128)(2,1)} async-done(((bf16[512,768]{1,0:T(8,128)(2,1)}), bf16[2048,768]{1,0:T(8,128)(2,1)}) %all-gather.11.cloned.1.call-update) | async-done | bytes 3145744 | tf_op jit(solution)/shard_map/all_gather | solution.py:1417
  284.9 23.2 %ffn_chunk.5 = (bf16[2048,512]{1,0:T(8,128)(2,1)}, bf16[2048,256]{1,0:T(8,128)(2,1)}, bf16[2048,768]{1,0:T(8,128)(2,1)}, bf16[512,768]{1,0:T(8,128)(2,1)}, bf16[512,768]{1,0:T(8,128)(2,1)}) custom-call(bf16[2048,2048]{1,0:T(8,128)(2,1)} %bitcast.46, bf16[2048,2048]{1,0:T(8,128)(2,1)} %bitcast.42, bf16[4,512,768]{2,1,0:T(8,128)(2,1)} %bitcast.37, ...), custom_call_target="tpu_custom_call" | custom-call | flops 22000001024 | bytes 70400000 | tf_op jit(solution)/shard_map/ffn_chunk/pallas_call | solution.py:87
  308.0 91.6 %ffn_back.1 = (f32[2,128,2048]{2,1,0:T(8,128)}, bf16[2,2,4,128,2048]{4,3,2,1,0:T(8,128)(2,1)}, f32[8,2048]{1,0:T(8,128)}, bf16[512,768]{1,0:T(8,128)(2,1)}, bf16...) custom-call(bf16[2048,512]{1,0:T(8,128)(2,1)} %get-tuple-element.81., ...), custom_call_target="tpu_custom_call" | custom-call | flops 89999998976 | bytes 288000000 | tf_op jit(solution)/shard_map/ffn_back/pallas_call | solution.py:87
  399.7 67.8 %attention_back.1 = (bf16[2048,768]{1,0:T(8,128)(2,1)}, bf16[4,512,768]{2,1,0:T(8,128)(2,1)}, bf16[2048,256]{1,0:T(8,128)(2,1)}, bf16[256,768]{1,0:T(8,128)(2,1)...) custom-call(s32[2,8,128]{2,1,0:T(8,128)} %get-tuple-element.70.refs_, ...), custom_call_target="tpu_custom_call" | custom-call | flops 70000001024 | bytes 224000000 | tf_op jit(solution)/shard_map/attention_back/pallas_call | solution.py:87
  467.5 76.3 %last_sums.1 = (bf16[2,512,512]{2,1,0:T(8,128)(2,1)}, f32[8,2048]{1,0:T(8,128)}, bf16[256,768]{1,0:T(8,128)(2,1)}, bf16[256,768]{1,0:T(8,128)(2,1)}, bf16[256,25...) custom-call(bf16[2048,768]{1,0:T(8,128)(2,1)} %get-tuple-element.103, ...), custom_call_target="tpu_custom_call" | custom-call | flops 99999997952 | bytes 320000000 | tf_op jit(solution)/shard_map/last_sums/pallas_call | solution.py:87
  543.8 1.5 fusion.13
  545.3 0.0 copy-start
  545.3 0.0 copy-start.1
  545.3 5.3 form.1
  550.6 0.0 copy-done
  550.6 1.0 copy.26
  551.6 0.0 copy-done.1
  551.6 1.0 copy.27
  (4 shorter events, 0.0 us)
Async XLA Ops:
  7.2 16.5 %copy-start.3 = (bf16[256]{0:T(256)(128)(2,1)S(1)}, bf16[256]{0:T(256)(128)(2,1)}, u32[]{:S(2)}) copy-start(bf16[256]{0:T(256)(128)(2,1)} %param.19) | copy-start | bytes 1540
  7.2 16.5 %copy-start.4 = (bf16[256]{0:T(256)(128)(2,1)S(1)}, bf16[256]{0:T(256)(128)(2,1)}, u32[]{:S(2)}) copy-start(bf16[256]{0:T(256)(128)(2,1)} %param.20) | copy-start | bytes 1540
  7.2 16.5 %copy-start.5 = (bf16[256]{0:T(256)(128)(2,1)S(1)}, bf16[256]{0:T(256)(128)(2,1)}, u32[]{:S(2)}) copy-start(bf16[256]{0:T(256)(128)(2,1)} %param.21) | copy-start | bytes 1540
  7.2 16.5 %copy-start.6 = (bf16[256]{0:T(256)(128)(2,1)S(1)}, bf16[256]{0:T(256)(128)(2,1)}, u32[]{:S(2)}) copy-start(bf16[256]{0:T(256)(128)(2,1)} %param.22) | copy-start | bytes 1540
  7.2 16.5 %copy-start.2 = (s32[2,1,4]{2,1,0:T(1,128)S(1)}, s32[2,1,4]{2,1,0:T(1,128)}, u32[]{:S(2)}) copy-start(s32[2,1,4]{2,1,0:T(1,128)} %param.13) | copy-start | bytes 100
  7.2 121.9 %all-gather.7.cloned.1.call-start = ((), (), s32[]{:S(2)}) async-start(), calls=%async_computation | async-start | bytes 5242880 | tf_op jit(solution)/shard_map/all_gather | solution.py:1417
  23.6 204.5 %all-gather.9.cloned.1.call-start = ((), (), s32[]{:S(2)}) async-start(), calls=%async_computation.1 | async-start | bytes 7864320 | tf_op jit(solution)/shard_map/all_gather | solution.py:1417
  25.5 53.9 %copy-start.7 = (s32[4]{0:T(128)S(1)}, s32[4]{0:T(128)}, u32[]{:S(2)}) copy-start(s32[4]{0:T(128)} %param.14) | copy-start | bytes 52
  79.1 205.7 %all-gather.11.cloned.1.call-start = ((), (), s32[]{:S(2)}) async-start(), calls=%async_computation.2 | async-start | bytes 3932160 | tf_op jit(solution)/shard_map/all_gather | solution.py:1417
  545.3 5.3 copy-start
  545.3 6.2 %copy-start.1 = (bf16[2,512,512]{2,1,0:T(8,128)(2,1)S(1)}, bf16[2,512,512]{2,1,0:T(8,128)(2,1)}, u32[]{:S(2)}) copy-start(bf16[2,512,512]{2,1,0:T(8,128)(2,1)} %get-tuple-element.152) | copy-start | bytes 3145732
Sparse Core Ops, SparseCore 0:
  23.7 82.2 all-gather.6
  107.6 113.8 all-gather.8
  223.1 61.7 all-gather.10

commit v7 on v6

--- a/solution.py
+++ b/solution.py
@@ -1365,7 +1365,9 @@
 
 
 def form_body(parts, *refs):
-    halves, (gu, down, qkv, out) = refs[: 2 * parts + 4], refs[2 * parts + 4 :]
+    halves, (one_in, two_in, gu, down, qkv, out, one_out, two_out) = refs[: 2 * parts + 4], refs[2 * parts + 4 :]
+    one_out[...] = one_in[...]
+    two_out[...] = two_in[...]
     y = lax.axis_index("y")
     one = halves[0].shape[1] // 3
 
@@ -1389,12 +1391,12 @@
             qkv[p, :, i * span : (i + 1) * span] = v[:, p * span : (p + 1) * span]
 
 
-def form(halves, w_gu, w_down, w_qkv, w_out):
+def form(halves, tokens, w_gu, w_down, w_qkv, w_out):
     parts = (len(halves) - 4) // 2
     return kernel(
-        functools.partial(form_body, parts), halves, [VMEM] * len(halves),
-        tuple(shaped(w.shape, F32) for w in (w_gu, w_down, w_qkv, w_out)),
-        (VMEM,) * 4, 8, "form",
+        functools.partial(form_body, parts), [*halves, *tokens], [VMEM] * (len(halves) + 2),
+        tuple(shaped(w.shape, F32) for w in (w_gu, w_down, w_qkv, w_out)) + tuple(shaped(t.shape) for t in tokens),
+        (VMEM,) * 6, 8, "form",
     )
 
 
@@ -1458,8 +1460,8 @@
     in_grad, sums, *r = last_sums(
         low, wa, x_all, mid_grad, gain1, vec2, grad2, got2, out_g, gout, qkv_g.reshape(width, -1), zn
     )
-    gu_grad, down_grad, qkv_grad, out_grad = form(
-        [*first, *r[:6]], w_gu, w_down, w_qkv, w_out
+    gu_grad, down_grad, qkv_grad, out_grad, layer_out, in_grad = form(
+        [*first, *r[:6]], [layer_out, in_grad], w_gu, w_down, w_qkv, w_out
     )
 
     mine = lax.dynamic_slice_in_dim(sums, (z * 2 + y) * g1.shape[0], g1.shape[0], 1)

time: 562 us -> 562 us (level)
  no operation moved by 1% of the time
where the time goes in v7:
time: 562 us; the launch traced here: 558 us
  Pallas kernels  522 us (93%)
  waiting for transfers between devices  15.3 us (3%)
  between operations  14.3 us (3%)
    pallas_call x12, Pallas kernels, kernel(): pl.pallas_call(without(body, len(ins), extra), grid=grid, in_specs=in_spe...  522 us
    all_gather x3, waiting for transfers between devices, gather_z(): return lax.all_gather(w, 'z', axis=0, tiled=False)  15.2 us
  transfers between devices with their start and end apart: 3, of which 1 were waited for; matrix products, arithmetic and copies ran while one was open for 1% of the time, Pallas kernels for 43%

profile of v7, /device:TPU:0, one launch (start us, length us, event | category | flops | bytes accessed | tf_op | source)
XLA Modules:
  0.0 558.5 jit_solution(17285302715560747047)
XLA Ops:
  7.2 0.0 copy-start.1
  7.2 0.0 copy-start.2
  7.2 0.0 copy-start.3
  7.2 0.0 copy-start.4
  7.2 0.0 copy-start
  7.2 0.0 all-gather.7.cloned.1.call-start
  7.3 16.3 %swap_attn.1.refs_6_ = bf16[512,1024]{1,0:T(8,128)(2,1)} custom-call(bf16[3,256,512]{2,1,0:T(8,128)(2,1)} %refs_0_.3, bf16[512,256]{1,0:T(8,128)(2,1)} %refs_1_.1), custom_call_target="tpu_custom_call" | custom-call | flops 14000000000 | bytes 44800000 | tf_op jit(solution)/shard_map/swap_attn/pallas_call | solution.py:87
  23.6 0.0 all-gather.7.cloned.1.call-update
  23.6 0.0 all-gather.9.cloned.1.call-start
  23.7 0.0 copy-done.1
  23.7 0.0 copy-done.2
  23.7 0.0 copy-done.3
  23.7 0.0 copy-done.4
  23.8 0.0 copy-done
  23.8 0.6 pad.12.refs_2_
  24.4 0.5 fusion.11.refs_3_
  24.9 0.6 fusion.7.refs_1_
  25.5 0.0 copy-start.5
  25.5 53.6 %gather_x.1 = (bf16[2,2,512,2048]{3,2,1,0:T(8,128)(2,1)}, f32[4,2,8,256]{3,2,1,0:T(8,128)}, s32[2,8,128]{2,1,0:T(8,128)}, f32[2048,128]{1,0:T(8,128)}, f32[2048,...) custom-call(bf16[2,512,512]{2,1,0:T(8,128)(2,1)} %refs_0_.4, f32[8,256]{1,0:T(8,128)} %fusion.7.refs_1_, s32[8,128]{1,0:T(8,128)} %pad.12.refs_2_, ...), custom_call_target="tpu_custom_call" | custom-call | flops 48000000000 | bytes 153600000 | tf_op jit(solution)/shard_map/gather_x/pallas_call | solution.py:87
  79.1 0.0 all-gather.9.cloned.1.call-update
  79.2 0.2 all-gather.11.cloned.1.call-start
  79.4 0.0 copy-done.5
  79.4 0.6 fusion.12
  80.0 0.7 compare_convert_fusion
  80.7 0.6 fusion.15
  81.3 1.6 fusion.14
  82.9 46.2 %gather_d.1 = (bf16[2,2,512,2048]{3,2,1,0:T(8,128)(2,1)}, bf16[2048,2048]{1,0:T(8,128)(2,1)}, bf16[512,768]{1,0:T(8,128)(2,1)}) custom-call(bf16[2,512,512]{2,1,0:T(8,128)(2,1)} %refs_0_.5, bf16[2,2,512,2048]{3,2,1,0:T(8,128)(2,1)} %get-tuple-element.73.refs_1_.refs_2_, f32[1,2048]{1,0:T(1,128)} %bitcast.18, f32[1,2048]{1,0:T(1,128)} %bitcast.23, ...), custom_call_target="tpu_custom_call" | custom-call | flops 48000000000 | bytes 153600000 | tf_op jit(solution)/shard_map/gather_d/pallas_call | solution.py:87
  129.1 0.0 all-gather.7.cloned.1.call-done
  129.1 19.1 %attention.1 = (bf16[2048,768]{1,0:T(8,128)(2,1)}, bf16[2048,256]{1,0:T(8,128)(2,1)}, bf16[512,768]{1,0:T(8,128)(2,1)}) custom-call(s32[2,8,128]{2,1,0:T(8,128)} %get-tuple-element.72.refs_0_, bf16[2048,2048]{1,0:T(8,128)(2,1)} %get-tuple-element.75.refs_1_.refs_7_, bf16[4,512,1024]{2,1,0:T(8,128)(2,1)} %bitcast.33, ...), custom_call_target="tpu_custom_call", output_to_operand_aliasing={{2}: (5, {})} | custom-call | flops 20000000000 | bytes 64000000 | tf_op jit(solution)/shard_map/attention/pallas_call | solution.py:87
  148.2 0.0 all-gather.11.cloned.1.call-update
  148.2 79.9 %attn_out.1 = (f32[2,128,2048]{2,1,0:T(8,128)}, bf16[2,2,4,128,2048]{4,3,2,1,0:T(8,128)(2,1)}) custom-call(bf16[2048,256]{1,0:T(8,128)(2,1)} %get-tuple-element.79.refs_0_.refs_2_, bf16[4,512,1024]{2,1,0:T(8,128)(2,1)} %bitcast.34, bf16[2,2,512,2048]{3,2,1,0:T(8,128)(2,1)} %get-tuple-element.73.refs_1_.refs_2_, f32[1,2048]{1,0:T(1,128)} %bitcast.20, ...), custom_call_target="tpu_custom_call" | custom-call | flops 85000003584 | bytes 272000000 | tf_op jit(solution)/shard_map/attn_out/pallas_call | solution.py:87
  228.0 0.0 all-gather.9.cloned.1.call-done
  228.1 21.0 %ffn_chunk.3 = (bf16[2048,512]{1,0:T(8,128)(2,1)}, bf16[2048,256]{1,0:T(8,128)(2,1)}, bf16[2048,768]{1,0:T(8,128)(2,1)}) custom-call(bf16[2048,2048]{1,0:T(8,128)(2,1)} %bitcast.44, bf16[2048,2048]{1,0:T(8,128)(2,1)} %bitcast.40, bf16[4,2,512,768]{3,2,1,0:T(8,128)(2,1)} %bitcast.29, f32[1,256]{1,0:T(1,128)} %get-tuple-element.144.refs_3_), custom_call_target="tpu_custom_call" | custom-call | flops 22000001024 | bytes 70400000 | tf_op jit(solution)/shard_map/ffn_chunk/pallas_call | solution.py:87
  249.1 20.5 %ffn_chunk.4 = (bf16[2048,512]{1,0:T(8,128)(2,1)}, bf16[2048,256]{1,0:T(8,128)(2,1)}, bf16[2048,768]{1,0:T(8,128)(2,1)}) custom-call(bf16[2048,2048]{1,0:T(8,128)(2,1)} %bitcast.45, bf16[2048,2048]{1,0:T(8,128)(2,1)} %bitcast.41, bf16[4,2,512,768]{3,2,1,0:T(8,128)(2,1)} %bitcast.30, f32[1,256]{1,0:T(1,128)} %get-tuple-element.143.refs_3_, ...), custom_call_target="tpu_custom_call" | custom-call | flops 22000001024 | bytes 70400000 | tf_op jit(solution)/shard_map/ffn_chunk/pallas_call | solution.py:87
  269.7 15.2 %all-gather.11.cloned.1.call-done = bf16[2048,768]{1,0:T(8,128)(2,1)} async-done(((bf16[512,768]{1,0:T(8,128)(2,1)}), bf16[2048,768]{1,0:T(8,128)(2,1)}) %all-gather.11.cloned.1.call-update) | async-done | bytes 3145744 | tf_op jit(solution)/shard_map/all_gather | solution.py:1419
  284.9 23.2 %ffn_chunk.5 = (bf16[2048,512]{1,0:T(8,128)(2,1)}, bf16[2048,256]{1,0:T(8,128)(2,1)}, bf16[2048,768]{1,0:T(8,128)(2,1)}, bf16[512,768]{1,0:T(8,128)(2,1)}, bf16[512,768]{1,0:T(8,128)(2,1)}) custom-call(bf16[2048,2048]{1,0:T(8,128)(2,1)} %bitcast.46, bf16[2048,2048]{1,0:T(8,128)(2,1)} %bitcast.42, bf16[4,512,768]{2,1,0:T(8,128)(2,1)} %bitcast.37, ...), custom_call_target="tpu_custom_call" | custom-call | flops 22000001024 | bytes 70400000 | tf_op jit(solution)/shard_map/ffn_chunk/pallas_call | solution.py:87
  308.0 91.6 %ffn_back.1 = (f32[2,128,2048]{2,1,0:T(8,128)}, bf16[2,2,4,128,2048]{4,3,2,1,0:T(8,128)(2,1)}, f32[8,2048]{1,0:T(8,128)}, bf16[512,768]{1,0:T(8,128)(2,1)}, bf16...) custom-call(bf16[2048,512]{1,0:T(8,128)(2,1)} %get-tuple-element.83., ...), custom_call_target="tpu_custom_call" | custom-call | flops 89999998976 | bytes 288000000 | tf_op jit(solution)/shard_map/ffn_back/pallas_call | solution.py:87
  399.6 67.8 %attention_back.1 = (bf16[2048,768]{1,0:T(8,128)(2,1)}, bf16[4,512,768]{2,1,0:T(8,128)(2,1)}, bf16[2048,256]{1,0:T(8,128)(2,1)}, bf16[256,768]{1,0:T(8,128)(2,1)...) custom-call(s32[2,8,128]{2,1,0:T(8,128)} %get-tuple-element.72.refs_, ...), custom_call_target="tpu_custom_call" | custom-call | flops 70000001024 | bytes 224000000 | tf_op jit(solution)/shard_map/attention_back/pallas_call | solution.py:87
  467.4 76.3 %last_sums.1 = (bf16[2,512,512]{2,1,0:T(8,128)(2,1)}, f32[8,2048]{1,0:T(8,128)}, bf16[256,768]{1,0:T(8,128)(2,1)}, bf16[256,768]{1,0:T(8,128)(2,1)}, bf16[256,25...) custom-call(bf16[2048,768]{1,0:T(8,128)(2,1)} %get-tuple-element.108, ...), custom_call_target="tpu_custom_call" | custom-call | flops 99999997952 | bytes 320000000 | tf_op jit(solution)/shard_map/last_sums/pallas_call | solution.py:87
  543.8 1.5 fusion.13
  545.3 6.4 %form.1 = (f32[2,256,1536]{2,1,0:T(8,128)}, f32[1536,256]{1,0:T(8,128)}, f32[3,256,512]{2,1,0:T(8,128)}, f32[512,256]{1,0:T(8,128)}, bf16[2,512,512]{2,1,0:T(8,128)(2,1)}, /*index=5*/bf16[2,512,512]{2,1,0:T(8,128)(2,1)}) custom-call(bf16[256,768]{1,0:T(8,128)(2,1)} %get-tuple-element.104.refs_0_, bf16[256,768]{1,0:T(8,128)(2,1)} %get-tuple-element.105.refs_1_, ...), custom_call_target="tpu_custom_call" | custom-call | flops 8000000000 | bytes 25600000 | tf_op jit(solution)/shard_map/form/pallas_call | solution.py:87
  (4 shorter events, 0.0 us)
Async XLA Ops:
  7.2 16.5 %copy-start.1 = (bf16[256]{0:T(256)(128)(2,1)S(1)}, bf16[256]{0:T(256)(128)(2,1)}, u32[]{:S(2)}) copy-start(bf16[256]{0:T(256)(128)(2,1)} %param.19) | copy-start | bytes 1540
  7.2 16.5 %copy-start.2 = (bf16[256]{0:T(256)(128)(2,1)S(1)}, bf16[256]{0:T(256)(128)(2,1)}, u32[]{:S(2)}) copy-start(bf16[256]{0:T(256)(128)(2,1)} %param.20) | copy-start | bytes 1540
  7.2 16.5 %copy-start.3 = (bf16[256]{0:T(256)(128)(2,1)S(1)}, bf16[256]{0:T(256)(128)(2,1)}, u32[]{:S(2)}) copy-start(bf16[256]{0:T(256)(128)(2,1)} %param.21) | copy-start | bytes 1540
  7.2 16.5 %copy-start.4 = (bf16[256]{0:T(256)(128)(2,1)S(1)}, bf16[256]{0:T(256)(128)(2,1)}, u32[]{:S(2)}) copy-start(bf16[256]{0:T(256)(128)(2,1)} %param.22) | copy-start | bytes 1540
  7.2 16.5 %copy-start = (s32[2,1,4]{2,1,0:T(1,128)S(1)}, s32[2,1,4]{2,1,0:T(1,128)}, u32[]{:S(2)}) copy-start(s32[2,1,4]{2,1,0:T(1,128)} %param.13) | copy-start | bytes 100
  7.2 121.9 %all-gather.7.cloned.1.call-start = ((), (), s32[]{:S(2)}) async-start(), calls=%async_computation | async-start | bytes 5242880 | tf_op jit(solution)/shard_map/all_gather | solution.py:1419
  23.6 204.4 %all-gather.9.cloned.1.call-start = ((), (), s32[]{:S(2)}) async-start(), calls=%async_computation.1 | async-start | bytes 7864320 | tf_op jit(solution)/shard_map/all_gather | solution.py:1419
  25.5 53.9 %copy-start.5 = (s32[4]{0:T(128)S(1)}, s32[4]{0:T(128)}, u32[]{:S(2)}) copy-start(s32[4]{0:T(128)} %param.14) | copy-start | bytes 52
  79.2 205.7 %all-gather.11.cloned.1.call-start = ((), (), s32[]{:S(2)}) async-start(), calls=%async_computation.2 | async-start | bytes 3932160 | tf_op jit(solution)/shard_map/all_gather | solution.py:1419
Sparse Core Ops, SparseCore 0:
  23.7 82.2 all-gather.6
  107.6 113.8 all-gather.8
  223.1 61.7 all-gather.10
